TPU v7x, 32 devices: a whole 2x2x4 slice. The times are simulated.
32 devices in a mesh: dp: 8 (over z, y), pipe: 4 (over x, core).
Axes of the slice: x: 2, y: 2, z: 4, core: 2. Of those that a mesh axis runs over, the one named last changes fastest.
Arguments:
- features: bfloat16 [2, 48, 13, 13, 512], P(None, 'dp', None, None, 'pipe'), may hold values from -6 to 6
- clip_counts: int32 [2, 16], P(None, 'dp'), may hold values from 1 to 3, as said below
- conv4_weight: bfloat16 [3, 3, 512, 512], replicated, may hold values from -0.09375 to 0.09375
- conv4_bias: float32 [512], replicated, may hold values from -3 to 3
- conv5_weight: bfloat16 [3, 3, 512, 512], replicated, may hold values from -0.09375 to 0.09375
- conv5_bias: float32 [512], replicated, may hold values from -3 to 3
- cotangent: bfloat16 [2, 48, 13, 13, 512], P(None, 'dp', None, None, 'pipe'), may hold values from -6 to 6
Outputs:
- conv5_out: bfloat16 [2, 48, 13, 13, 512], P(None, 'dp', None, None, 'pipe')
- input_grad: bfloat16 [2, 48, 13, 13, 512], P(None, 'dp', None, None, 'pipe')
- conv4_weight_grad: float32 [3, 3, 512, 512], P(None, None, 'pipe', 'dp')
- conv4_bias_grad: float32 [512], P('dp')
- conv5_weight_grad: float32 [3, 3, 512, 512], P(None, None, 'pipe', 'dp')
- conv5_bias_grad: float32 [512], P('dp')
Inputs may be any that keep to these rules, and one draw needn't show every extreme that they name: `clip_counts`: each video's clips fill the next slots of its device's 6 slots in order, 2 videos a device and micro-batch.
All inputs are finite; a program needn't handle non-finite values.
Results may differ from a plain program's by a relative error of at most 0.012.
Values may be sent and summed in bfloat16 or wider, within the bound.
No kernel may reach another device: no remote copies, remote signals or barrier semaphores. Data moves between devices by JAX's collectives and lax.ppermute only.
A program may use at most 128 MiB of HBM per device.

v0:
```python
import jax
import jax.numpy as jnp
from jax import lax
from jax.sharding import PartitionSpec as P


def convolve(field, kernel):
    return lax.conv_general_dilated(
        field,
        kernel,
        (1, 1),
        "SAME",
        dimension_numbers=("NHWC", "HWIO", "NHWC"),
        preferred_element_type=jnp.float32,
    )


def weight_grad(field, slope):
    side_len = field.shape[1]
    padded = jnp.pad(field, ((0, 0), (1, 1), (1, 1), (0, 0)))
    tap_rows = []
    for row_tap in range(3):
        tap_line = []
        for col_tap in range(3):
            window = padded[:, row_tap : row_tap + side_len, col_tap : col_tap + side_len, :]
            tap_line.append(
                jnp.einsum("nyxc,nyxd->cd", window, slope, preferred_element_type=jnp.float32)
            )
        tap_rows.append(jnp.stack(tap_line))
    return jnp.stack(tap_rows)


def silu_slope(upstream, mask_rows, pre_act):
    sigmoid_val = jax.nn.sigmoid(pre_act)
    return (
        upstream.astype(jnp.float32)
        * mask_rows
        * sigmoid_val
        * (1.0 + pre_act * (1.0 - sigmoid_val))
    ).astype(jnp.bfloat16)


def body(features, clip_counts, conv4_weight, conv4_bias, conv5_weight, conv5_bias, cotangent):
    section_number = lax.axis_index("pipe")
    micro = features.shape[0]
    slots = features.shape[1]
    live_count = jnp.sum(clip_counts, axis=1)
    slot_mask = (jnp.arange(slots, dtype=jnp.int32)[None, :] < live_count[:, None]).astype(
        jnp.float32
    )
    share = features.shape[4]
    start = section_number * share
    mask_rows = slot_mask.reshape(-1)[:, None, None, None]
    own4 = lax.dynamic_slice_in_dim(conv4_weight, start, share, 2)
    own5 = lax.dynamic_slice_in_dim(conv5_weight, start, share, 2)
    bias4_share = lax.dynamic_slice_in_dim(conv4_bias, start, share, 0)
    bias5_share = lax.dynamic_slice_in_dim(conv5_bias, start, share, 0)
    flat_in = features.reshape((micro * slots,) + features.shape[2:])
    flat_cot = cotangent.reshape((micro * slots,) + cotangent.shape[2:])
    pre4 = (
        lax.psum_scatter(convolve(flat_in, own4), "pipe", scatter_dimension=3, tiled=True)
        + bias4_share
    )
    hidden = (mask_rows * jax.nn.silu(pre4)).astype(jnp.bfloat16)
    pre5 = (
        lax.psum_scatter(convolve(hidden, own5), "pipe", scatter_dimension=3, tiled=True)
        + bias5_share
    )
    out_flat = (mask_rows * jax.nn.silu(pre5)).astype(jnp.bfloat16)
    slope5 = silu_slope(flat_cot, mask_rows, pre5)
    slope5_all = lax.all_gather(slope5, "pipe", axis=3, tiled=True)
    kernel5_term = weight_grad(hidden, slope5_all)
    bias5_term = jnp.sum(slope5_all.astype(jnp.float32), axis=(0, 1, 2))
    back_hidden = convolve(slope5_all, jnp.flip(own5, (0, 1)).transpose(0, 1, 3, 2)).astype(
        jnp.bfloat16
    )
    slope4 = silu_slope(back_hidden, mask_rows, pre4)
    slope4_all = lax.all_gather(slope4, "pipe", axis=3, tiled=True)
    kernel4_term = weight_grad(flat_in, slope4_all)
    bias4_term = jnp.sum(slope4_all.astype(jnp.float32), axis=(0, 1, 2))
    grad_flat = convolve(slope4_all, jnp.flip(own4, (0, 1)).transpose(0, 1, 3, 2)).astype(
        jnp.bfloat16
    )
    grad_w4, grad_w5, grad_b4, grad_b5 = (
        lax.psum_scatter(kernel4_term, "dp", scatter_dimension=3, tiled=True),
        lax.psum_scatter(kernel5_term, "dp", scatter_dimension=3, tiled=True),
        lax.psum_scatter(bias4_term, "dp", scatter_dimension=0, tiled=True),
        lax.psum_scatter(bias5_term, "dp", scatter_dimension=0, tiled=True),
    )
    conv5_out = out_flat.reshape(features.shape)
    input_grad = grad_flat.reshape(features.shape)
    return (conv5_out, input_grad, grad_w4, grad_b4, grad_w5, grad_b5)


def solution(mesh):
    return jax.shard_map(
        body,
        mesh=mesh,
        in_specs=(
            P(None, "dp", None, None, "pipe"),
            P(None, "dp"),
            P(),
            P(),
            P(),
            P(),
            P(None, "dp", None, None, "pipe"),
        ),
        out_specs=(
            P(None, "dp", None, None, "pipe"),
            P(None, "dp", None, None, "pipe"),
            P(None, None, "pipe", "dp"),
            P("dp"),
            P(None, None, "pipe", "dp"),
            P("dp"),
        ),
        check_vma=False,
    )
```

profile of v0, /device:TPU:0, one launch (start us, length us, event | category | flops | bytes accessed | tf_op | source)
XLA Modules:
  0.0 457.6 jit_solution(2635205474762088788)
XLA Ops:
  7.2 1.1 copy.86
  8.4 6.9 %fusion.12 = f32[12,13,13,512]{3,0,2,1:T(8,128)} fusion(bf16[3,3,512,512]{3,2,1,0:T(8,128)(2,1)} %param.9, s32[]{:T(128)S(6)} %select_n.2, bf16[12,13,13,128]{3,1,2,0:T(8,128)(2,1)S(1)} %bitcast.132), kind=kOutput, calls=%fused_computation.39 | convolution fusion | flops 2153250816 | bytes 5852164 | tf_op jit(solution)/shard_map/conv_general_dilated | solution.py:8
  15.4 0.8 dynamic_slice.13
  16.4 55.1 %reduce-scatter.3.cloned.1.call-done = f32[12,13,13,128]{3,0,2,1:T(8,128)} async-done(((f32[12,13,13,512]{3,0,2,1:T(8,128)}), f32[12,13,13,128]{3,0,2,1:T(8,128)}) %reduce-scatter.3.cloned.1.call-update) | async-done | bytes 1038352 | tf_op jit(solution)/shard_map/reduce_scatter | solution.py:61
  71.5 1.7 multiply_convert_fusion.2
  73.3 6.7 %fusion.9 = f32[12,13,13,512]{3,0,2,1:T(8,128)} fusion(bf16[12,13,13,128]{3,0,2,1:T(8,128)(2,1)S(1)} %multiply_convert_fusion.2, bf16[3,3,512,512]{3,2,1,0:T(8,128)(2,1)} %param.11, s32[]{:T(128)S(6)} %select_n.2), kind=kOutput, calls=%fused_computation.36 | convolution fusion | flops 2153250816 | bytes 5852164 | tf_op jit(solution)/shard_map/conv_general_dilated | solution.py:8
  80.0 0.8 dynamic_slice.15
  81.2 52.3 %reduce-scatter.5.cloned.1.call-done = f32[12,13,13,128]{3,0,2,1:T(8,128)} async-done(((f32[12,13,13,512]{3,0,2,1:T(8,128)}), f32[12,13,13,128]{3,0,2,1:T(8,128)}) %reduce-scatter.5.cloned.1.call-update) | async-done | bytes 1038352 | tf_op jit(solution)/shard_map/reduce_scatter | solution.py:66
  133.5 3.3 fusion.4
  136.9 2.8 pad_slice_fusion.7
  139.6 24.1 %all-gather.3.cloned.1.call-done = bf16[12,13,13,512]{3,0,2,1:T(8,128)(2,1)} async-done(((bf16[12,13,13,128]{3,0,2,1:T(8,128)(2,1)}), bf16[12,13,13,512]{3,0,2,1:T(8,128)(2,1)}) %all-gather.3.cloned.1.call-update) | async-done | bytes 2076688 | tf_op jit(solution)/shard_map/all_gather | solution.py:71
  163.7 9.6 %multiply_convert_fusion = bf16[12,13,13,128]{3,0,2,1:T(8,128)(2,1)} fusion(f32[12,13,13,128]{3,0,2,1:T(8,128)} %reduce-scatter.3.cloned.1.call-done, bf16[12,13,13,512]{3,0,2,1:T(8,128)(2,1)} %all-gather.3.cloned.1.call-done, bf16[3,3,512,512]{3,2,1,0:T(8,128)(2,1)} %param.11, s32[]{:T(128)S(6)} %select_n.2, f32[128]{0:T(128)S(1)} %dynamic_slice.13, ...), kind=kOutput, calls=%fused_computation.10 | convolution fusion | flops 2156625408 | bytes 5852724 | tf_op jit(solution)/shard_map/conv_general_dilated | solution.py:8
  173.7 1.8 convolution_bitcast_fusion.10
  175.5 0.6 convolution_bitcast_fusion.9
  176.6 0.6 convolution_bitcast_fusion.8
  177.2 0.6 convolution_bitcast_fusion.12
  178.3 0.6 convolution_bitcast_fusion.16
  179.0 0.6 convolution_bitcast_fusion.15
  180.0 0.6 convolution_bitcast_fusion.14
  180.8 0.6 convolution_bitcast_fusion.13
  181.8 0.6 convolution_bitcast_fusion.11
  182.9 2.9 copy.122
  185.7 14.6 %all-gather.5.cloned.1.call-done = bf16[12,13,13,512]{3,0,2,1:T(8,128)(2,1)} async-done(((bf16[12,13,13,128]{3,0,2,1:T(8,128)(2,1)}), bf16[12,13,13,512]{3,0,2,1:T(8,128)(2,1)}) %all-gather.5.cloned.1.call-update) | async-done | bytes 2076688 | tf_op jit(solution)/shard_map/all_gather | solution.py:78
  200.3 4.4 convolution_bitcast_fusion.2
  204.7 2.5 convolution_bitcast_fusion.1
  207.3 2.5 convolution_bitcast_fusion
  209.9 2.5 convolution_bitcast_fusion.6
  212.5 10.4 %convolution_bitcast_fusion.5 = f32[1,128,512]{2,1,0:T(8,128)S(1)} fusion(bf16[12,13,13,128]{3,1,2,0:T(8,128)(2,1)S(1)} %bitcast.137, bf16[12,13,13,512]{3,0,2,1:T(8,128)(2,1)S(1)} %copy-done.2), kind=kOutput, calls=%fused_computation.22 | convolution fusion | flops 265814016 | bytes 2857984 | tf_op jit(solution)/shard_map/nyxc,nyxd->cd/dot_general | solution.py:27
  222.9 2.5 convolution_bitcast_fusion.4
  225.4 2.5 convolution_bitcast_fusion.3
  227.9 0.6 fusion.5
  228.5 2.5 convolution_bitcast_fusion.7
  231.4 3.0 copy.103
  234.4 0.6 copy-done.17
  235.0 0.6 dynamic-slice
  236.5 1.2 copy.123
  237.7 0.6 convert_reduce_fusion
  238.3 0.6 convert_reduce_fusion.1
  239.0 22.6 %all-reduce.6 = (f32[512]{0:T(512)S(1)}, f32[512]{0:T(512)S(1)}) all-reduce(f32[512]{0:T(512)S(1)} %convert_reduce_fusion.1, f32[512]{0:T(512)S(1)} %convert_reduce_fusion), channel_id=5, replica_groups=mesh['dp'=8,'pipe'=4] {'dp'}, use_global_device_ids=true, to_apply=%region_5.6.clone | all-reduce | flops 1024 | bytes 8192
  261.6 0.6 dynamic-slice.3
  262.2 0.6 dynamic-slice.7
  262.8 7.9 %convolution_convert_fusion = bf16[12,13,13,128]{3,0,2,1:T(8,128)(2,1)S(1)} fusion(bf16[12,13,13,512]{3,0,2,1:T(8,128)(2,1)S(1)} %copy-done.4, bf16[3,3,512,512]{3,2,1,0:T(8,128)(2,1)} %param.9, s32[]{:T(128)S(6)} %select_n.2), kind=kOutput, calls=%fused_computation.15 | convolution fusion | flops 2153510400 | bytes 3775492 | tf_op jit(solution)/shard_map/conv_general_dilated | solution.py:8
  270.9 1.2 copy.124
  272.1 175.1 %all-reduce.10.cloned.1.call-done = (f32[3,3,128,512]{2,1,0,3:T(4,128)}, f32[3,3,128,512]{2,1,0,3:T(4,128)}) async-done(((f32[3,3,128,512]{2,1,0,3:T(4,128)}, f32[3,3,128,512]{2,1,0,3:T(4,128)}), (f32[3,3,128,512]{2,1,0,3:T(4,128)}, f32[3,3,128,512]{2,1,0,3:T(4,128)})) %all-reduce.10.cloned.1.call-update) | async-done | bytes 4718608
  447.2 1.1 constant_dynamic-slice_fusion.1
  448.3 1.1 constant_dynamic-slice_fusion
  449.3 0.7 copy.126
  450.1 0.7 copy.125
  (58 shorter events, 4.6 us)
Async XLA Ops:
  7.2 64.4 %reduce-scatter.3.cloned.1.call-start = ((), (), s32[]{:S(2)}) async-start(), calls=%async_computation.2 | async-start | bytes 6922240 | tf_op jit(solution)/shard_map/reduce_scatter | solution.py:61
  8.4 6.9 %copy-start.13 = (bf16[2,6,13,13,128]{4,2,3,1,0:T(8,128)(2,1)}, bf16[2,6,13,13,128]{4,2,3,1,0:T(8,128)(2,1)S(1)}, u32[]{:S(2)}) copy-start(bf16[2,6,13,13,128]{4,2,3,1,0:T(8,128)(2,1)S(1)} %copy.86) | copy-start | bytes 1557508
  15.3 0.8 copy-start.16
  15.3 118.2 %reduce-scatter.5.cloned.1.call-start = ((), (), s32[]{:S(2)}) async-start(), calls=%async_computation.3 | async-start | bytes 6922240 | tf_op jit(solution)/shard_map/reduce_scatter | solution.py:66
  80.0 1.1 copy-start.15
  80.0 83.8 %all-gather.3.cloned.1.call-start = ((), (), s32[]{:S(2)}) async-start(), calls=%async_computation.4 | async-start | bytes 3461120 | tf_op jit(solution)/shard_map/all_gather | solution.py:71
  136.8 63.5 %all-gather.5.cloned.1.call-start = ((), (), s32[]{:S(2)}) async-start(), calls=%async_computation.5 | async-start | bytes 3461120 | tf_op jit(solution)/shard_map/all_gather | solution.py:78
  163.7 10.0 %copy-start = (bf16[12,13,13,512]{3,0,2,1:T(8,128)(2,1)S(1)}, bf16[12,13,13,512]{3,0,2,1:T(8,128)(2,1)}, u32[]{:S(2)}) copy-start(bf16[12,13,13,512]{3,0,2,1:T(8,128)(2,1)} %all-gather.3.cloned.1.call-done) | copy-start | bytes 6230020
  173.4 273.8 %all-reduce.10.cloned.1.call-start = ((), (), s32[]{:S(2)}) async-start(), calls=%async_computation.6 | async-start | bytes 12582912
  173.7 1.8 copy-start.12
  175.5 1.1 copy-start.11
  177.2 1.1 copy-start.10
  177.8 1.2 copy-start.9
  178.8 1.2 copy-start.8
  179.6 1.2 copy-start.7
  180.6 1.2 copy-start.6
  182.8 17.4 %copy-start.14 = (bf16[2,6,13,13,128]{4,2,3,1,0:T(8,128)(2,1)S(1)}, bf16[2,6,13,13,128]{4,2,3,1,0:T(8,128)(2,1)}, u32[]{:S(2)}) copy-start(bf16[2,6,13,13,128]{4,2,3,1,0:T(8,128)(2,1)} %copy-done.13) | copy-start | bytes 1557508
  200.3 4.5 copy-start.2
  234.4 0.7 copy-start.17
  234.4 1.9 copy-start.5
  234.4 3.3 copy-start.1
  236.3 2.0 copy-start.3
  238.3 24.4 %copy-start.4 = (bf16[12,13,13,512]{3,0,2,1:T(8,128)(2,1)S(1)}, bf16[12,13,13,512]{3,0,2,1:T(8,128)(2,1)}, u32[]{:S(2)}) copy-start(bf16[12,13,13,512]{3,0,2,1:T(8,128)(2,1)} %all-gather.5.cloned.1.call-done) | copy-start | bytes 6230020
Sparse Core Ops, SparseCore 0:
  15.4 56.0 reduce-scatter.2
  80.1 53.3 reduce-scatter.4
  136.9 26.7 all-gather.2
  173.5 26.7 all-gather.4
  234.5 212.6 all-reduce.9
where the time goes:
time: 461 us; the launch traced here: 458 us
  waiting for transfers between devices  321 us (70%)
  matrix products  68.2 us (15%)
  blocking collectives  22.6 us (5%)
  local copies, waits for them, and re-layouts  22.4 us (5%)
  between operations  15 us (3%)
  other arithmetic  7.59 us (2%)
    unnamed x6, waiting for transfers between devices  175 us
    reduce_scatter x1, waiting for transfers between devices, body(): lax.psum_scatter(convolve(flat_in, own4), 'pipe', scatter_dimension=3, ti...  55.1 us
    reduce_scatter x1, waiting for transfers between devices, body(): lax.psum_scatter(convolve(hidden, own5), 'pipe', scatter_dimension=3, til...  52.3 us
    dot_general x18, matrix products, weight_grad(): jnp.einsum('nyxc,nyxd->cd', window, slope, preferred_element_type=jnp.flo...  37 us
    conv_general_dilated x4, matrix products, convolve(): lax.conv_general_dilated(field, kernel, (1, 1), 'SAME', dimension_numbers...  31.1 us
    all_gather x1, waiting for transfers between devices, body(): slope5_all = lax.all_gather(slope5, 'pipe', axis=3, tiled=True)  24.1 us
    unnamed x1, blocking collectives  22.6 us
    all_gather x1, waiting for transfers between devices, body(): slope4_all = lax.all_gather(slope4, 'pipe', axis=3, tiled=True)  14.6 us
  transfers between devices with their start and end apart: 5, of which 5 were waited for; matrix products, arithmetic and copies ran while one was open for 6% of the time, Pallas kernels for 0%

commit v1 on v0

v1 whole, which is shorter than its diff:
```python
import functools

import jax
import jax.numpy as jnp
from jax import lax
from jax.experimental import pallas as pl
from jax.experimental.pallas import tpu as pltpu
from jax.sharding import PartitionSpec as P

WIDE = 16
SLOTS = 8
BF16 = jnp.bfloat16
F32 = jnp.float32
VMEM_LIMIT = 16 * 1024 * 1024


def swap(value, axis_name, size, bit):
    return lax.ppermute(value, axis_name, [(i, i ^ bit) for i in range(size)])


def zero_edges(shifted):
    rows = shifted.shape[1]
    edge = jnp.zeros((shifted.shape[0], WIDE, shifted.shape[2]), BF16)
    shifted[:, :WIDE, :] = edge
    shifted[:, rows - WIDE :, :] = edge


def put_shifted(shifted, first_clip, lanes_of, value):
    clips, cells, width = value.shape
    flat = value.astype(F32).reshape(clips * cells, width)
    turned = (
        pltpu.roll(flat, 1, 0),
        flat,
        pltpu.roll(flat, clips * cells - 1, 0),
    )
    for tap, one in enumerate(turned):
        shifted[first_clip : first_clip + clips, WIDE : WIDE + cells, lanes_of(tap)] = (
            one.astype(BF16).reshape(clips, cells, width)
        )


def rows_of(shifted, tap):
    clips, rows, width = shifted.shape
    cells = rows - 2 * WIDE
    return shifted[:, tap * WIDE : tap * WIDE + cells, :].reshape(clips * cells, width)


def valid_of(info, clips, cells, side):
    column = lax.broadcasted_iota(jnp.int32, (clips * cells, 1), 0)
    inside = (column % WIDE) < side
    clip = column // cells
    live = clip < 0
    for n in range(clips):
        live = live | ((clip == n) & (info[2 + n] > 0))
    return (inside & live).astype(F32)


def fill_from_quarters(info, shifted, quarters):
    zero_edges(shifted)
    channels = shifted.shape[2] // 3
    share = quarters[0].shape[-1]
    for k, quarter in enumerate(quarters):
        at = (info[0] ^ k) * share

        def lanes(tap, at=at):
            return pl.ds(pl.multiple_of(tap * channels + at, share), share)

        put_shifted(shifted, 0, lanes, quarter[...])


def fill_whole(shifted, field):
    zero_edges(shifted)
    channels = shifted.shape[2] // 3
    share = 128
    for at in range(0, channels, share):

        def lanes(tap, at=at):
            return pl.ds(tap * channels + at, share)

        put_shifted(shifted, 0, lanes, field[:, :, at : at + share])


def forward_dot(shifted, weight_of):
    total = None
    for tap in range(3):
        block = weight_of(tap)
        term = jnp.dot(
            rows_of(shifted, tap),
            block.reshape(-1, block.shape[2]),
            preferred_element_type=F32,
        )
        total = term if total is None else total + term
    return total


def backward_dot(shifted, weight, rows):
    total = None
    for tap in range(3):
        first = 3 * (2 - tap)
        block = jnp.concatenate([weight[first + j, rows, :] for j in (2, 1, 0)], axis=1)
        term = lax.dot_general(
            rows_of(shifted, tap),
            block,
            (((1,), (1,)), ((), ())),
            preferred_element_type=F32,
        )
        total = term if total is None else total + term
    return total


def half_of(half, width):
    return pl.ds(pl.multiple_of(half * width, width), width)


def split_quarters(info, value):
    share = value.shape[1] // 2
    left, right = value[:, :share], value[:, share:]
    odd = (info[0] % 2) == 1
    return jnp.where(odd, right, left), jnp.where(odd, left, right)


def put_halves(info, half, value, kept, sent):
    size = value.shape[1] // 4
    left, right = value[:, : 2 * size], value[:, 2 * size :]
    place = info[1]
    crossed = ((place // 2) % 2) == 1
    low = jnp.where(crossed, right, left)
    high = jnp.where(crossed, left, right)
    first = lax.broadcasted_iota(jnp.int32, low.shape, 1) < size
    evens = jnp.where(first, low, pltpu.roll(high, size, 1))
    odds = jnp.where(first, pltpu.roll(low, size, 1), high)
    odd = (place % 2) == 1
    at = pl.ds(pl.multiple_of((half ^ (place // 4)) * 2 * size, 2 * size), 2 * size)
    shape = kept.shape[:2] + (2 * size,)
    kept[:, :, at] = jnp.where(odd, odds, evens).astype(BF16).reshape(shape)
    sent[:, :, at] = jnp.where(odd, evens, odds).astype(BF16).reshape(shape)


def fill_from_pair(info, shifted, same, other):
    zero_edges(shifted)
    share = same.shape[-1]
    for k, quarter in enumerate((same, other)):
        at = ((info[0] % 2) ^ k) * share

        def lanes(tap, at=at):
            return pl.ds(pl.multiple_of(2 * tap * share + at, share), share)

        put_shifted(shifted, 0, lanes, quarter[...])


def pick_kernel(info, pair, out, sem):
    copy = pltpu.make_async_copy(pair.at[1 - info[0] % 2], out, sem)
    copy.start()
    copy.wait()


def conv4_part_kernel(info, near, q1, weight, partial, rest, shifted, own, sems):
    depth = own.shape[1]

    def part_of(half):
        return weight.at[:, half_of(half, depth), :]

    first = pltpu.make_async_copy(part_of(info[0] // 2), own, sems.at[0])
    second = pltpu.make_async_copy(part_of(1 - info[0] // 2), rest, sems.at[1])
    first.start()
    second.start()
    fill_from_pair(info, shifted, near.at[info[0] % 2], q1)
    first.wait()

    @pl.loop(0, 2)
    def _(half):
        lanes = half_of(half, depth)
        partial[half] = forward_dot(shifted, lambda tap: own[3 * tap : 3 * tap + 3, :, lanes])

    second.wait()


def conv4_kernel(side, info, partial, far, q3, bias, weight, later, *refs):
    hidden, factor, fetched, shifted, sem = refs
    clips, cells, share = q3.shape
    copy = pltpu.make_async_copy(later, fetched, sem)
    copy.start()
    fill_from_pair(info, shifted, far.at[info[0] % 2], q3)
    valid = valid_of(info, clips, cells, side)

    @pl.loop(0, 2)
    def _(half):
        lanes = half_of(half, 2 * share)
        pre = forward_dot(shifted, lambda tap: weight[3 * tap : 3 * tap + 3, :, lanes])
        pre = pre + partial[half] + bias[half]
        sig = jax.nn.sigmoid(pre)
        factor[half] = valid * sig * (1.0 + pre * (1.0 - sig))
        even, odd = split_quarters(info, (valid * pre * sig).astype(BF16))
        pair = half ^ (info[0] // 2)
        hidden[pair] = even.reshape(q3.shape)
        hidden[2 + pair] = odd.reshape(q3.shape)

    copy.wait()


def conv5_kernel(side, info, hidden, c0, c1, c2, c3, bias, weight, *refs):
    o0, o1, o23, slope, kept, sent, shifted, upstream = refs
    clips, cells, share = c1.shape
    fill_from_quarters(info, shifted, (hidden.at[0], hidden.at[2], hidden.at[1], hidden.at[3]))
    for k, quarter in enumerate((c0.at[info[0] % 2], c1, c2.at[info[0] % 2], c3)):
        at = pl.multiple_of((info[0] ^ k) * share, share)
        upstream[:, pl.ds(at, share)] = quarter[...].reshape(clips * cells, share)
    valid = valid_of(info, clips, cells, side)

    @pl.loop(0, 2)
    def _(half):
        lanes = half_of(half, 2 * share)
        pre = forward_dot(shifted, lambda tap: weight[3 * tap : 3 * tap + 3, :, lanes])
        pre = pre + bias[half]
        sig = jax.nn.sigmoid(pre)
        put_outputs(info, half, (valid * pre * sig).astype(BF16), o0, o1, o23)
        cot = upstream[:, lanes].astype(F32)
        down = cot * valid * sig * (1.0 + pre * (1.0 - sig))
        slope[:, :, lanes] = down.astype(BF16).reshape(clips, cells, 2 * share)
        put_halves(info, half, down, kept, sent)


def put_outputs(info, half, value, o0, o1, o23):
    even, odd = split_quarters(info, value)
    even, odd = even.reshape(o0.shape), odd.reshape(o0.shape)

    @pl.when(half == info[0] // 2)
    def _():
        o0[...] = even
        o1[...] = odd

    @pl.when(half != info[0] // 2)
    def _():
        o23[0] = even
        o23[1] = odd


def back5_kernel(info, field, factor, weight, later, slope, kept, sent, fetched, shifted, sem):
    copy = pltpu.make_async_copy(later, fetched, sem)
    copy.start()
    fill_whole(shifted, field)
    width = field.shape[2] // 2

    @pl.loop(0, 2)
    def _(half):
        lanes = half_of(half, width)
        back = backward_dot(shifted, weight, lanes).astype(BF16).astype(F32)
        down = back * factor[half]
        slope[:, :, lanes] = down.astype(BF16).reshape(slope.shape[:2] + (width,))
        put_halves(info, half, down, kept, sent)

    copy.wait()


def back4_kernel(info, field, weight, o0, o1, o23, shifted):
    fill_whole(shifted, field)

    @pl.loop(0, 2)
    def _(half):
        back = backward_dot(shifted, weight, half_of(half, field.shape[2] // 2))
        put_outputs(info, half, back.astype(BF16), o0, o1, o23)


def join_kernel(side, info, p0, p1, far, p3, out):
    clips, cells, share = p0.shape
    for k, one in enumerate((p0, p1, far.at[0], p3)):
        value = one[...].reshape(clips, cells // WIDE, WIDE, share)
        first = pl.multiple_of((info[0] ^ k) * clips, clips)
        out[pl.ds(first, clips)] = value[:, :, :side, :]


def grad_kernel(chunks, sources, by_core, n_maps, info, *refs):
    n_outs = 2 * len(chunks)
    scratch = refs[-3:]
    outs = refs[-3 - n_outs : -3]
    shifted, slopes, turned = scratch
    slope_refs = refs[n_maps : n_maps + 4]
    clips, cells, channels = slope_refs[0].shape
    share = shifted.shape[2] // 6
    rows = clips * cells
    size = channels // 4
    zero_edges(shifted)
    for x_bit, quarter in enumerate(sources):
        for n, (at, index) in enumerate(quarter):

            def lanes(tap, x_bit=x_bit):
                return pl.ds((2 * tap + x_bit) * share, share)

            if by_core:
                index = index ^ (info[0] % 2)
            put_shifted(shifted, n * clips, lanes, refs[at][index])
    for n, one in enumerate(slope_refs):
        slopes[n * rows : (n + 1) * rows, :] = one[...].reshape(rows, channels)
    spare = slopes.shape[0] - 4 * rows
    slopes[4 * rows :, :] = jnp.zeros((spare, channels), BF16)
    turned[...] = slopes[...].T

    def place_of(chunk, u, x_bit):
        order = chunks[chunk][0]
        bits = {"x": x_bit, "a": u & 1, "b": u >> 1}
        return outs[2 * chunk + bits[order[0]]], 2 * bits[order[1]] + bits[order[2]]

    for i in range(3):
        window = jnp.concatenate(
            [rows_of(shifted, i), jnp.zeros((spare, shifted.shape[2]), BF16)], axis=0
        )
        part = jnp.dot(turned[...], window, preferred_element_type=F32).astype(BF16)
        for j in range(3):
            tap = 3 * i + j
            chunk = max(c for c in range(len(chunks)) if chunks[c][1] <= tap)
            first = (tap - chunks[chunk][1]) * size
            for x_bit in range(2):
                lane = (2 * j + x_bit) * share
                for u in range(4):
                    out, slot = place_of(chunk, u, x_bit)
                    out[slot, first : first + size, :] = part[
                        u * size : (u + 1) * size, lane : lane + share
                    ]
    total = jnp.sum(slopes[...].astype(F32), axis=0, keepdims=True)
    total = jnp.broadcast_to(total, (WIDE, channels))
    first = chunks[0][2] * size
    for u in range(4):
        both = total[:, 2 * size * (u // 2) : 2 * size * (u // 2 + 1)]
        row = (pltpu.roll(both, size, 1) if u % 2 else both).astype(BF16)
        for x_bit in range(2):
            out, slot = place_of(0, u, x_bit)
            out[slot, first : first + WIDE, :] = row


def body(sizes, features, clip_counts, conv4_weight, conv4_bias, conv5_weight, conv5_bias, cotangent):
    n_dp, n_pipe = sizes
    place = lax.axis_index("pipe")
    row = lax.axis_index("dp")
    micro, slots, side, _, share = features.shape
    group = micro * slots // n_pipe
    channels = conv4_weight.shape[3]
    cells = side * WIDE
    fine = n_dp // SLOTS
    size = channels // SLOTS

    def over_core(value):
        return swap(value, "pipe", n_pipe, 1)

    def over_x(value):
        return swap(value, "pipe", n_pipe, 2)

    def over_y(value):
        return swap(value, "dp", n_dp, fine)

    def over_a(value):
        return swap(value, "dp", n_dp, 2 * fine)

    def over_b(value):
        return swap(value, "dp", n_dp, 4 * fine)

    steps = {"x": over_x, "a": over_a, "b": over_b}

    live_count = jnp.sum(clip_counts, axis=1)
    slot = place * group + jnp.arange(group, dtype=jnp.int32)
    live = (slot % slots < live_count[slot // slots]).astype(jnp.int32)
    info = jnp.concatenate([jnp.stack([place, row // fine]).astype(jnp.int32), live])

    def wide(maps):
        flat = maps.reshape((micro * slots,) + maps.shape[2:])
        flat = jnp.pad(flat, ((0, 0), (0, 0), (0, WIDE - side), (0, 0)))
        return flat.reshape(micro * slots, cells, share)

    core = place % 2

    def clips_of(flat, start, count):
        return lax.dynamic_slice_in_dim(flat, start * group, count * group, 0)

    flat = wide(features)
    pair_dims = (2, group, cells, share)
    near = clips_of(flat, place - core, 2).reshape(pair_dims)
    far = over_x(clips_of(flat, (place - core) ^ 2, 2).reshape(pair_dims))
    q1 = over_core(clips_of(flat, place ^ 1, 1))

    flat = wide(cotangent)
    cot_near = clips_of(flat, place - core, 2).reshape(pair_dims)
    cot_far = over_x(clips_of(flat, (place - core) ^ 2, 2).reshape(pair_dims))


    weight_t = jax.ShapeDtypeStruct((9, channels, channels), BF16)
    weight4 = pltpu.with_memory_space_constraint(conv4_weight.reshape(weight_t.shape), pltpu.HBM)
    weight5 = pltpu.with_memory_space_constraint(conv5_weight.reshape(weight_t.shape), pltpu.HBM)
    bias4 = conv4_bias.reshape(2, 1, channels // 2)
    bias5 = conv5_bias.reshape(2, 1, channels // 2)
    half = channels // 2

    def shape_of(*dims, kind=BF16):
        return jax.ShapeDtypeStruct(dims, kind)

    quarter_t = shape_of(group, cells, share)
    pair_t = shape_of(2, group, cells, share)
    four_t = shape_of(4, group, cells, share)
    half_t = shape_of(group, cells, half)
    whole_t = shape_of(group, cells, channels)
    factor_t = shape_of(2, group * cells, half, kind=F32)

    vmem = pl.BlockSpec(memory_space=pltpu.VMEM)
    anywhere = pl.BlockSpec(memory_space=pl.ANY)
    hbm = pl.BlockSpec(memory_space=pltpu.HBM)

    def shifted_of(depth):
        return pltpu.VMEM((group, cells + 2 * WIDE, 3 * depth), BF16)

    work = 2 * group * cells * 9 * channels * channels

    def call(kernel, name, grid, in_specs, out_specs, out_shape, scratch=(), after=(), flops=0, limit=VMEM_LIMIT):
        n_in = len(in_specs)

        def run(info, *refs):
            kernel(info, *refs[:n_in], *refs[n_in + len(after) :])

        called = pl.pallas_call(
            run,
            grid_spec=pltpu.PrefetchScalarGridSpec(
                num_scalar_prefetch=1,
                grid=grid,
                in_specs=in_specs + [anywhere] * len(after),
                out_specs=out_specs,
                scratch_shapes=scratch,
            ),
            out_shape=out_shape,
            compiler_params=pltpu.CompilerParams(vmem_limit_bytes=limit),
            cost_estimate=pl.CostEstimate(
                flops=flops, bytes_accessed=0, transcendentals=0
            ),
            name=name,
        )
        return lambda *args: called(info, *args, *after)

    def picked(pair):
        (part,) = call(
            pick_kernel,
            "pick",
            (),
            [anywhere],
            [anywhere],
            [quarter_t],
            [pltpu.SemaphoreType.DMA],
            limit=1024 * 1024,
        )(pair)
        return part

    def kernel_grad(name, chunks, sources, by_core, maps, slopes, after):
        out_shape = []
        for n, (_, _, taps) in enumerate(chunks):
            rows = taps * size + (0 if n else WIDE)
            out_shape += [shape_of(4, rows, share)] * 2
        depth = -(-4 * group * cells // 256) * 256
        return call(
            functools.partial(grad_kernel, chunks, sources, by_core, len(maps)),
            name,
            (),
            [vmem] * (len(maps) + 4),
            [vmem] * len(out_shape),
            out_shape,
            [
                pltpu.VMEM((4 * group, cells + 2 * WIDE, 6 * share), BF16),
                pltpu.VMEM((depth, half), BF16),
                pltpu.VMEM((half, depth), BF16),
            ],
            after,
            flops=work * 0 // 8,
        )(*maps, *slopes)

    def held(name, values, after):
        return pl.pallas_call(
            lambda *refs: None,
            in_specs=[anywhere] * (len(values) + len(after)),
            out_specs=[anywhere] * len(values),
            out_shape=[shape_of(*value.shape) for value in values],
            input_output_aliases={n: n for n in range(len(values))},
            compiler_params=pltpu.CompilerParams(vmem_limit_bytes=1024 * 1024),
            cost_estimate=pl.CostEstimate(flops=0, bytes_accessed=0, transcendentals=0),
            name=name,
        )(*values, *after)

    def sends(blocks, chunks):
        kept, sent = blocks[0::2], blocks[1::2]
        return kept, [steps[chunk[0][0]](one) for chunk, one in zip(chunks, sent)]

    def halved(total, chunk, level, after=()):
        cut = total.shape[0] // 2
        kept, moved = total[:cut], steps[chunk[0][level]](total[cut:])
        if after:
            (kept,) = held("after_step", [kept], after)
        return kept + moved

    def finished(totals, chunks):
        totals = [total[0] for total in totals]
        at = chunks[0][2] * size
        bias = totals[0][at:]
        parts = [totals[0][:at]] + totals[1:]
        parts = [part.reshape(-1, size, share) for part in parts]
        bit = fine // 2
        while bit:
            mine = (row // bit) % 2
            bias = bias + swap(bias, "dp", n_dp, bit)
            for n, part in enumerate(parts):
                cut = part.shape[1] // 2
                sent = lax.dynamic_slice_in_dim(part, (1 - mine) * cut, cut, 1)
                kept = lax.dynamic_slice_in_dim(part, mine * cut, cut, 1)
                parts[n] = kept + swap(sent, "dp", n_dp, bit)
            bit //= 2
        per_dp = channels // n_dp
        own = lax.dynamic_slice_in_dim(bias[0], (row % fine) * per_dp, per_dp, 0)
        grads = jnp.concatenate([part.transpose(0, 2, 1).astype(F32) for part in parts])
        return grads.reshape(3, 3, share, per_dp), own.astype(F32)

    def joined(name, o0, o1, far, o3, after):
        (maps,) = call(
            functools.partial(join_kernel, side),
            name,
            (),
            [vmem] * 4,
            [vmem],
            [shape_of(micro * slots, side, side, share)],
            after=[after],
            flops=work * 0 // 8,
        )(o0, o1, far, o3)
        return maps.reshape(features.shape)

    partial4, rest4 = call(
        conv4_part_kernel,
        "conv4_part",
        (),
        [vmem] * 2 + [hbm],
        [vmem] * 2,
        [factor_t, shape_of(9, half, channels)],
        [
            shifted_of(half),
            pltpu.VMEM((9, half, channels), BF16),
            pltpu.SemaphoreType.DMA((2,)),
        ],
        flops=work * 0 // 8,
    )(near, q1, weight4)
    (far,) = held("after_part", [far], [partial4])
    q3 = over_core(picked(far))
    cot1 = over_core(picked(cot_near))
    near_y = over_y(near)
    far_y = over_y(far)

    hidden, factor4, near5 = call(
        functools.partial(conv4_kernel, side),
        "conv4",
        (),
        [vmem] * 5 + [hbm],
        [vmem] * 3,
        [four_t, factor_t, weight_t],
        [shifted_of(half), pltpu.SemaphoreType.DMA],
        [near_y],
        flops=work * 0 // 8,
    )(partial4, far, q3, bias4, rest4, weight5)
    hidden_y = over_y(hidden)
    (cot_far,) = held("after_conv4", [cot_far], [factor4])
    cots = [cot_near, cot1, cot_far, over_core(picked(cot_far))]

    *outs, slope5, kept5, sent5 = call(
        functools.partial(conv5_kernel, side),
        "conv5",
        (),
        [vmem] * 7,
        [vmem] * 6,
        [quarter_t, quarter_t, pair_t, whole_t, half_t, half_t],
        [shifted_of(channels), pltpu.VMEM((group * cells, channels), BF16)],
        [far_y],
        flops=work * 0 // 8,
    )(hidden, *cots, bias5, near5)
    out_far = over_x(outs[2])
    hidden_core = over_core(hidden[2:])


    kept5_core, across5 = over_core(kept5), over_y(sent5)

    slope4, kept4, sent4, near4 = call(
        back5_kernel,
        "back5",
        (),
        [vmem] * 3 + [hbm],
        [vmem] * 4,
        [whole_t, half_t, half_t, weight_t],
        [shifted_of(channels), pltpu.SemaphoreType.DMA],
        [hidden_core],
        flops=work * 0 // 8,
    )(slope5, factor4, near5, weight4)
    kept4_core, across4 = over_core(kept4), over_y(sent4)

    backs = call(
        back4_kernel,
        "back4",
        (),
        [vmem] * 2,
        [vmem] * 3,
        [quarter_t, quarter_t, pair_t],
        [shifted_of(channels)],
        [kept5_core],
        flops=work * 8 // 8,
    )(slope4, near4)
    back_far = over_x(backs[2])

    across5, hidden_y, out_far = held("after_back", [across5, hidden_y, out_far], [backs[0]])
    out3 = over_core(out_far[1])

    hidden_both, across5_core = over_core(hidden_y[2:]), over_core(across5)

    chunks5 = (("xab", 0, 4), ("axb", 4, 5))
    own, other = 0, 1
    chunks4 = (("axb", 0, 5), ("xab", 5, 4))
    blocks5 = kernel_grad(
        "grad5",
        chunks5,
        (((0, 0), (1, 0), (2, 0), (3, 0)), ((0, 1), (1, 1), (2, 1), (3, 1))),
        False,
        (hidden, hidden_core, hidden_y, hidden_both),
        (kept5, kept5_core, across5, across5_core),
        [out3, kept4_core, backs[0]],
    )
    (across4,) = held("after_grad5", [across4], [blocks5[0], back_far])
    across4_core = over_core(across4)
    blocks4 = kernel_grad(
        "grad4",
        chunks4,
        (((0, own), (0, other), (2, own), (2, other)), ((1, own), (1, other), (3, own), (3, other))),
        True,
        (near, far, near_y, far_y),
        (kept4, kept4_core, across4, across4_core),
        [blocks5[0]],
    )

    kept5, moved5 = sends(blocks5, chunks5)
    kept4, moved4 = sends(blocks4, chunks4)
    a4_0, b4_0 = [kept + moved for kept, moved in zip(kept4, moved4)]
    a4_1 = halved(a4_0, chunks4[0], 1)
    b4_1 = halved(b4_0, chunks4[1], 1)
    a4_2 = halved(a4_1, chunks4[0], 2)
    b4_2 = halved(b4_1, chunks4[1], 2)
    a5_0 = held("after_grad4", kept5[:1], [blocks4[0]])[0] + moved5[0]
    b5_0 = held("after_grad4", kept5[1:], [blocks4[0]])[0] + moved5[1]
    a5_1 = halved(a5_0, chunks5[0], 1, [a4_0])
    b5_1 = halved(b5_0, chunks5[1], 1, [b4_0])
    a5_2 = halved(a5_1, chunks5[0], 2, [b4_1])
    b5_2 = halved(b5_1, chunks5[1], 2, [b4_1])
    out1, = held("after_step", [outs[1]], [b5_0])
    out1_core = over_core(out1)


    back1, back_far = held("after_step", [backs[1], back_far], [a4_0])
    conv5_out = joined("join_out", outs[0], out1_core, out_far, out3, b4_1)
    input_grad = joined(
        "join_grad", backs[0], over_core(back1), back_far, over_core(back_far[1]), b4_0
    )
    grad_w5, grad_b5 = finished([a5_2, b5_2], chunks5)
    grad_w4, grad_b4 = finished([a4_2, b4_2], chunks4)
    return (conv5_out, input_grad, grad_w4, grad_b4, grad_w5, grad_b5)


def solution(mesh):
    sizes = (mesh.shape["dp"], mesh.shape["pipe"])
    return jax.shard_map(
        functools.partial(body, sizes),
        mesh=mesh,
        in_specs=(
            P(None, "dp", None, None, "pipe"),
            P(None, "dp"),
            P(),
            P(),
            P(),
            P(),
            P(None, "dp", None, None, "pipe"),
        ),
        out_specs=(
            P(None, "dp", None, None, "pipe"),
            P(None, "dp", None, None, "pipe"),
            P(None, None, "pipe", "dp"),
            P("dp"),
            P(None, None, "pipe", "dp"),
            P("dp"),
        ),
        check_vma=False,
    )
```

time: 461 us -> 91.7 us (0.20)
  waiting for transfers between devices: 321 us -> 13.8 us
  matrix products: 68.2 us -> 0 us
  Pallas kernels: 0 us -> 34.4 us
  starting transfers between devices: 0.46 us -> 32.9 us
  blocking collectives: 22.6 us -> 0 us
  local copies, waits for them, and re-layouts: 22.4 us -> 5.88 us
  between operations: 15 us -> 1.17 us
    unnamed x6 -> x0, waiting for transfers between devices: 175 us -> none
    reduce_scatter x2 -> x0, waiting for transfers between devices: 107 us -> none  [the longest x1 55.1 us: body(): lax.psum_scatter(convolve(flat_in, own4), 'pipe', scatter_dimension=3, ti...]
    all_gather x2 -> x0, waiting for transfers between devices: 38.7 us -> none  [the longest x1 24.1 us: body(): slope5_all = lax.all_gather(slope5, 'pipe', axis=3, tiled=True)]
    dot_general x18 -> x0, matrix products: 37 us -> none  [weight_grad(): jnp.einsum('nyxc,nyxd->cd', window, slope, preferred_element_type=jnp.flo...]
    pallas_call x0 -> x24, Pallas kernels: none -> 34.4 us  [the longest x12 34.4 us: call(): return lambda *args: called(info, *args, *after)]
    ppermute x0 -> x35, starting transfers between devices: none -> 32.9 us  [swap(): return lax.ppermute(value, axis_name, [(i, i ^ bit) for i in range(size)])]
    conv_general_dilated x4 -> x0, matrix products: 31.1 us -> none  [convolve(): lax.conv_general_dilated(field, kernel, (1, 1), 'SAME', dimension_numbers...]
    unnamed x1 -> x0, blocking collectives: 22.6 us -> none
  transfers between devices with their start and end apart: 5 -> 35, of which waited for: 5 -> 11; matrix products, arithmetic and copies ran while one was open for 6% -> 7% of each run, Pallas kernels for 0% -> 38%
where the time goes in v1:
time: 91.7 us; the launch traced here: 91.5 us
  Pallas kernels  34.4 us (38%)
  starting transfers between devices  32.9 us (36%)
  waiting for transfers between devices  13.8 us (15%)
  local copies, waits for them, and re-layouts  5.88 us (6%)
  other arithmetic  3.31 us (4%)
  between operations  1.17 us (1%)
    pallas_call x12, Pallas kernels, call(): return lambda *args: called(info, *args, *after)  34.4 us
    ppermute x35, starting transfers between devices, swap(): return lax.ppermute(value, axis_name, [(i, i ^ bit) for i in range(size)])  32.9 us
    ppermute x35, waiting for transfers between devices, swap(): return lax.ppermute(value, axis_name, [(i, i ^ bit) for i in range(size)])  13.8 us
    unnamed x10, local copies, waits for them, and re-layouts  4.69 us
  transfers between devices with their start and end apart: 35, of which 11 were waited for; matrix products, arithmetic and copies ran while one was open for 7% of the time, Pallas kernels for 38%

profile of v1, /device:TPU:0, one launch (start us, length us, event | category | flops | bytes accessed | tf_op | source)
XLA Modules:
  0.0 91.5 jit_solution(9219329162972295380)
XLA Ops:
  0.7 1.1 %copy.30 = bf16[2,6,13,13,128]{4,3,2,1,0:T(8,128)(2,1)S(1)} copy(bf16[2,6,13,13,128]{4,0,3,2,1:T(2,128)(2,1)} %param.7) | data formatting | bytes 1038336 | tf_op args[0]
  2.0 0.5 collective-permute-start
  2.5 2.6 %collective-permute-start.1 = (bf16[2,3,208,128]{3,2,1,0:T(8,128)(2,1)S(1)}, bf16[2,3,208,128]{3,2,1,0:T(8,128)(2,1)S(1)}, u32[]{:S(2)}, u32[]{:S(2)}) collective-permute-start(bf16[2,3,208,128]{3,2,1,0:T(8,128)(2,1)S(1)} %bitcast.70), channel_id=1, source_target_pairs={{0,2},{1,3},{2,0},{3,1},{4,6},{5,7},{6,4},{7,5},{8,10},{9,11},{10,... | collective-permute-start | bytes 958472 | tf_op jit(solution)/shard_map/ppermute | solution.py:18
  5.1 1.5 %collective-permute-start.3 = (bf16[2,3,208,128]{3,2,1,0:T(8,128)(2,1)S(1)}, bf16[2,3,208,128]{3,2,1,0:T(8,128)(2,1)S(1)}, u32[]{:S(2)}, u32[]{:S(2)}) collective-permute-start(bf16[2,3,208,128]{3,2,1,0:T(8,128)(2,1)S(1)} %bitcast.48), channel_id=1, source_target_pairs={{0,4},{4,0},{8,12},{12,8},{16,20},{20,16},{24,28},{28,24},{1,5},{5... | collective-permute-start | bytes 958472 | tf_op jit(solution)/shard_map/ppermute | solution.py:18
  6.6 1.1 %copy.31 = bf16[2,6,13,13,128]{4,3,2,1,0:T(8,128)(2,1)S(1)} copy(bf16[2,6,13,13,128]{4,0,3,2,1:T(2,128)(2,1)} %param.13) | data formatting | bytes 1038336 | tf_op args[6]
  8.0 0.6 collective-permute-start.5
  8.7 0.6 gather_fusion
  9.5 4.2 %conv4_part.1 = (f32[2,624,256]{2,1,0:T(8,128)S(1)}, bf16[9,256,512]{2,1,0:T(8,128)(2,1)S(1)}) custom-call(s32[5]{0:T(128)S(1)} %pad_add_fusion.info, bf16[2,3,208,128]{3,2,1,0:T(8,128)(2,1)S(1)} %bitcast.49, bf16[3,208,128]{2,1,0:T(8,128)(2,1)S(1)} %collective-permute-done.refs_1_, bf16[9,512,512]{2,1,0:T(8,128)(2,1)} %bitcast.57), custom_call_target="tpu_custom_call" | custom-call | tf_op jit(solution)/shard_map/conv4_part/pallas_call | solution.py:432
  13.7 0.8 pick.3
  14.5 1.9 %collective-permute-start.7 = (bf16[2,3,208,128]{3,2,1,0:T(8,128)(2,1)S(1)}, bf16[2,3,208,128]{3,2,1,0:T(8,128)(2,1)S(1)}, u32[]{:S(2)}, u32[]{:S(2)}) collective-permute-start(bf16[2,3,208,128]{3,2,1,0:T(8,128)(2,1)S(1)} %after_part.1.refs_0_.refs_1_), channel_id=1, source_target_pairs={{0,4},{4,0},{8,12},{12,8},{16,20},{20,16},{24,28},{28,24},{1,5},{5... | collective-permute-start | bytes 958472 | tf_op jit(solution)/shard_map/ppermute | solution.py:18
  16.4 0.8 pick.4
  17.4 3.2 %conv4.1 = (bf16[4,3,208,128]{3,2,1,0:T(8,128)(2,1)S(1)}, f32[2,624,256]{2,1,0:T(8,128)S(1)}, bf16[9,512,512]{2,1,0:T(8,128)(2,1)S(1)}) custom-call(s32[5]{0:T(128)S(1)} %pad_add_fusion.info, f32[2,624,256]{2,1,0:T(8,128)S(1)} %get-tuple-element.37.refs_1_.refs_0_, bf16[2,3,208,128]{3,2,1,0:T(8,128)(2,1)S(1)} %after_part.1.refs_0_.refs_1_, ...), custom_call_target="tpu_custom_call" | custom-call | tf_op jit(solution)/shard_map/conv4/pallas_call | solution.py:432
  20.7 0.8 pick.5
  21.8 1.0 %collective-permute-start.10 = (bf16[4,3,208,128]{3,2,1,0:T(8,128)(2,1)S(1)}, bf16[4,3,208,128]{3,2,1,0:T(8,128)(2,1)S(1)}, u32[]{:S(2)}, u32[]{:S(2)}) collective-permute-start(bf16[4,3,208,128]{3,2,1,0:T(8,128)(2,1)S(1)} %get-tuple-element.39.refs_0_), channel_id=1, source_target_pairs={{0,4},{4,0},{8,12},{12,8},{16,20},{20,16},{24,28},{28,24},{1,5},{5... | collective-permute-start | bytes 1916936 | tf_op jit(solution)/shard_map/ppermute | solution.py:18
  23.1 1.4 %collective-permute-done.7.refs_7_.refs_3_ = bf16[2,3,208,128]{3,2,1,0:T(8,128)(2,1)S(1)} collective-permute-done((bf16[2,3,208,128]{3,2,1,0:T(8,128)(2,1)S(1)}, bf16[2,3,208,128]{3,2,1,0:T(8,128)(2,1)S(1)}, u32[]{:S(2)}, u32[]{:S(2)}) %collective-permute-start.7) | collective-permute-done | bytes 319520 | tf_op jit(solution)/shard_map/ppermute | solution.py:18
  24.5 5.6 %conv5.1 = (bf16[3,208,128]{2,1,0:T(8,128)(2,1)S(1)}, bf16[3,208,128]{2,1,0:T(8,128)(2,1)S(1)}, bf16[2,3,208,128]{3,2,1,0:T(8,128)(2,1)S(1)}, bf16[3,208,512]{2,...) custom-call(s32[5]{0:T(128)S(1)} %pad_add_fusion.info, ...), custom_call_target="tpu_custom_call" | custom-call | tf_op jit(solution)/shard_map/conv5/pallas_call | solution.py:432
  30.2 1.9 %collective-permute-start.11 = (bf16[2,3,208,128]{3,2,1,0:T(8,128)(2,1)S(1)}, bf16[2,3,208,128]{3,2,1,0:T(8,128)(2,1)S(1)}, u32[]{:S(2)}, u32[]{:S(2)}) collective-permute-start(bf16[2,3,208,128]{3,2,1,0:T(8,128)(2,1)S(1)} %get-tuple-element.45), channel_id=1, source_target_pairs={{0,2},{1,3},{2,0},{3,1},{4,6},{5,7},{6,4},{7,5},{8,10},{9,11},{10,... | collective-permute-start | bytes 958472 | tf_op jit(solution)/shard_map/ppermute | solution.py:18
  32.1 1.8 %collective-permute-start.9 = (bf16[3,208,256]{2,1,0:T(8,128)(2,1)S(1)}, bf16[3,208,256]{2,1,0:T(8,128)(2,1)S(1)}, u32[]{:S(2)}, u32[]{:S(2)}) collective-permute-start(bf16[3,208,256]{2,1,0:T(8,128)(2,1)S(1)} %get-tuple-element.44), channel_id=1, source_target_pairs={{0,4},{4,0},{8,12},{12,8},{16,20},{20,16},{24,28},{28,24},{1,5},{5... | collective-permute-start | bytes 958472 | tf_op jit(solution)/shard_map/ppermute | solution.py:18
  33.9 4.5 %back5.1 = (bf16[3,208,512]{2,1,0:T(8,128)(2,1)S(1)}, bf16[3,208,256]{2,1,0:T(8,128)(2,1)S(1)}, bf16[3,208,256]{2,1,0:T(8,128)(2,1)S(1)}, bf16[9,512,512]{2,1,0:T(8,128)(2,1)S(1)}) custom-call(s32[5]{0:T(128)S(1)} %pad_add_fusion.info, bf16[3,208,512]{2,1,0:T(8,128)(2,1)S(1)} %get-tuple-element.46.refs_0_, f32[2,624,256]{2,1,0:T(8,128)S(1)} %get-tuple-element.40.refs_1_, ...), custom_call_target="tpu_custom_call" | custom-call | tf_op jit(solution)/shard_map/back5/pallas_call | solution.py:432
  38.8 4.6 %back4.1 = (bf16[3,208,128]{2,1,0:T(8,128)(2,1)S(1)}, bf16[3,208,128]{2,1,0:T(8,128)(2,1)S(1)}, bf16[2,3,208,128]{3,2,1,0:T(8,128)(2,1)S(1)}) custom-call(s32[5]{0:T(128)S(1)} %pad_add_fusion.info, bf16[3,208,512]{2,1,0:T(8,128)(2,1)S(1)} %get-tuple-element.47.refs_0_, bf16[9,512,512]{2,1,0:T(8,128)(2,1)S(1)} %get-tuple-element.48.refs_1_, ...), custom_call_target="tpu_custom_call" | custom-call | flops 2944401408 | tf_op jit(solution)/shard_map/back4/pallas_call | solution.py:432
  43.9 2.0 %collective-permute-done.9.refs_0_ = bf16[3,208,256]{2,1,0:T(8,128)(2,1)S(1)} collective-permute-done((bf16[3,208,256]{2,1,0:T(8,128)(2,1)S(1)}, bf16[3,208,256]{2,1,0:T(8,128)(2,1)S(1)}, u32[]{:S(2)}, u32[]{:S(2)}) %collective-permute-start.9) | collective-permute-done | bytes 319520 | tf_op jit(solution)/shard_map/ppermute | solution.py:18
  46.7 1.6 %collective-permute-done.15.refs_8_.refs_3_ = bf16[3,208,128]{2,1,0:T(8,128)(2,1)S(1)} collective-permute-done((bf16[3,208,128]{2,1,0:T(8,128)(2,1)S(1)}, bf16[3,208,128]{2,1,0:T(8,128)(2,1)S(1)}, u32[]{:S(2)}, u32[]{:S(2)}) %collective-permute-start.15) | collective-permute-done | bytes 159776 | tf_op jit(solution)/shard_map/ppermute | solution.py:18
  48.3 4.3 %grad5.1 = (bf16[4,272,128]{2,1,0:T(8,128)(2,1)S(1)}, bf16[4,272,128]{2,1,0:T(8,128)(2,1)S(1)}, bf16[4,320,128]{2,1,0:T(8,128)(2,1)S(1)}, bf16[4,320,128]{2,1,0:T(8,128)(2,1)S(1)}) custom-call(s32[5]{0:T(128)S(1)} %pad_add_fusion.info, bf16[4,3,208,128]{3,2,1,0:T(8,128)(2,1)S(1)} %get-tuple-element.39.refs_0_, ...), custom_call_target="tpu_custom_call" | custom-call | tf_op jit(solution)/shard_map/grad5/pallas_call | solution.py:432
  52.7 1.6 %collective-permute-start.20 = (bf16[4,320,128]{2,1,0:T(8,128)(2,1)S(1)}, bf16[4,320,128]{2,1,0:T(8,128)(2,1)S(1)}, u32[]{:S(2)}, u32[]{:S(2)}) collective-permute-start(bf16[4,320,128]{2,1,0:T(8,128)(2,1)S(1)} %get-tuple-element.60), channel_id=1, source_target_pairs={{0,8},{4,12},{8,0},{12,4},{16,24},{20,28},{24,16},{28,20},{1,9},{5... | collective-permute-start | bytes 983048 | tf_op jit(solution)/shard_map/ppermute | solution.py:18
  54.3 1.6 %collective-permute-start.30 = (bf16[4,272,128]{2,1,0:T(8,128)(2,1)S(1)}, bf16[4,272,128]{2,1,0:T(8,128)(2,1)S(1)}, u32[]{:S(2)}, u32[]{:S(2)}) collective-permute-start(bf16[4,272,128]{2,1,0:T(8,128)(2,1)S(1)} %get-tuple-element.67), channel_id=1, source_target_pairs={{0,2},{1,3},{2,0},{3,1},{4,6},{5,7},{6,4},{7,5},{8,10},{9,11},{10,... | collective-permute-start | bytes 835592 | tf_op jit(solution)/shard_map/ppermute | solution.py:18
  55.9 4.3 %grad4.1 = (bf16[4,336,128]{2,1,0:T(8,128)(2,1)S(1)}, bf16[4,336,128]{2,1,0:T(8,128)(2,1)S(1)}, bf16[4,256,128]{2,1,0:T(8,128)(2,1)S(1)}, bf16[4,256,128]{2,1,0:T(8,128)(2,1)S(1)}) custom-call(s32[5]{0:T(128)S(1)} %pad_add_fusion.info, bf16[2,3,208,128]{3,2,1,0:T(8,128)(2,1)S(1)} %bitcast.50, bf16[2,3,208,128]{3,2,1,0:T(8,128)(2,1)S(1)} %after_part.1.refs_0_.refs_1_, ...), custom_call_target="tpu_custom_call" | custom-call | tf_op jit(solution)/shard_map/grad4/pallas_call | solution.py:432
  60.7 1.5 %collective-permute-start.22 = (bf16[4,256,128]{2,1,0:T(8,128)(2,1)S(1)}, bf16[4,256,128]{2,1,0:T(8,128)(2,1)S(1)}, u32[]{:S(2)}, u32[]{:S(2)}) collective-permute-start(bf16[4,256,128]{2,1,0:T(8,128)(2,1)S(1)} %get-tuple-element.62), channel_id=1, source_target_pairs={{0,2},{1,3},{2,0},{3,1},{4,6},{5,7},{6,4},{7,5},{8,10},{9,11},{10,... | collective-permute-start | bytes 786440 | tf_op jit(solution)/shard_map/ppermute | solution.py:18
  62.2 1.3 %collective-permute-done.30 = bf16[4,272,128]{2,1,0:T(8,128)(2,1)S(1)} collective-permute-done((bf16[4,272,128]{2,1,0:T(8,128)(2,1)S(1)}, bf16[4,272,128]{2,1,0:T(8,128)(2,1)S(1)}, u32[]{:S(2)}, u32[]{:S(2)}) %collective-permute-start.30) | collective-permute-done | bytes 278560 | tf_op jit(solution)/shard_map/ppermute | solution.py:18
  63.7 1.6 %collective-permute-start.33 = (bf16[2,320,128]{2,1,0:T(8,128)(2,1)S(1)}, bf16[2,320,128]{2,1,0:T(8,128)(2,1)S(1)}, u32[]{:S(2)}, u32[]{:S(2)}) collective-permute-start(bf16[2,320,128]{2,1,0:T(8,128)(2,1)S(1)} %get-tuple-element.84), channel_id=1, source_target_pairs={{0,2},{1,3},{2,0},{3,1},{4,6},{5,7},{6,4},{7,5},{8,10},{9,11},{10,... | collective-permute-start | bytes 491528 | tf_op jit(solution)/shard_map/ppermute | solution.py:18
  65.3 1.0 %collective-permute-start.31 = (bf16[2,272,128]{2,1,0:T(8,128)(2,1)S(1)}, bf16[2,272,128]{2,1,0:T(8,128)(2,1)S(1)}, u32[]{:S(2)}, u32[]{:S(2)}) collective-permute-start(bf16[2,272,128]{2,1,0:T(8,128)(2,1)S(1)} %get-tuple-element.86), channel_id=1, source_target_pairs={{0,8},{4,12},{8,0},{12,4},{16,24},{20,28},{24,16},{28,20},{1,9},{5... | collective-permute-start | bytes 417800 | tf_op jit(solution)/shard_map/ppermute | solution.py:18
  66.3 3.6 %collective-permute-done.22 = bf16[4,256,128]{2,1,0:T(8,128)(2,1)S(1)} collective-permute-done((bf16[4,256,128]{2,1,0:T(8,128)(2,1)S(1)}, bf16[4,256,128]{2,1,0:T(8,128)(2,1)S(1)}, u32[]{:S(2)}, u32[]{:S(2)}) %collective-permute-start.22) | collective-permute-done | bytes 262176 | tf_op jit(solution)/shard_map/ppermute | solution.py:18
  70.0 1.6 %collective-permute-start.23 = (bf16[2,256,128]{2,1,0:T(8,128)(2,1)S(1)}, bf16[2,256,128]{2,1,0:T(8,128)(2,1)S(1)}, u32[]{:S(2)}, u32[]{:S(2)}) collective-permute-start(bf16[2,256,128]{2,1,0:T(8,128)(2,1)S(1)} %slice.107), channel_id=1, source_target_pairs={{0,8},{4,12},{8,0},{12,4},{16,24},{20,28},{24,16},{28,20},{1,9},{5... | collective-permute-start | bytes 393224 | tf_op jit(solution)/shard_map/ppermute | solution.py:18
  71.7 0.8 collective-permute-done.33
  72.6 2.7 %collective-permute-start.34 = (bf16[1,320,128]{2,1,0:T(8,128)(2,1)S(1)}, bf16[1,320,128]{2,1,0:T(8,128)(2,1)S(1)}, u32[]{:S(2)}, u32[]{:S(2)}) collective-permute-start(bf16[1,320,128]{2,1,0:T(8,128)(2,1)S(1)} %get-tuple-element.88), channel_id=1, source_target_pairs={{0,16},{4,20},{8,24},{12,28},{16,0},{20,4},{24,8},{28,12},{1,17},{... | collective-permute-start | bytes 245768 | tf_op jit(solution)/shard_map/ppermute | solution.py:18
  75.4 1.5 %collective-permute-start.32 = (bf16[1,272,128]{2,1,0:T(8,128)(2,1)S(1)}, bf16[1,272,128]{2,1,0:T(8,128)(2,1)S(1)}, u32[]{:S(2)}, u32[]{:S(2)}) collective-permute-start(bf16[1,272,128]{2,1,0:T(8,128)(2,1)S(1)} %get-tuple-element.90), channel_id=1, source_target_pairs={{0,16},{4,20},{8,24},{12,28},{16,0},{20,4},{24,8},{28,12},{1,17},{... | collective-permute-start | bytes 208904 | tf_op jit(solution)/shard_map/ppermute | solution.py:18
  76.9 1.5 %collective-permute-start.27 = (bf16[2,336,128]{2,1,0:T(8,128)(2,1)S(1)}, bf16[2,336,128]{2,1,0:T(8,128)(2,1)S(1)}, u32[]{:S(2)}, u32[]{:S(2)}) collective-permute-start(bf16[2,336,128]{2,1,0:T(8,128)(2,1)S(1)} %slice.109), channel_id=1, source_target_pairs={{0,2},{1,3},{2,0},{3,1},{4,6},{5,7},{6,4},{7,5},{8,10},{9,11},{10,... | collective-permute-start | bytes 516104 | tf_op jit(solution)/shard_map/ppermute | solution.py:18
  78.6 0.6 collective-permute-start.25
  79.1 0.7 join_out.1
  79.8 1.2 %copy.32 = bf16[2,6,13,13,128]{4,0,3,2,1:T(2,128)(2,1)} copy(bf16[2,6,13,13,128]{4,3,2,1,0:T(8,128)(2,1)S(1)} %bitcast.54) | data formatting | bytes 1038336
  81.0 0.6 collective-permute-done.34
  81.6 1.0 %collective-permute-start.29 = (bf16[1,256,128]{2,1,0:T(8,128)(2,1)S(1)}, bf16[1,256,128]{2,1,0:T(8,128)(2,1)S(1)}, u32[]{:S(2)}, u32[]{:S(2)}) collective-permute-start(bf16[1,256,128]{2,1,0:T(8,128)(2,1)S(1)} %slice.114), channel_id=1, source_target_pairs={{0,16},{4,20},{8,24},{12,28},{16,0},{20,4},{24,8},{28,12},{1,17},{... | collective-permute-start | bytes 196616 | tf_op jit(solution)/shard_map/ppermute | solution.py:18
  82.8 0.7 convert.16
  84.1 1.9 %collective-permute-start.28 = (bf16[1,336,128]{2,1,0:T(8,128)(2,1)S(1)}, bf16[1,336,128]{2,1,0:T(8,128)(2,1)S(1)}, u32[]{:S(2)}, u32[]{:S(2)}) collective-permute-start(bf16[1,336,128]{2,1,0:T(8,128)(2,1)S(1)} %slice.111), channel_id=1, source_target_pairs={{0,16},{4,20},{8,24},{12,28},{16,0},{20,4},{24,8},{28,12},{1,17},{... | collective-permute-start | bytes 258056 | tf_op jit(solution)/shard_map/ppermute | solution.py:18
  86.0 1.4 %collective-permute-done.29 = bf16[1,256,128]{2,1,0:T(8,128)(2,1)S(1)} collective-permute-done((bf16[1,256,128]{2,1,0:T(8,128)(2,1)S(1)}, bf16[1,256,128]{2,1,0:T(8,128)(2,1)S(1)}, u32[]{:S(2)}, u32[]{:S(2)}) %collective-permute-start.29) | collective-permute-done | bytes 65568 | tf_op jit(solution)/shard_map/ppermute | solution.py:18
  87.4 0.7 join_grad.1
  88.1 1.2 %copy.33 = bf16[2,6,13,13,128]{4,0,3,2,1:T(2,128)(2,1)} copy(bf16[2,6,13,13,128]{4,3,2,1,0:T(8,128)(2,1)S(1)} %bitcast.53) | data formatting | bytes 1038336
  89.3 0.9 collective-permute-done.28
  90.7 0.7 convert.14
  (99 shorter events, 5.8 us)
Async XLA Ops:
  0.6 8.0 %copy-start = (s32[2,2]{1,0:T(2,128)S(1)}, s32[2,2]{1,0:T(2,128)}, u32[]{:S(2)}) copy-start(s32[2,2]{1,0:T(2,128)} %param.8) | copy-start | bytes 52
  2.0 7.5 %collective-permute-start = (bf16[3,208,128]{2,1,0:T(8,128)(2,1)S(1)}, bf16[3,208,128]{2,1,0:T(8,128)(2,1)S(1)}, u32[]{:S(2)}, u32[]{:S(2)}) collective-permute-start(bf16[3,208,128]{2,1,0:T(8,128)(2,1)S(1)} %constant_dynamic-slice_fusion.3), channel_id=1, source_target_pairs={{0,1},{1,0},{2,3},{3,2},{4,5},{5,4},{6,7},{7,6},{8,9},{9,8},{10,11... | collective-permute-start | bytes 479240 | tf_op jit(solution)/shard_map/ppermute | solution.py:18
  2.5 11.1 %collective-permute-start.1 = (bf16[2,3,208,128]{3,2,1,0:T(8,128)(2,1)S(1)}, bf16[2,3,208,128]{3,2,1,0:T(8,128)(2,1)S(1)}, u32[]{:S(2)}, u32[]{:S(2)}) collective-permute-start(bf16[2,3,208,128]{3,2,1,0:T(8,128)(2,1)S(1)} %bitcast.70), channel_id=1, source_target_pairs={{0,2},{1,3},{2,0},{3,1},{4,6},{5,7},{6,4},{7,5},{8,10},{9,11},{10,... | collective-permute-start | bytes 958472 | tf_op jit(solution)/shard_map/ppermute | solution.py:18
  5.1 12.3 %collective-permute-start.3 = (bf16[2,3,208,128]{3,2,1,0:T(8,128)(2,1)S(1)}, bf16[2,3,208,128]{3,2,1,0:T(8,128)(2,1)S(1)}, u32[]{:S(2)}, u32[]{:S(2)}) collective-permute-start(bf16[2,3,208,128]{3,2,1,0:T(8,128)(2,1)S(1)} %bitcast.48), channel_id=1, source_target_pairs={{0,4},{4,0},{8,12},{12,8},{16,20},{20,16},{24,28},{28,24},{1,5},{5... | collective-permute-start | bytes 958472 | tf_op jit(solution)/shard_map/ppermute | solution.py:18
  7.9 9.5 %copy-start.2 = (f32[512]{0:T(512)S(1)}, f32[512]{0:T(512)}, u32[]{:S(2)}) copy-start(f32[512]{0:T(512)} %param.10) | copy-start | bytes 6148
  8.0 12.7 %collective-permute-start.5 = (bf16[2,3,208,128]{3,2,1,0:T(8,128)(2,1)S(1)}, bf16[2,3,208,128]{3,2,1,0:T(8,128)(2,1)S(1)}, u32[]{:S(2)}, u32[]{:S(2)}) collective-permute-start(bf16[2,3,208,128]{3,2,1,0:T(8,128)(2,1)S(1)} %bitcast.69), channel_id=1, source_target_pairs={{0,2},{1,3},{2,0},{3,1},{4,6},{5,7},{6,4},{7,5},{8,10},{9,11},{10,... | collective-permute-start | bytes 958472 | tf_op jit(solution)/shard_map/ppermute | solution.py:18
  14.4 3.0 %collective-permute-start.2 = (bf16[3,208,128]{2,1,0:T(8,128)(2,1)S(1)}, bf16[3,208,128]{2,1,0:T(8,128)(2,1)S(1)}, u32[]{:S(2)}, u32[]{:S(2)}) collective-permute-start(bf16[3,208,128]{2,1,0:T(8,128)(2,1)S(1)} %pick.3), channel_id=1, source_target_pairs={{0,1},{1,0},{2,3},{3,2},{4,5},{5,4},{6,7},{7,6},{8,9},{9,8},{10,11... | collective-permute-start | bytes 479240 | tf_op jit(solution)/shard_map/ppermute | solution.py:18
  14.5 10.0 %collective-permute-start.7 = (bf16[2,3,208,128]{3,2,1,0:T(8,128)(2,1)S(1)}, bf16[2,3,208,128]{3,2,1,0:T(8,128)(2,1)S(1)}, u32[]{:S(2)}, u32[]{:S(2)}) collective-permute-start(bf16[2,3,208,128]{3,2,1,0:T(8,128)(2,1)S(1)} %after_part.1.refs_0_.refs_1_), channel_id=1, source_target_pairs={{0,4},{4,0},{8,12},{12,8},{16,20},{20,16},{24,28},{28,24},{1,5},{5... | collective-permute-start | bytes 958472 | tf_op jit(solution)/shard_map/ppermute | solution.py:18
  17.2 5.9 %collective-permute-start.4 = (bf16[3,208,128]{2,1,0:T(8,128)(2,1)S(1)}, bf16[3,208,128]{2,1,0:T(8,128)(2,1)S(1)}, u32[]{:S(2)}, u32[]{:S(2)}) collective-permute-start(bf16[3,208,128]{2,1,0:T(8,128)(2,1)S(1)} %pick.4), channel_id=1, source_target_pairs={{0,1},{1,0},{2,3},{3,2},{4,5},{5,4},{6,7},{7,6},{8,9},{9,8},{10,11... | collective-permute-start | bytes 479240 | tf_op jit(solution)/shard_map/ppermute | solution.py:18
  17.4 7.1 %copy-start.1 = (f32[512]{0:T(512)S(1)}, f32[512]{0:T(512)}, u32[]{:S(2)}) copy-start(f32[512]{0:T(512)} %param.12) | copy-start | bytes 6148
  21.4 1.6 %collective-permute-start.6 = (bf16[3,208,128]{2,1,0:T(8,128)(2,1)S(1)}, bf16[3,208,128]{2,1,0:T(8,128)(2,1)S(1)}, u32[]{:S(2)}, u32[]{:S(2)}) collective-permute-start(bf16[3,208,128]{2,1,0:T(8,128)(2,1)S(1)} %pick.5), channel_id=1, source_target_pairs={{0,1},{1,0},{2,3},{3,2},{4,5},{5,4},{6,7},{7,6},{8,9},{9,8},{10,11... | collective-permute-start | bytes 479240 | tf_op jit(solution)/shard_map/ppermute | solution.py:18
  21.8 24.1 %collective-permute-start.10 = (bf16[4,3,208,128]{3,2,1,0:T(8,128)(2,1)S(1)}, bf16[4,3,208,128]{3,2,1,0:T(8,128)(2,1)S(1)}, u32[]{:S(2)}, u32[]{:S(2)}) collective-permute-start(bf16[4,3,208,128]{3,2,1,0:T(8,128)(2,1)S(1)} %get-tuple-element.39.refs_0_), channel_id=1, source_target_pairs={{0,4},{4,0},{8,12},{12,8},{16,20},{20,16},{24,28},{28,24},{1,5},{5... | collective-permute-start | bytes 1916936 | tf_op jit(solution)/shard_map/ppermute | solution.py:18
  22.8 11.0 %collective-permute-start.8 = (bf16[2,3,208,128]{3,2,1,0:T(8,128)(2,1)S(1)}, bf16[2,3,208,128]{3,2,1,0:T(8,128)(2,1)S(1)}, u32[]{:S(2)}, u32[]{:S(2)}) collective-permute-start(bf16[2,3,208,128]{3,2,1,0:T(8,128)(2,1)S(1)} %slice.82), channel_id=1, source_target_pairs={{0,1},{1,0},{2,3},{3,2},{4,5},{5,4},{6,7},{7,6},{8,9},{9,8},{10,11... | collective-permute-start | bytes 958472 | tf_op jit(solution)/shard_map/ppermute | solution.py:18
  30.1 8.4 %collective-permute-start.12 = (bf16[3,208,256]{2,1,0:T(8,128)(2,1)S(1)}, bf16[3,208,256]{2,1,0:T(8,128)(2,1)S(1)}, u32[]{:S(2)}, u32[]{:S(2)}) collective-permute-start(bf16[3,208,256]{2,1,0:T(8,128)(2,1)S(1)} %get-tuple-element.49.refs_4_), channel_id=1, source_target_pairs={{0,1},{1,0},{2,3},{3,2},{4,5},{5,4},{6,7},{7,6},{8,9},{9,8},{10,11... | collective-permute-start | bytes 958472 | tf_op jit(solution)/shard_map/ppermute | solution.py:18
  30.2 13.3 %collective-permute-start.11 = (bf16[2,3,208,128]{3,2,1,0:T(8,128)(2,1)S(1)}, bf16[2,3,208,128]{3,2,1,0:T(8,128)(2,1)S(1)}, u32[]{:S(2)}, u32[]{:S(2)}) collective-permute-start(bf16[2,3,208,128]{3,2,1,0:T(8,128)(2,1)S(1)} %get-tuple-element.45), channel_id=1, source_target_pairs={{0,2},{1,3},{2,0},{3,1},{4,6},{5,7},{6,4},{7,5},{8,10},{9,11},{10,... | collective-permute-start | bytes 958472 | tf_op jit(solution)/shard_map/ppermute | solution.py:18
  32.1 13.8 %collective-permute-start.9 = (bf16[3,208,256]{2,1,0:T(8,128)(2,1)S(1)}, bf16[3,208,256]{2,1,0:T(8,128)(2,1)S(1)}, u32[]{:S(2)}, u32[]{:S(2)}) collective-permute-start(bf16[3,208,256]{2,1,0:T(8,128)(2,1)S(1)} %get-tuple-element.44), channel_id=1, source_target_pairs={{0,4},{4,0},{8,12},{12,8},{16,20},{20,16},{24,28},{28,24},{1,5},{5... | collective-permute-start | bytes 958472 | tf_op jit(solution)/shard_map/ppermute | solution.py:18
  38.4 8.1 %collective-permute-start.16 = (bf16[3,208,256]{2,1,0:T(8,128)(2,1)S(1)}, bf16[3,208,256]{2,1,0:T(8,128)(2,1)S(1)}, u32[]{:S(2)}, u32[]{:S(2)}) collective-permute-start(bf16[3,208,256]{2,1,0:T(8,128)(2,1)S(1)} %get-tuple-element.54.refs_4_), channel_id=1, source_target_pairs={{0,1},{1,0},{2,3},{3,2},{4,5},{5,4},{6,7},{7,6},{8,9},{9,8},{10,11... | collective-permute-start | bytes 958472 | tf_op jit(solution)/shard_map/ppermute | solution.py:18
  38.5 15.8 %collective-permute-start.17 = (bf16[3,208,256]{2,1,0:T(8,128)(2,1)S(1)}, bf16[3,208,256]{2,1,0:T(8,128)(2,1)S(1)}, u32[]{:S(2)}, u32[]{:S(2)}) collective-permute-start(bf16[3,208,256]{2,1,0:T(8,128)(2,1)S(1)} %get-tuple-element.56), channel_id=1, source_target_pairs={{0,4},{4,0},{8,12},{12,8},{16,20},{20,16},{24,28},{28,24},{1,5},{5... | collective-permute-start | bytes 958472 | tf_op jit(solution)/shard_map/ppermute | solution.py:18
  43.5 10.8 %collective-permute-start.18 = (bf16[2,3,208,128]{3,2,1,0:T(8,128)(2,1)S(1)}, bf16[2,3,208,128]{3,2,1,0:T(8,128)(2,1)S(1)}, u32[]{:S(2)}, u32[]{:S(2)}) collective-permute-start(bf16[2,3,208,128]{3,2,1,0:T(8,128)(2,1)S(1)} %get-tuple-element.58), channel_id=1, source_target_pairs={{0,2},{1,3},{2,0},{3,1},{4,6},{5,7},{6,4},{7,5},{8,10},{9,11},{10,... | collective-permute-start | bytes 958472 | tf_op jit(solution)/shard_map/ppermute | solution.py:18
  45.9 2.4 %collective-permute-start.13 = (bf16[2,3,208,128]{3,2,1,0:T(8,128)(2,1)S(1)}, bf16[2,3,208,128]{3,2,1,0:T(8,128)(2,1)S(1)}, u32[]{:S(2)}, u32[]{:S(2)}) collective-permute-start(bf16[2,3,208,128]{3,2,1,0:T(8,128)(2,1)S(1)} %slice.83), channel_id=1, source_target_pairs={{0,1},{1,0},{2,3},{3,2},{4,5},{5,4},{6,7},{7,6},{8,9},{9,8},{10,11... | collective-permute-start | bytes 958472 | tf_op jit(solution)/shard_map/ppermute | solution.py:18
  46.0 2.3 %collective-permute-start.14 = (bf16[3,208,256]{2,1,0:T(8,128)(2,1)S(1)}, bf16[3,208,256]{2,1,0:T(8,128)(2,1)S(1)}, u32[]{:S(2)}, u32[]{:S(2)}) collective-permute-start(bf16[3,208,256]{2,1,0:T(8,128)(2,1)S(1)} %get-tuple-element.52.refs_6_), channel_id=1, source_target_pairs={{0,1},{1,0},{2,3},{3,2},{4,5},{5,4},{6,7},{7,6},{8,9},{9,8},{10,11... | collective-permute-start | bytes 958472 | tf_op jit(solution)/shard_map/ppermute | solution.py:18
  46.5 1.8 %collective-permute-start.15 = (bf16[3,208,128]{2,1,0:T(8,128)(2,1)S(1)}, bf16[3,208,128]{2,1,0:T(8,128)(2,1)S(1)}, u32[]{:S(2)}, u32[]{:S(2)}) collective-permute-start(bf16[3,208,128]{2,1,0:T(8,128)(2,1)S(1)} %slice_bitcast_fusion.1), channel_id=1, source_target_pairs={{0,1},{1,0},{2,3},{3,2},{4,5},{5,4},{6,7},{7,6},{8,9},{9,8},{10,11... | collective-permute-start | bytes 479240 | tf_op jit(solution)/shard_map/ppermute | solution.py:18
  52.7 10.9 %collective-permute-start.20 = (bf16[4,320,128]{2,1,0:T(8,128)(2,1)S(1)}, bf16[4,320,128]{2,1,0:T(8,128)(2,1)S(1)}, u32[]{:S(2)}, u32[]{:S(2)}) collective-permute-start(bf16[4,320,128]{2,1,0:T(8,128)(2,1)S(1)} %get-tuple-element.60), channel_id=1, source_target_pairs={{0,8},{4,12},{8,0},{12,4},{16,24},{20,28},{24,16},{28,20},{1,9},{5... | collective-permute-start | bytes 983048 | tf_op jit(solution)/shard_map/ppermute | solution.py:18
  54.3 1.6 %collective-permute-start.19 = (bf16[3,208,256]{2,1,0:T(8,128)(2,1)S(1)}, bf16[3,208,256]{2,1,0:T(8,128)(2,1)S(1)}, u32[]{:S(2)}, u32[]{:S(2)}) collective-permute-start(bf16[3,208,256]{2,1,0:T(8,128)(2,1)S(1)} %after_grad5.1.refs_6_), channel_id=1, source_target_pairs={{0,1},{1,0},{2,3},{3,2},{4,5},{5,4},{6,7},{7,6},{8,9},{9,8},{10,11... | collective-permute-start | bytes 958472 | tf_op jit(solution)/shard_map/ppermute | solution.py:18
  54.3 9.2 %collective-permute-start.30 = (bf16[4,272,128]{2,1,0:T(8,128)(2,1)S(1)}, bf16[4,272,128]{2,1,0:T(8,128)(2,1)S(1)}, u32[]{:S(2)}, u32[]{:S(2)}) collective-permute-start(bf16[4,272,128]{2,1,0:T(8,128)(2,1)S(1)} %get-tuple-element.67), channel_id=1, source_target_pairs={{0,2},{1,3},{2,0},{3,1},{4,6},{5,7},{6,4},{7,5},{8,10},{9,11},{10,... | collective-permute-start | bytes 835592 | tf_op jit(solution)/shard_map/ppermute | solution.py:18
  60.2 15.0 %collective-permute-start.24 = (bf16[4,336,128]{2,1,0:T(8,128)(2,1)S(1)}, bf16[4,336,128]{2,1,0:T(8,128)(2,1)S(1)}, u32[]{:S(2)}, u32[]{:S(2)}) collective-permute-start(bf16[4,336,128]{2,1,0:T(8,128)(2,1)S(1)} %get-tuple-element.64), channel_id=1, source_target_pairs={{0,8},{4,12},{8,0},{12,4},{16,24},{20,28},{24,16},{28,20},{1,9},{5... | collective-permute-start | bytes 1032200 | tf_op jit(solution)/shard_map/ppermute | solution.py:18
  60.7 9.2 %collective-permute-start.22 = (bf16[4,256,128]{2,1,0:T(8,128)(2,1)S(1)}, bf16[4,256,128]{2,1,0:T(8,128)(2,1)S(1)}, u32[]{:S(2)}, u32[]{:S(2)}) collective-permute-start(bf16[4,256,128]{2,1,0:T(8,128)(2,1)S(1)} %get-tuple-element.62), channel_id=1, source_target_pairs={{0,2},{1,3},{2,0},{3,1},{4,6},{5,7},{6,4},{7,5},{8,10},{9,11},{10,... | collective-permute-start | bytes 786440 | tf_op jit(solution)/shard_map/ppermute | solution.py:18
  63.7 8.8 %collective-permute-start.33 = (bf16[2,320,128]{2,1,0:T(8,128)(2,1)S(1)}, bf16[2,320,128]{2,1,0:T(8,128)(2,1)S(1)}, u32[]{:S(2)}, u32[]{:S(2)}) collective-permute-start(bf16[2,320,128]{2,1,0:T(8,128)(2,1)S(1)} %get-tuple-element.84), channel_id=1, source_target_pairs={{0,2},{1,3},{2,0},{3,1},{4,6},{5,7},{6,4},{7,5},{8,10},{9,11},{10,... | collective-permute-start | bytes 491528 | tf_op jit(solution)/shard_map/ppermute | solution.py:18
  65.3 10.1 %collective-permute-start.31 = (bf16[2,272,128]{2,1,0:T(8,128)(2,1)S(1)}, bf16[2,272,128]{2,1,0:T(8,128)(2,1)S(1)}, u32[]{:S(2)}, u32[]{:S(2)}) collective-permute-start(bf16[2,272,128]{2,1,0:T(8,128)(2,1)S(1)} %get-tuple-element.86), channel_id=1, source_target_pairs={{0,8},{4,12},{8,0},{12,4},{16,24},{20,28},{24,16},{28,20},{1,9},{5... | collective-permute-start | bytes 417800 | tf_op jit(solution)/shard_map/ppermute | solution.py:18
  66.3 12.2 %collective-permute-start.21 = (bf16[3,208,128]{2,1,0:T(8,128)(2,1)S(1)}, bf16[3,208,128]{2,1,0:T(8,128)(2,1)S(1)}, u32[]{:S(2)}, u32[]{:S(2)}) collective-permute-start(bf16[3,208,128]{2,1,0:T(8,128)(2,1)S(1)} %after_step.6), channel_id=1, source_target_pairs={{0,1},{1,0},{2,3},{3,2},{4,5},{5,4},{6,7},{7,6},{8,9},{9,8},{10,11... | collective-permute-start | bytes 479240 | tf_op jit(solution)/shard_map/ppermute | solution.py:18
  70.0 8.4 %collective-permute-start.23 = (bf16[2,256,128]{2,1,0:T(8,128)(2,1)S(1)}, bf16[2,256,128]{2,1,0:T(8,128)(2,1)S(1)}, u32[]{:S(2)}, u32[]{:S(2)}) collective-permute-start(bf16[2,256,128]{2,1,0:T(8,128)(2,1)S(1)} %slice.107), channel_id=1, source_target_pairs={{0,8},{4,12},{8,0},{12,4},{16,24},{20,28},{24,16},{28,20},{1,9},{5... | collective-permute-start | bytes 393224 | tf_op jit(solution)/shard_map/ppermute | solution.py:18
  72.6 9.0 %collective-permute-start.34 = (bf16[1,320,128]{2,1,0:T(8,128)(2,1)S(1)}, bf16[1,320,128]{2,1,0:T(8,128)(2,1)S(1)}, u32[]{:S(2)}, u32[]{:S(2)}) collective-permute-start(bf16[1,320,128]{2,1,0:T(8,128)(2,1)S(1)} %get-tuple-element.88), channel_id=1, source_target_pairs={{0,16},{4,20},{8,24},{12,28},{16,0},{20,4},{24,8},{28,12},{1,17},{... | collective-permute-start | bytes 245768 | tf_op jit(solution)/shard_map/ppermute | solution.py:18
  75.4 7.3 %collective-permute-start.32 = (bf16[1,272,128]{2,1,0:T(8,128)(2,1)S(1)}, bf16[1,272,128]{2,1,0:T(8,128)(2,1)S(1)}, u32[]{:S(2)}, u32[]{:S(2)}) collective-permute-start(bf16[1,272,128]{2,1,0:T(8,128)(2,1)S(1)} %get-tuple-element.90), channel_id=1, source_target_pairs={{0,16},{4,20},{8,24},{12,28},{16,0},{20,4},{24,8},{28,12},{1,17},{... | collective-permute-start | bytes 208904 | tf_op jit(solution)/shard_map/ppermute | solution.py:18
  76.9 7.1 %collective-permute-start.27 = (bf16[2,336,128]{2,1,0:T(8,128)(2,1)S(1)}, bf16[2,336,128]{2,1,0:T(8,128)(2,1)S(1)}, u32[]{:S(2)}, u32[]{:S(2)}) collective-permute-start(bf16[2,336,128]{2,1,0:T(8,128)(2,1)S(1)} %slice.109), channel_id=1, source_target_pairs={{0,2},{1,3},{2,0},{3,1},{4,6},{5,7},{6,4},{7,5},{8,10},{9,11},{10,... | collective-permute-start | bytes 516104 | tf_op jit(solution)/shard_map/ppermute | solution.py:18
  78.4 8.9 %collective-permute-start.26 = (bf16[3,208,128]{2,1,0:T(8,128)(2,1)S(1)}, bf16[3,208,128]{2,1,0:T(8,128)(2,1)S(1)}, u32[]{:S(2)}, u32[]{:S(2)}) collective-permute-start(bf16[3,208,128]{2,1,0:T(8,128)(2,1)S(1)} %slice_bitcast_fusion), channel_id=1, source_target_pairs={{0,1},{1,0},{2,3},{3,2},{4,5},{5,4},{6,7},{7,6},{8,9},{9,8},{10,11... | collective-permute-start | bytes 479240 | tf_op jit(solution)/shard_map/ppermute | solution.py:18
  78.6 8.8 %collective-permute-start.25 = (bf16[3,208,128]{2,1,0:T(8,128)(2,1)S(1)}, bf16[3,208,128]{2,1,0:T(8,128)(2,1)S(1)}, u32[]{:S(2)}, u32[]{:S(2)}) collective-permute-start(bf16[3,208,128]{2,1,0:T(8,128)(2,1)S(1)} %get-tuple-element.65), channel_id=1, source_target_pairs={{0,1},{1,0},{2,3},{3,2},{4,5},{5,4},{6,7},{7,6},{8,9},{9,8},{10,11... | collective-permute-start | bytes 479240 | tf_op jit(solution)/shard_map/ppermute | solution.py:18
  81.6 5.8 %collective-permute-start.29 = (bf16[1,256,128]{2,1,0:T(8,128)(2,1)S(1)}, bf16[1,256,128]{2,1,0:T(8,128)(2,1)S(1)}, u32[]{:S(2)}, u32[]{:S(2)}) collective-permute-start(bf16[1,256,128]{2,1,0:T(8,128)(2,1)S(1)} %slice.114), channel_id=1, source_target_pairs={{0,16},{4,20},{8,24},{12,28},{16,0},{20,4},{24,8},{28,12},{1,17},{... | collective-permute-start | bytes 196616 | tf_op jit(solution)/shard_map/ppermute | solution.py:18
  84.1 6.1 %collective-permute-start.28 = (bf16[1,336,128]{2,1,0:T(8,128)(2,1)S(1)}, bf16[1,336,128]{2,1,0:T(8,128)(2,1)S(1)}, u32[]{:S(2)}, u32[]{:S(2)}) collective-permute-start(bf16[1,336,128]{2,1,0:T(8,128)(2,1)S(1)} %slice.111), channel_id=1, source_target_pairs={{0,16},{4,20},{8,24},{12,28},{16,0},{20,4},{24,8},{28,12},{1,17},{... | collective-permute-start | bytes 258056 | tf_op jit(solution)/shard_map/ppermute | solution.py:18

commit v2 on v1

--- a/solution.py
+++ b/solution.py
@@ -117,6 +117,20 @@
     left, right = value[:, :share], value[:, share:]
     odd = (info[0] % 2) == 1
     return jnp.where(odd, right, left), jnp.where(odd, left, right)
+
+
+def put_pairs(info, half, value, kept, sent):
+    size = value.shape[1] // 4
+    left, right = value[:, : 2 * size], value[:, 2 * size :]
+    place = info[1]
+    second = ((place // 2) % 2) == 1
+    odd = (place % 2) == 1
+    own, other = jnp.where(second, right, left), jnp.where(second, left, right)
+    at = pl.ds(pl.multiple_of((half ^ (place // 4)) * 2 * size, 2 * size), 2 * size)
+    shape = kept.shape[:2] + (2 * size,)
+    for one, out in ((own, kept), (other, sent)):
+        ordered = jnp.where(odd, pltpu.roll(one, size, 1), one)
+        out[:, :, at] = ordered.astype(BF16).reshape(shape)
 
 
 def put_halves(info, half, value, kept, sent):
@@ -202,7 +216,7 @@
     o0, o1, o23, slope, kept, sent, shifted, upstream = refs
     clips, cells, share = c1.shape
     fill_from_quarters(info, shifted, (hidden.at[0], hidden.at[2], hidden.at[1], hidden.at[3]))
-    for k, quarter in enumerate((c0.at[info[0] % 2], c1, c2.at[info[0] % 2], c3)):
+    for k, quarter in enumerate((c0, c1, c2.at[0], c3.at[0])):
         at = pl.multiple_of((info[0] ^ k) * share, share)
         upstream[:, pl.ds(at, share)] = quarter[...].reshape(clips * cells, share)
     valid = valid_of(info, clips, cells, side)
@@ -247,7 +261,7 @@
         back = backward_dot(shifted, weight, lanes).astype(BF16).astype(F32)
         down = back * factor[half]
         slope[:, :, lanes] = down.astype(BF16).reshape(slope.shape[:2] + (width,))
-        put_halves(info, half, down, kept, sent)
+        put_pairs(info, half, down, kept, sent)
 
     copy.wait()
 
@@ -297,7 +311,7 @@
 
     def place_of(chunk, u, x_bit):
         order = chunks[chunk][0]
-        bits = {"x": x_bit, "a": u & 1, "b": u >> 1}
+        bits = {"x": x_bit, "y": u & 1, "a": u & 1, "b": u >> 1}
         return outs[2 * chunk + bits[order[0]]], 2 * bits[order[1]] + bits[order[2]]
 
     for i in range(3):
@@ -353,7 +367,7 @@
     def over_b(value):
         return swap(value, "dp", n_dp, 4 * fine)
 
-    steps = {"x": over_x, "a": over_a, "b": over_b}
+    steps = {"x": over_x, "y": over_y, "a": over_a, "b": over_b}
 
     live_count = jnp.sum(clip_counts, axis=1)
     slot = place * group + jnp.arange(group, dtype=jnp.int32)
@@ -377,8 +391,8 @@
     q1 = over_core(clips_of(flat, place ^ 1, 1))
 
     flat = wide(cotangent)
-    cot_near = clips_of(flat, place - core, 2).reshape(pair_dims)
-    cot_far = over_x(clips_of(flat, (place - core) ^ 2, 2).reshape(pair_dims))
+    cot_own, cot_other = clips_of(flat, place, 1), clips_of(flat, place ^ 1, 1)
+    cot_far = over_x(jnp.stack([clips_of(flat, place ^ 2, 1), clips_of(flat, place ^ 3, 1)]))
 
 
     weight_t = jax.ShapeDtypeStruct((9, channels, channels), BF16)
@@ -535,13 +549,13 @@
             pltpu.VMEM((9, half, channels), BF16),
             pltpu.SemaphoreType.DMA((2,)),
         ],
+        [cot_own, cot_other],
         flops=work * 0 // 8,
     )(near, q1, weight4)
     (far,) = held("after_part", [far], [partial4])
     q3 = over_core(picked(far))
-    cot1 = over_core(picked(cot_near))
-    near_y = over_y(near)
-    far_y = over_y(far)
+    near_a = over_a(near)
+    far_a = over_a(far)
 
     hidden, factor4, near5 = call(
         functools.partial(conv4_kernel, side),
@@ -551,12 +565,12 @@
         [vmem] * 3,
         [four_t, factor_t, weight_t],
         [shifted_of(half), pltpu.SemaphoreType.DMA],
-        [near_y],
+        [near_a],
         flops=work * 0 // 8,
     )(partial4, far, q3, bias4, rest4, weight5)
     hidden_y = over_y(hidden)
     (cot_far,) = held("after_conv4", [cot_far], [factor4])
-    cots = [cot_near, cot1, cot_far, over_core(picked(cot_far))]
+    cots = [cot_own, over_core(cot_other), cot_far, over_core(cot_far[1:])]
 
     *outs, slope5, kept5, sent5 = call(
         functools.partial(conv5_kernel, side),
@@ -566,7 +580,7 @@
         [vmem] * 6,
         [quarter_t, quarter_t, pair_t, whole_t, half_t, half_t],
         [shifted_of(channels), pltpu.VMEM((group * cells, channels), BF16)],
-        [far_y],
+        [far_a],
         flops=work * 0 // 8,
     )(hidden, *cots, bias5, near5)
     out_far = over_x(outs[2])
@@ -586,7 +600,7 @@
         [hidden_core],
         flops=work * 0 // 8,
     )(slope5, factor4, near5, weight4)
-    kept4_core, across4 = over_core(kept4), over_y(sent4)
+    kept4_core, across4 = over_core(kept4), over_a(sent4)
 
     backs = call(
         back4_kernel,
@@ -608,7 +622,7 @@
 
     chunks5 = (("xab", 0, 4), ("axb", 4, 5))
     own, other = 0, 1
-    chunks4 = (("axb", 0, 5), ("xab", 5, 4))
+    chunks4 = (("xyb", 0, 4), ("yxb", 4, 5))
     blocks5 = kernel_grad(
         "grad5",
         chunks5,
@@ -625,7 +639,7 @@
         chunks4,
         (((0, own), (0, other), (2, own), (2, other)), ((1, own), (1, other), (3, own), (3, other))),
         True,
-        (near, far, near_y, far_y),
+        (near, far, near_a, far_a),
         (kept4, kept4_core, across4, across4_core),
         [blocks5[0]],
     )

time: 91.7 us -> 92.9 us (1.013)
  waiting for transfers between devices: 13.8 us -> 20.6 us
  starting transfers between devices: 32.9 us -> 28.8 us
  Pallas kernels: 34.4 us -> 32.9 us
    ppermute x35, waiting for transfers between devices: 13.8 us -> 20.6 us  [swap(): return lax.ppermute(value, axis_name, [(i, i ^ bit) for i in range(size)])]
    ppermute x35, starting transfers between devices: 32.9 us -> 28.8 us  [swap(): return lax.ppermute(value, axis_name, [(i, i ^ bit) for i in range(size)])]
    pallas_call x12 -> x10, Pallas kernels: 34.4 us -> 32.9 us  [call(): return lambda *args: called(info, *args, *after)]
  transfers between devices with their start and end apart: 35 -> 35, of which waited for: 11 -> 12; matrix products, arithmetic and copies ran while one was open for 7% -> 8% of each run, Pallas kernels for 38% -> 35%
where the time goes in v2:
time: 92.9 us; the launch traced here: 92.7 us
  Pallas kernels  32.9 us (35%)
  starting transfers between devices  28.8 us (31%)
  waiting for transfers between devices  20.6 us (22%)
  local copies, waits for them, and re-layouts  5.89 us (6%)
  other arithmetic  3.35 us (4%)
  between operations  1.16 us (1%)
    pallas_call x10, Pallas kernels, call(): return lambda *args: called(info, *args, *after)  32.9 us
    ppermute x35, starting transfers between devices, swap(): return lax.ppermute(value, axis_name, [(i, i ^ bit) for i in range(size)])  28.8 us
    ppermute x35, waiting for transfers between devices, swap(): return lax.ppermute(value, axis_name, [(i, i ^ bit) for i in range(size)])  20.6 us
    unnamed x10, local copies, waits for them, and re-layouts  4.69 us
  transfers between devices with their start and end apart: 35, of which 12 were waited for; matrix products, arithmetic and copies ran while one was open for 8% of the time, Pallas kernels for 35%

profile of v2, /device:TPU:0, one launch (start us, length us, event | category | flops | bytes accessed | tf_op | source)
XLA Modules:
  0.0 92.7 jit_solution(351329039874295315)
XLA Ops:
  0.7 1.1 %copy.30 = bf16[2,6,13,13,128]{4,3,2,1,0:T(8,128)(2,1)S(1)} copy(bf16[2,6,13,13,128]{4,0,3,2,1:T(2,128)(2,1)} %param.7) | data formatting | bytes 1038336 | tf_op args[0]
  2.0 0.5 collective-permute-start
  2.5 2.6 %collective-permute-start.1 = (bf16[2,3,208,128]{3,2,1,0:T(8,128)(2,1)S(1)}, bf16[2,3,208,128]{3,2,1,0:T(8,128)(2,1)S(1)}, u32[]{:S(2)}, u32[]{:S(2)}) collective-permute-start(bf16[2,3,208,128]{3,2,1,0:T(8,128)(2,1)S(1)} %bitcast.69), channel_id=1, source_target_pairs={{0,2},{1,3},{2,0},{3,1},{4,6},{5,7},{6,4},{7,5},{8,10},{9,11},{10,... | collective-permute-start | bytes 958472 | tf_op jit(solution)/shard_map/ppermute | solution.py:18
  5.1 1.6 %collective-permute-start.3 = (bf16[2,3,208,128]{3,2,1,0:T(8,128)(2,1)S(1)}, bf16[2,3,208,128]{3,2,1,0:T(8,128)(2,1)S(1)}, u32[]{:S(2)}, u32[]{:S(2)}) collective-permute-start(bf16[2,3,208,128]{3,2,1,0:T(8,128)(2,1)S(1)} %bitcast.50), channel_id=1, source_target_pairs={{0,8},{4,12},{8,0},{12,4},{16,24},{20,28},{24,16},{28,20},{1,9},{5... | collective-permute-start | bytes 958472 | tf_op jit(solution)/shard_map/ppermute | solution.py:18
  6.7 1.1 %copy.31 = bf16[2,6,13,13,128]{4,3,2,1,0:T(8,128)(2,1)S(1)} copy(bf16[2,6,13,13,128]{4,0,3,2,1:T(2,128)(2,1)} %param.13) | data formatting | bytes 1038336 | tf_op args[6]
  8.1 0.6 collective-permute-start.5
  8.8 0.6 gather_fusion
  9.6 4.2 %conv4_part.1 = (f32[2,624,256]{2,1,0:T(8,128)S(1)}, bf16[9,256,512]{2,1,0:T(8,128)(2,1)S(1)}) custom-call(s32[5]{0:T(128)S(1)} %pad_add_fusion.info, bf16[2,3,208,128]{3,2,1,0:T(8,128)(2,1)S(1)} %bitcast.51, bf16[3,208,128]{2,1,0:T(8,128)(2,1)S(1)} %collective-permute-done.refs_1_, bf16[9,512,512]{2,1,0:T(8,128)(2,1)} %bitcast.57, ...), custom_call_target="tpu_custom_call" | custom-call | tf_op jit(solution)/shard_map/conv4_part/pallas_call | solution.py:446
  13.8 0.8 pick.1
  14.6 1.8 %collective-permute-start.7 = (bf16[2,3,208,128]{3,2,1,0:T(8,128)(2,1)S(1)}, bf16[2,3,208,128]{3,2,1,0:T(8,128)(2,1)S(1)}, u32[]{:S(2)}, u32[]{:S(2)}) collective-permute-start(bf16[2,3,208,128]{3,2,1,0:T(8,128)(2,1)S(1)} %after_part.1.refs_0_.refs_1_), channel_id=1, source_target_pairs={{0,8},{4,12},{8,0},{12,4},{16,24},{20,28},{24,16},{28,20},{1,9},{5... | collective-permute-start | bytes 958472 | tf_op jit(solution)/shard_map/ppermute | solution.py:18
  16.6 3.2 %conv4.1 = (bf16[4,3,208,128]{3,2,1,0:T(8,128)(2,1)S(1)}, f32[2,624,256]{2,1,0:T(8,128)S(1)}, bf16[9,512,512]{2,1,0:T(8,128)(2,1)S(1)}) custom-call(s32[5]{0:T(128)S(1)} %pad_add_fusion.info, f32[2,624,256]{2,1,0:T(8,128)S(1)} %get-tuple-element.37.refs_1_.refs_0_, bf16[2,3,208,128]{3,2,1,0:T(8,128)(2,1)S(1)} %after_part.1.refs_0_.refs_1_, ...), custom_call_target="tpu_custom_call" | custom-call | tf_op jit(solution)/shard_map/conv4/pallas_call | solution.py:446
  20.3 1.8 %collective-permute-start.10 = (bf16[4,3,208,128]{3,2,1,0:T(8,128)(2,1)S(1)}, bf16[4,3,208,128]{3,2,1,0:T(8,128)(2,1)S(1)}, u32[]{:S(2)}, u32[]{:S(2)}) collective-permute-start(bf16[4,3,208,128]{3,2,1,0:T(8,128)(2,1)S(1)} %get-tuple-element.39.refs_0_), channel_id=1, source_target_pairs={{0,4},{4,0},{8,12},{12,8},{16,20},{20,16},{24,28},{28,24},{1,5},{5... | collective-permute-start | bytes 1916936 | tf_op jit(solution)/shard_map/ppermute | solution.py:18
  22.3 2.3 %collective-permute-done.7.refs_7_.refs_3_ = bf16[2,3,208,128]{3,2,1,0:T(8,128)(2,1)S(1)} collective-permute-done((bf16[2,3,208,128]{3,2,1,0:T(8,128)(2,1)S(1)}, bf16[2,3,208,128]{3,2,1,0:T(8,128)(2,1)S(1)}, u32[]{:S(2)}, u32[]{:S(2)}) %collective-permute-start.7) | collective-permute-done | bytes 319520 | tf_op jit(solution)/shard_map/ppermute | solution.py:18
  24.6 5.6 %conv5.1 = (bf16[3,208,128]{2,1,0:T(8,128)(2,1)S(1)}, bf16[3,208,128]{2,1,0:T(8,128)(2,1)S(1)}, bf16[2,3,208,128]{3,2,1,0:T(8,128)(2,1)S(1)}, bf16[3,208,512]{2,...) custom-call(s32[5]{0:T(128)S(1)} %pad_add_fusion.info, ...), custom_call_target="tpu_custom_call" | custom-call | tf_op jit(solution)/shard_map/conv5/pallas_call | solution.py:446
  30.3 1.7 %collective-permute-start.11 = (bf16[2,3,208,128]{3,2,1,0:T(8,128)(2,1)S(1)}, bf16[2,3,208,128]{3,2,1,0:T(8,128)(2,1)S(1)}, u32[]{:S(2)}, u32[]{:S(2)}) collective-permute-start(bf16[2,3,208,128]{3,2,1,0:T(8,128)(2,1)S(1)} %get-tuple-element.45), channel_id=1, source_target_pairs={{0,2},{1,3},{2,0},{3,1},{4,6},{5,7},{6,4},{7,5},{8,10},{9,11},{10,... | collective-permute-start | bytes 958472 | tf_op jit(solution)/shard_map/ppermute | solution.py:18
  32.0 1.5 %collective-permute-start.9 = (bf16[3,208,256]{2,1,0:T(8,128)(2,1)S(1)}, bf16[3,208,256]{2,1,0:T(8,128)(2,1)S(1)}, u32[]{:S(2)}, u32[]{:S(2)}) collective-permute-start(bf16[3,208,256]{2,1,0:T(8,128)(2,1)S(1)} %get-tuple-element.44), channel_id=1, source_target_pairs={{0,4},{4,0},{8,12},{12,8},{16,20},{20,16},{24,28},{28,24},{1,5},{5... | collective-permute-start | bytes 958472 | tf_op jit(solution)/shard_map/ppermute | solution.py:18
  33.5 4.5 %back5.1 = (bf16[3,208,512]{2,1,0:T(8,128)(2,1)S(1)}, bf16[3,208,256]{2,1,0:T(8,128)(2,1)S(1)}, bf16[3,208,256]{2,1,0:T(8,128)(2,1)S(1)}, bf16[9,512,512]{2,1,0:T(8,128)(2,1)S(1)}) custom-call(s32[5]{0:T(128)S(1)} %pad_add_fusion.info, bf16[3,208,512]{2,1,0:T(8,128)(2,1)S(1)} %get-tuple-element.46.refs_0_, f32[2,624,256]{2,1,0:T(8,128)S(1)} %get-tuple-element.40.refs_1_, ...), custom_call_target="tpu_custom_call" | custom-call | tf_op jit(solution)/shard_map/back5/pallas_call | solution.py:446
  38.1 1.6 %collective-permute-start.17 = (bf16[3,208,256]{2,1,0:T(8,128)(2,1)S(1)}, bf16[3,208,256]{2,1,0:T(8,128)(2,1)S(1)}, u32[]{:S(2)}, u32[]{:S(2)}) collective-permute-start(bf16[3,208,256]{2,1,0:T(8,128)(2,1)S(1)} %get-tuple-element.56), channel_id=1, source_target_pairs={{0,8},{4,12},{8,0},{12,4},{16,24},{20,28},{24,16},{28,20},{1,9},{5... | collective-permute-start | bytes 958472 | tf_op jit(solution)/shard_map/ppermute | solution.py:18
  39.8 4.6 %back4.1 = (bf16[3,208,128]{2,1,0:T(8,128)(2,1)S(1)}, bf16[3,208,128]{2,1,0:T(8,128)(2,1)S(1)}, bf16[2,3,208,128]{3,2,1,0:T(8,128)(2,1)S(1)}) custom-call(s32[5]{0:T(128)S(1)} %pad_add_fusion.info, bf16[3,208,512]{2,1,0:T(8,128)(2,1)S(1)} %get-tuple-element.47.refs_0_, bf16[9,512,512]{2,1,0:T(8,128)(2,1)S(1)} %get-tuple-element.48.refs_1_, ...), custom_call_target="tpu_custom_call" | custom-call | flops 2944401408 | tf_op jit(solution)/shard_map/back4/pallas_call | solution.py:446
  44.4 0.6 collective-permute-start.18
  45.8 1.6 %collective-permute-done.15.refs_8_.refs_3_ = bf16[3,208,128]{2,1,0:T(8,128)(2,1)S(1)} collective-permute-done((bf16[3,208,128]{2,1,0:T(8,128)(2,1)S(1)}, bf16[3,208,128]{2,1,0:T(8,128)(2,1)S(1)}, u32[]{:S(2)}, u32[]{:S(2)}) %collective-permute-start.15) | collective-permute-done | bytes 159776 | tf_op jit(solution)/shard_map/ppermute | solution.py:18
  47.4 4.3 %grad5.1 = (bf16[4,272,128]{2,1,0:T(8,128)(2,1)S(1)}, bf16[4,272,128]{2,1,0:T(8,128)(2,1)S(1)}, bf16[4,320,128]{2,1,0:T(8,128)(2,1)S(1)}, bf16[4,320,128]{2,1,0:T(8,128)(2,1)S(1)}) custom-call(s32[5]{0:T(128)S(1)} %pad_add_fusion.info, bf16[4,3,208,128]{3,2,1,0:T(8,128)(2,1)S(1)} %get-tuple-element.39.refs_0_, ...), custom_call_target="tpu_custom_call" | custom-call | tf_op jit(solution)/shard_map/grad5/pallas_call | solution.py:446
  51.8 2.3 %collective-permute-done.18.refs_2_.refs_1_ = bf16[2,3,208,128]{3,2,1,0:T(8,128)(2,1)S(1)} collective-permute-done((bf16[2,3,208,128]{3,2,1,0:T(8,128)(2,1)S(1)}, bf16[2,3,208,128]{3,2,1,0:T(8,128)(2,1)S(1)}, u32[]{:S(2)}, u32[]{:S(2)}) %collective-permute-start.18) | collective-permute-done | bytes 319520 | tf_op jit(solution)/shard_map/ppermute | solution.py:18
  54.1 0.5 collective-permute-start.30
  55.1 0.6 collective-permute-done.19.refs_7_
  55.7 4.3 %grad4.1 = (bf16[4,272,128]{2,1,0:T(8,128)(2,1)S(1)}, bf16[4,272,128]{2,1,0:T(8,128)(2,1)S(1)}, bf16[4,320,128]{2,1,0:T(8,128)(2,1)S(1)}, bf16[4,320,128]{2,1,0:T(8,128)(2,1)S(1)}) custom-call(s32[5]{0:T(128)S(1)} %pad_add_fusion.info, bf16[2,3,208,128]{3,2,1,0:T(8,128)(2,1)S(1)} %bitcast.52, bf16[2,3,208,128]{3,2,1,0:T(8,128)(2,1)S(1)} %after_part.1.refs_0_.refs_1_, ...), custom_call_target="tpu_custom_call" | custom-call | tf_op jit(solution)/shard_map/grad4/pallas_call | solution.py:446
  60.0 0.9 %collective-permute-start.24 = (bf16[4,272,128]{2,1,0:T(8,128)(2,1)S(1)}, bf16[4,272,128]{2,1,0:T(8,128)(2,1)S(1)}, u32[]{:S(2)}, u32[]{:S(2)}) collective-permute-start(bf16[4,272,128]{2,1,0:T(8,128)(2,1)S(1)} %get-tuple-element.64), channel_id=1, source_target_pairs={{0,2},{1,3},{2,0},{3,1},{4,6},{5,7},{6,4},{7,5},{8,10},{9,11},{10,... | collective-permute-start | bytes 835592 | tf_op jit(solution)/shard_map/ppermute | solution.py:18
  61.0 2.5 %collective-permute-done.30 = bf16[4,272,128]{2,1,0:T(8,128)(2,1)S(1)} collective-permute-done((bf16[4,272,128]{2,1,0:T(8,128)(2,1)S(1)}, bf16[4,272,128]{2,1,0:T(8,128)(2,1)S(1)}, u32[]{:S(2)}, u32[]{:S(2)}) %collective-permute-start.30) | collective-permute-done | bytes 278560 | tf_op jit(solution)/shard_map/ppermute | solution.py:18
  64.6 1.5 %collective-permute-start.33 = (bf16[2,320,128]{2,1,0:T(8,128)(2,1)S(1)}, bf16[2,320,128]{2,1,0:T(8,128)(2,1)S(1)}, u32[]{:S(2)}, u32[]{:S(2)}) collective-permute-start(bf16[2,320,128]{2,1,0:T(8,128)(2,1)S(1)} %get-tuple-element.86), channel_id=1, source_target_pairs={{0,2},{1,3},{2,0},{3,1},{4,6},{5,7},{6,4},{7,5},{8,10},{9,11},{10,... | collective-permute-start | bytes 491528 | tf_op jit(solution)/shard_map/ppermute | solution.py:18
  66.2 3.4 %collective-permute-done.24 = bf16[4,272,128]{2,1,0:T(8,128)(2,1)S(1)} collective-permute-done((bf16[4,272,128]{2,1,0:T(8,128)(2,1)S(1)}, bf16[4,272,128]{2,1,0:T(8,128)(2,1)S(1)}, u32[]{:S(2)}, u32[]{:S(2)}) %collective-permute-start.24) | collective-permute-done | bytes 278560 | tf_op jit(solution)/shard_map/ppermute | solution.py:18
  69.8 2.7 %collective-permute-start.32 = (bf16[1,272,128]{2,1,0:T(8,128)(2,1)S(1)}, bf16[1,272,128]{2,1,0:T(8,128)(2,1)S(1)}, u32[]{:S(2)}, u32[]{:S(2)}) collective-permute-start(bf16[1,272,128]{2,1,0:T(8,128)(2,1)S(1)} %get-tuple-element.92), channel_id=1, source_target_pairs={{0,16},{4,20},{8,24},{12,28},{16,0},{20,4},{24,8},{28,12},{1,17},{... | collective-permute-start | bytes 208904 | tf_op jit(solution)/shard_map/ppermute | solution.py:18
  72.5 0.5 collective-permute-start.27
  73.2 0.6 collective-permute-start.25
  73.8 3.7 %collective-permute-done.27 = bf16[2,272,128]{2,1,0:T(8,128)(2,1)S(1)} collective-permute-done((bf16[2,272,128]{2,1,0:T(8,128)(2,1)S(1)}, bf16[2,272,128]{2,1,0:T(8,128)(2,1)S(1)}, u32[]{:S(2)}, u32[]{:S(2)}) %collective-permute-start.27) | collective-permute-done | bytes 139296 | tf_op jit(solution)/shard_map/ppermute | solution.py:18
  77.5 1.0 %collective-permute-start.28 = (bf16[1,272,128]{2,1,0:T(8,128)(2,1)S(1)}, bf16[1,272,128]{2,1,0:T(8,128)(2,1)S(1)}, u32[]{:S(2)}, u32[]{:S(2)}) collective-permute-start(bf16[1,272,128]{2,1,0:T(8,128)(2,1)S(1)} %slice.116), channel_id=1, source_target_pairs={{0,16},{4,20},{8,24},{12,28},{16,0},{20,4},{24,8},{28,12},{1,17},{... | collective-permute-start | bytes 208904 | tf_op jit(solution)/shard_map/ppermute | solution.py:18
  78.6 0.6 collective-permute-start.23
  79.2 2.4 %collective-permute-start.34 = (bf16[1,320,128]{2,1,0:T(8,128)(2,1)S(1)}, bf16[1,320,128]{2,1,0:T(8,128)(2,1)S(1)}, u32[]{:S(2)}, u32[]{:S(2)}) collective-permute-start(bf16[1,320,128]{2,1,0:T(8,128)(2,1)S(1)} %get-tuple-element.90), channel_id=1, source_target_pairs={{0,16},{4,20},{8,24},{12,28},{16,0},{20,4},{24,8},{28,12},{1,17},{... | collective-permute-start | bytes 245768 | tf_op jit(solution)/shard_map/ppermute | solution.py:18
  81.5 0.7 join_grad.1
  82.2 1.2 %copy.33 = bf16[2,6,13,13,128]{4,0,3,2,1:T(2,128)(2,1)} copy(bf16[2,6,13,13,128]{4,3,2,1,0:T(8,128)(2,1)S(1)} %bitcast.54) | data formatting | bytes 1038336
  83.4 1.1 %collective-permute-done.28 = bf16[1,272,128]{2,1,0:T(8,128)(2,1)S(1)} collective-permute-done((bf16[1,272,128]{2,1,0:T(8,128)(2,1)S(1)}, bf16[1,272,128]{2,1,0:T(8,128)(2,1)S(1)}, u32[]{:S(2)}, u32[]{:S(2)}) %collective-permute-start.28) | collective-permute-done | bytes 69664 | tf_op jit(solution)/shard_map/ppermute | solution.py:18
  84.6 0.5 fusion.2
  85.2 0.5 fusion.1
  85.7 0.9 %collective-permute-start.29 = (bf16[1,320,128]{2,1,0:T(8,128)(2,1)S(1)}, bf16[1,320,128]{2,1,0:T(8,128)(2,1)S(1)}, u32[]{:S(2)}, u32[]{:S(2)}) collective-permute-start(bf16[1,320,128]{2,1,0:T(8,128)(2,1)S(1)} %slice.119), channel_id=1, source_target_pairs={{0,16},{4,20},{8,24},{12,28},{16,0},{20,4},{24,8},{28,12},{1,17},{... | collective-permute-start | bytes 245768 | tf_op jit(solution)/shard_map/ppermute | solution.py:18
  86.8 0.7 convert.16
  87.6 0.7 join_out.1
  88.3 1.2 %copy.32 = bf16[2,6,13,13,128]{4,0,3,2,1:T(2,128)(2,1)} copy(bf16[2,6,13,13,128]{4,3,2,1,0:T(8,128)(2,1)S(1)} %bitcast.53) | data formatting | bytes 1038336
  89.5 2.4 %collective-permute-done.29 = bf16[1,320,128]{2,1,0:T(8,128)(2,1)S(1)} collective-permute-done((bf16[1,320,128]{2,1,0:T(8,128)(2,1)S(1)}, bf16[1,320,128]{2,1,0:T(8,128)(2,1)S(1)}, u32[]{:S(2)}, u32[]{:S(2)}) %collective-permute-start.29) | collective-permute-done | bytes 81952 | tf_op jit(solution)/shard_map/ppermute | solution.py:18
  91.9 0.7 convert.14
  (99 shorter events, 4.8 us)
Async XLA Ops:
  0.6 8.1 %copy-start = (s32[2,2]{1,0:T(2,128)S(1)}, s32[2,2]{1,0:T(2,128)}, u32[]{:S(2)}) copy-start(s32[2,2]{1,0:T(2,128)} %param.8) | copy-start | bytes 52
  2.0 7.6 %collective-permute-start = (bf16[3,208,128]{2,1,0:T(8,128)(2,1)S(1)}, bf16[3,208,128]{2,1,0:T(8,128)(2,1)S(1)}, u32[]{:S(2)}, u32[]{:S(2)}) collective-permute-start(bf16[3,208,128]{2,1,0:T(8,128)(2,1)S(1)} %constant_dynamic-slice_fusion.3), channel_id=1, source_target_pairs={{0,1},{1,0},{2,3},{3,2},{4,5},{5,4},{6,7},{7,6},{8,9},{9,8},{10,11... | collective-permute-start | bytes 479240 | tf_op jit(solution)/shard_map/ppermute | solution.py:18
  2.5 11.2 %collective-permute-start.1 = (bf16[2,3,208,128]{3,2,1,0:T(8,128)(2,1)S(1)}, bf16[2,3,208,128]{3,2,1,0:T(8,128)(2,1)S(1)}, u32[]{:S(2)}, u32[]{:S(2)}) collective-permute-start(bf16[2,3,208,128]{3,2,1,0:T(8,128)(2,1)S(1)} %bitcast.69), channel_id=1, source_target_pairs={{0,2},{1,3},{2,0},{3,1},{4,6},{5,7},{6,4},{7,5},{8,10},{9,11},{10,... | collective-permute-start | bytes 958472 | tf_op jit(solution)/shard_map/ppermute | solution.py:18
  5.1 11.5 %collective-permute-start.3 = (bf16[2,3,208,128]{3,2,1,0:T(8,128)(2,1)S(1)}, bf16[2,3,208,128]{3,2,1,0:T(8,128)(2,1)S(1)}, u32[]{:S(2)}, u32[]{:S(2)}) collective-permute-start(bf16[2,3,208,128]{3,2,1,0:T(8,128)(2,1)S(1)} %bitcast.50), channel_id=1, source_target_pairs={{0,8},{4,12},{8,0},{12,4},{16,24},{20,28},{24,16},{28,20},{1,9},{5... | collective-permute-start | bytes 958472 | tf_op jit(solution)/shard_map/ppermute | solution.py:18
  8.0 8.6 %copy-start.2 = (f32[512]{0:T(512)S(1)}, f32[512]{0:T(512)}, u32[]{:S(2)}) copy-start(f32[512]{0:T(512)} %param.10) | copy-start | bytes 6148
  8.1 12.1 %collective-permute-start.5 = (bf16[2,3,208,128]{3,2,1,0:T(8,128)(2,1)S(1)}, bf16[2,3,208,128]{3,2,1,0:T(8,128)(2,1)S(1)}, u32[]{:S(2)}, u32[]{:S(2)}) collective-permute-start(bf16[2,3,208,128]{3,2,1,0:T(8,128)(2,1)S(1)} %pad_maximum_fusion), channel_id=1, source_target_pairs={{0,2},{1,3},{2,0},{3,1},{4,6},{5,7},{6,4},{7,5},{8,10},{9,11},{10,... | collective-permute-start | bytes 958472 | tf_op jit(solution)/shard_map/ppermute | solution.py:18
  14.5 2.1 %collective-permute-start.2 = (bf16[3,208,128]{2,1,0:T(8,128)(2,1)S(1)}, bf16[3,208,128]{2,1,0:T(8,128)(2,1)S(1)}, u32[]{:S(2)}, u32[]{:S(2)}) collective-permute-start(bf16[3,208,128]{2,1,0:T(8,128)(2,1)S(1)} %pick.1), channel_id=1, source_target_pairs={{0,1},{1,0},{2,3},{3,2},{4,5},{5,4},{6,7},{7,6},{8,9},{9,8},{10,11... | collective-permute-start | bytes 479240 | tf_op jit(solution)/shard_map/ppermute | solution.py:18
  14.6 10.0 %collective-permute-start.7 = (bf16[2,3,208,128]{3,2,1,0:T(8,128)(2,1)S(1)}, bf16[2,3,208,128]{3,2,1,0:T(8,128)(2,1)S(1)}, u32[]{:S(2)}, u32[]{:S(2)}) collective-permute-start(bf16[2,3,208,128]{3,2,1,0:T(8,128)(2,1)S(1)} %after_part.1.refs_0_.refs_1_), channel_id=1, source_target_pairs={{0,8},{4,12},{8,0},{12,4},{16,24},{20,28},{24,16},{28,20},{1,9},{5... | collective-permute-start | bytes 958472 | tf_op jit(solution)/shard_map/ppermute | solution.py:18
  16.5 5.9 %collective-permute-start.4 = (bf16[3,208,128]{2,1,0:T(8,128)(2,1)S(1)}, bf16[3,208,128]{2,1,0:T(8,128)(2,1)S(1)}, u32[]{:S(2)}, u32[]{:S(2)}) collective-permute-start(bf16[3,208,128]{2,1,0:T(8,128)(2,1)S(1)} %get-tuple-element.82.refs_4_), channel_id=1, source_target_pairs={{0,1},{1,0},{2,3},{3,2},{4,5},{5,4},{6,7},{7,6},{8,9},{9,8},{10,11... | collective-permute-start | bytes 479240 | tf_op jit(solution)/shard_map/ppermute | solution.py:18
  16.6 8.0 %copy-start.1 = (f32[512]{0:T(512)S(1)}, f32[512]{0:T(512)}, u32[]{:S(2)}) copy-start(f32[512]{0:T(512)} %param.12) | copy-start | bytes 6148
  20.1 2.2 %collective-permute-start.6 = (bf16[1,3,208,128]{3,2,1,0:T(8,128)(2,1)S(1)}, bf16[1,3,208,128]{3,2,1,0:T(8,128)(2,1)S(1)}, u32[]{:S(2)}, u32[]{:S(2)}) collective-permute-start(bf16[1,3,208,128]{3,2,1,0:T(8,128)(2,1)S(1)} %slice.110), channel_id=1, source_target_pairs={{0,1},{1,0},{2,3},{3,2},{4,5},{5,4},{6,7},{7,6},{8,9},{9,8},{10,11... | collective-permute-start | bytes 479240 | tf_op jit(solution)/shard_map/ppermute | solution.py:18
  20.3 24.7 %collective-permute-start.10 = (bf16[4,3,208,128]{3,2,1,0:T(8,128)(2,1)S(1)}, bf16[4,3,208,128]{3,2,1,0:T(8,128)(2,1)S(1)}, u32[]{:S(2)}, u32[]{:S(2)}) collective-permute-start(bf16[4,3,208,128]{3,2,1,0:T(8,128)(2,1)S(1)} %get-tuple-element.39.refs_0_), channel_id=1, source_target_pairs={{0,4},{4,0},{8,12},{12,8},{16,20},{20,16},{24,28},{28,24},{1,5},{5... | collective-permute-start | bytes 1916936 | tf_op jit(solution)/shard_map/ppermute | solution.py:18
  22.1 11.4 %collective-permute-start.8 = (bf16[2,3,208,128]{3,2,1,0:T(8,128)(2,1)S(1)}, bf16[2,3,208,128]{3,2,1,0:T(8,128)(2,1)S(1)}, u32[]{:S(2)}, u32[]{:S(2)}) collective-permute-start(bf16[2,3,208,128]{3,2,1,0:T(8,128)(2,1)S(1)} %slice.86), channel_id=1, source_target_pairs={{0,1},{1,0},{2,3},{3,2},{4,5},{5,4},{6,7},{7,6},{8,9},{9,8},{10,11... | collective-permute-start | bytes 958472 | tf_op jit(solution)/shard_map/ppermute | solution.py:18
  30.2 8.0 %collective-permute-start.12 = (bf16[3,208,256]{2,1,0:T(8,128)(2,1)S(1)}, bf16[3,208,256]{2,1,0:T(8,128)(2,1)S(1)}, u32[]{:S(2)}, u32[]{:S(2)}) collective-permute-start(bf16[3,208,256]{2,1,0:T(8,128)(2,1)S(1)} %get-tuple-element.49.refs_4_), channel_id=1, source_target_pairs={{0,1},{1,0},{2,3},{3,2},{4,5},{5,4},{6,7},{7,6},{8,9},{9,8},{10,11... | collective-permute-start | bytes 958472 | tf_op jit(solution)/shard_map/ppermute | solution.py:18
  30.3 14.2 %collective-permute-start.11 = (bf16[2,3,208,128]{3,2,1,0:T(8,128)(2,1)S(1)}, bf16[2,3,208,128]{3,2,1,0:T(8,128)(2,1)S(1)}, u32[]{:S(2)}, u32[]{:S(2)}) collective-permute-start(bf16[2,3,208,128]{3,2,1,0:T(8,128)(2,1)S(1)} %get-tuple-element.45), channel_id=1, source_target_pairs={{0,2},{1,3},{2,0},{3,1},{4,6},{5,7},{6,4},{7,5},{8,10},{9,11},{10,... | collective-permute-start | bytes 958472 | tf_op jit(solution)/shard_map/ppermute | solution.py:18
  32.0 13.0 %collective-permute-start.9 = (bf16[3,208,256]{2,1,0:T(8,128)(2,1)S(1)}, bf16[3,208,256]{2,1,0:T(8,128)(2,1)S(1)}, u32[]{:S(2)}, u32[]{:S(2)}) collective-permute-start(bf16[3,208,256]{2,1,0:T(8,128)(2,1)S(1)} %get-tuple-element.44), channel_id=1, source_target_pairs={{0,4},{4,0},{8,12},{12,8},{16,20},{20,16},{24,28},{28,24},{1,5},{5... | collective-permute-start | bytes 958472 | tf_op jit(solution)/shard_map/ppermute | solution.py:18
  38.1 7.6 %collective-permute-start.16 = (bf16[3,208,256]{2,1,0:T(8,128)(2,1)S(1)}, bf16[3,208,256]{2,1,0:T(8,128)(2,1)S(1)}, u32[]{:S(2)}, u32[]{:S(2)}) collective-permute-start(bf16[3,208,256]{2,1,0:T(8,128)(2,1)S(1)} %get-tuple-element.54.refs_4_), channel_id=1, source_target_pairs={{0,1},{1,0},{2,3},{3,2},{4,5},{5,4},{6,7},{7,6},{8,9},{9,8},{10,11... | collective-permute-start | bytes 958472 | tf_op jit(solution)/shard_map/ppermute | solution.py:18
  38.1 13.6 %collective-permute-start.17 = (bf16[3,208,256]{2,1,0:T(8,128)(2,1)S(1)}, bf16[3,208,256]{2,1,0:T(8,128)(2,1)S(1)}, u32[]{:S(2)}, u32[]{:S(2)}) collective-permute-start(bf16[3,208,256]{2,1,0:T(8,128)(2,1)S(1)} %get-tuple-element.56), channel_id=1, source_target_pairs={{0,8},{4,12},{8,0},{12,4},{16,24},{20,28},{24,16},{28,20},{1,9},{5... | collective-permute-start | bytes 958472 | tf_op jit(solution)/shard_map/ppermute | solution.py:18
  44.4 9.7 %collective-permute-start.18 = (bf16[2,3,208,128]{3,2,1,0:T(8,128)(2,1)S(1)}, bf16[2,3,208,128]{3,2,1,0:T(8,128)(2,1)S(1)}, u32[]{:S(2)}, u32[]{:S(2)}) collective-permute-start(bf16[2,3,208,128]{3,2,1,0:T(8,128)(2,1)S(1)} %get-tuple-element.58), channel_id=1, source_target_pairs={{0,2},{1,3},{2,0},{3,1},{4,6},{5,7},{6,4},{7,5},{8,10},{9,11},{10,... | collective-permute-start | bytes 958472 | tf_op jit(solution)/shard_map/ppermute | solution.py:18
  45.1 2.4 %collective-permute-start.13 = (bf16[2,3,208,128]{3,2,1,0:T(8,128)(2,1)S(1)}, bf16[2,3,208,128]{3,2,1,0:T(8,128)(2,1)S(1)}, u32[]{:S(2)}, u32[]{:S(2)}) collective-permute-start(bf16[2,3,208,128]{3,2,1,0:T(8,128)(2,1)S(1)} %slice.87), channel_id=1, source_target_pairs={{0,1},{1,0},{2,3},{3,2},{4,5},{5,4},{6,7},{7,6},{8,9},{9,8},{10,11... | collective-permute-start | bytes 958472 | tf_op jit(solution)/shard_map/ppermute | solution.py:18
  45.1 2.3 %collective-permute-start.14 = (bf16[3,208,256]{2,1,0:T(8,128)(2,1)S(1)}, bf16[3,208,256]{2,1,0:T(8,128)(2,1)S(1)}, u32[]{:S(2)}, u32[]{:S(2)}) collective-permute-start(bf16[3,208,256]{2,1,0:T(8,128)(2,1)S(1)} %get-tuple-element.52.refs_6_), channel_id=1, source_target_pairs={{0,1},{1,0},{2,3},{3,2},{4,5},{5,4},{6,7},{7,6},{8,9},{9,8},{10,11... | collective-permute-start | bytes 958472 | tf_op jit(solution)/shard_map/ppermute | solution.py:18
  45.7 1.8 %collective-permute-start.15 = (bf16[3,208,128]{2,1,0:T(8,128)(2,1)S(1)}, bf16[3,208,128]{2,1,0:T(8,128)(2,1)S(1)}, u32[]{:S(2)}, u32[]{:S(2)}) collective-permute-start(bf16[3,208,128]{2,1,0:T(8,128)(2,1)S(1)} %slice_bitcast_fusion.1), channel_id=1, source_target_pairs={{0,1},{1,0},{2,3},{3,2},{4,5},{5,4},{6,7},{7,6},{8,9},{9,8},{10,11... | collective-permute-start | bytes 479240 | tf_op jit(solution)/shard_map/ppermute | solution.py:18
  54.1 1.6 %collective-permute-start.19 = (bf16[3,208,256]{2,1,0:T(8,128)(2,1)S(1)}, bf16[3,208,256]{2,1,0:T(8,128)(2,1)S(1)}, u32[]{:S(2)}, u32[]{:S(2)}) collective-permute-start(bf16[3,208,256]{2,1,0:T(8,128)(2,1)S(1)} %after_grad5.1.refs_6_), channel_id=1, source_target_pairs={{0,1},{1,0},{2,3},{3,2},{4,5},{5,4},{6,7},{7,6},{8,9},{9,8},{10,11... | collective-permute-start | bytes 958472 | tf_op jit(solution)/shard_map/ppermute | solution.py:18
  54.1 9.3 %collective-permute-start.30 = (bf16[4,272,128]{2,1,0:T(8,128)(2,1)S(1)}, bf16[4,272,128]{2,1,0:T(8,128)(2,1)S(1)}, u32[]{:S(2)}, u32[]{:S(2)}) collective-permute-start(bf16[4,272,128]{2,1,0:T(8,128)(2,1)S(1)} %get-tuple-element.67), channel_id=1, source_target_pairs={{0,2},{1,3},{2,0},{3,1},{4,6},{5,7},{6,4},{7,5},{8,10},{9,11},{10,... | collective-permute-start | bytes 835592 | tf_op jit(solution)/shard_map/ppermute | solution.py:18
  54.6 9.8 %collective-permute-start.20 = (bf16[4,320,128]{2,1,0:T(8,128)(2,1)S(1)}, bf16[4,320,128]{2,1,0:T(8,128)(2,1)S(1)}, u32[]{:S(2)}, u32[]{:S(2)}) collective-permute-start(bf16[4,320,128]{2,1,0:T(8,128)(2,1)S(1)} %get-tuple-element.60), channel_id=1, source_target_pairs={{0,8},{4,12},{8,0},{12,4},{16,24},{20,28},{24,16},{28,20},{1,9},{5... | collective-permute-start | bytes 983048 | tf_op jit(solution)/shard_map/ppermute | solution.py:18
  60.0 9.6 %collective-permute-start.24 = (bf16[4,272,128]{2,1,0:T(8,128)(2,1)S(1)}, bf16[4,272,128]{2,1,0:T(8,128)(2,1)S(1)}, u32[]{:S(2)}, u32[]{:S(2)}) collective-permute-start(bf16[4,272,128]{2,1,0:T(8,128)(2,1)S(1)} %get-tuple-element.64), channel_id=1, source_target_pairs={{0,2},{1,3},{2,0},{3,1},{4,6},{5,7},{6,4},{7,5},{8,10},{9,11},{10,... | collective-permute-start | bytes 835592 | tf_op jit(solution)/shard_map/ppermute | solution.py:18
  63.5 6.2 %collective-permute-start.31 = (bf16[2,272,128]{2,1,0:T(8,128)(2,1)S(1)}, bf16[2,272,128]{2,1,0:T(8,128)(2,1)S(1)}, u32[]{:S(2)}, u32[]{:S(2)}) collective-permute-start(bf16[2,272,128]{2,1,0:T(8,128)(2,1)S(1)} %get-tuple-element.88), channel_id=1, source_target_pairs={{0,8},{4,12},{8,0},{12,4},{16,24},{20,28},{24,16},{28,20},{1,9},{5... | collective-permute-start | bytes 417800 | tf_op jit(solution)/shard_map/ppermute | solution.py:18
  63.8 9.2 %collective-permute-start.22 = (bf16[4,320,128]{2,1,0:T(8,128)(2,1)S(1)}, bf16[4,320,128]{2,1,0:T(8,128)(2,1)S(1)}, u32[]{:S(2)}, u32[]{:S(2)}) collective-permute-start(bf16[4,320,128]{2,1,0:T(8,128)(2,1)S(1)} %get-tuple-element.62), channel_id=1, source_target_pairs={{0,4},{4,0},{8,12},{12,8},{16,20},{20,16},{24,28},{28,24},{1,5},{5... | collective-permute-start | bytes 983048 | tf_op jit(solution)/shard_map/ppermute | solution.py:18
  64.6 8.6 %collective-permute-start.33 = (bf16[2,320,128]{2,1,0:T(8,128)(2,1)S(1)}, bf16[2,320,128]{2,1,0:T(8,128)(2,1)S(1)}, u32[]{:S(2)}, u32[]{:S(2)}) collective-permute-start(bf16[2,320,128]{2,1,0:T(8,128)(2,1)S(1)} %get-tuple-element.86), channel_id=1, source_target_pairs={{0,2},{1,3},{2,0},{3,1},{4,6},{5,7},{6,4},{7,5},{8,10},{9,11},{10,... | collective-permute-start | bytes 491528 | tf_op jit(solution)/shard_map/ppermute | solution.py:18
  66.2 21.4 %collective-permute-start.21 = (bf16[3,208,128]{2,1,0:T(8,128)(2,1)S(1)}, bf16[3,208,128]{2,1,0:T(8,128)(2,1)S(1)}, u32[]{:S(2)}, u32[]{:S(2)}) collective-permute-start(bf16[3,208,128]{2,1,0:T(8,128)(2,1)S(1)} %after_step.6), channel_id=1, source_target_pairs={{0,1},{1,0},{2,3},{3,2},{4,5},{5,4},{6,7},{7,6},{8,9},{9,8},{10,11... | collective-permute-start | bytes 479240 | tf_op jit(solution)/shard_map/ppermute | solution.py:18
  69.8 15.3 %collective-permute-start.32 = (bf16[1,272,128]{2,1,0:T(8,128)(2,1)S(1)}, bf16[1,272,128]{2,1,0:T(8,128)(2,1)S(1)}, u32[]{:S(2)}, u32[]{:S(2)}) collective-permute-start(bf16[1,272,128]{2,1,0:T(8,128)(2,1)S(1)} %get-tuple-element.92), channel_id=1, source_target_pairs={{0,16},{4,20},{8,24},{12,28},{16,0},{20,4},{24,8},{28,12},{1,17},{... | collective-permute-start | bytes 208904 | tf_op jit(solution)/shard_map/ppermute | solution.py:18
  72.5 5.1 %collective-permute-start.27 = (bf16[2,272,128]{2,1,0:T(8,128)(2,1)S(1)}, bf16[2,272,128]{2,1,0:T(8,128)(2,1)S(1)}, u32[]{:S(2)}, u32[]{:S(2)}) collective-permute-start(bf16[2,272,128]{2,1,0:T(8,128)(2,1)S(1)} %slice.114), channel_id=1, source_target_pairs={{0,4},{4,0},{8,12},{12,8},{16,20},{20,16},{24,28},{28,24},{1,5},{5... | collective-permute-start | bytes 417800 | tf_op jit(solution)/shard_map/ppermute | solution.py:18
  73.0 5.6 %collective-permute-start.26 = (bf16[3,208,128]{2,1,0:T(8,128)(2,1)S(1)}, bf16[3,208,128]{2,1,0:T(8,128)(2,1)S(1)}, u32[]{:S(2)}, u32[]{:S(2)}) collective-permute-start(bf16[3,208,128]{2,1,0:T(8,128)(2,1)S(1)} %slice_bitcast_fusion), channel_id=1, source_target_pairs={{0,1},{1,0},{2,3},{3,2},{4,5},{5,4},{6,7},{7,6},{8,9},{9,8},{10,11... | collective-permute-start | bytes 479240 | tf_op jit(solution)/shard_map/ppermute | solution.py:18
  73.2 6.0 %collective-permute-start.25 = (bf16[3,208,128]{2,1,0:T(8,128)(2,1)S(1)}, bf16[3,208,128]{2,1,0:T(8,128)(2,1)S(1)}, u32[]{:S(2)}, u32[]{:S(2)}) collective-permute-start(bf16[3,208,128]{2,1,0:T(8,128)(2,1)S(1)} %get-tuple-element.65), channel_id=1, source_target_pairs={{0,1},{1,0},{2,3},{3,2},{4,5},{5,4},{6,7},{7,6},{8,9},{9,8},{10,11... | collective-permute-start | bytes 479240 | tf_op jit(solution)/shard_map/ppermute | solution.py:18
  77.5 7.0 %collective-permute-start.28 = (bf16[1,272,128]{2,1,0:T(8,128)(2,1)S(1)}, bf16[1,272,128]{2,1,0:T(8,128)(2,1)S(1)}, u32[]{:S(2)}, u32[]{:S(2)}) collective-permute-start(bf16[1,272,128]{2,1,0:T(8,128)(2,1)S(1)} %slice.116), channel_id=1, source_target_pairs={{0,16},{4,20},{8,24},{12,28},{16,0},{20,4},{24,8},{28,12},{1,17},{... | collective-permute-start | bytes 208904 | tf_op jit(solution)/shard_map/ppermute | solution.py:18
  78.6 6.5 %collective-permute-start.23 = (bf16[2,320,128]{2,1,0:T(8,128)(2,1)S(1)}, bf16[2,320,128]{2,1,0:T(8,128)(2,1)S(1)}, u32[]{:S(2)}, u32[]{:S(2)}) collective-permute-start(bf16[2,320,128]{2,1,0:T(8,128)(2,1)S(1)} %slice.112), channel_id=1, source_target_pairs={{0,2},{1,3},{2,0},{3,1},{4,6},{5,7},{6,4},{7,5},{8,10},{9,11},{10,... | collective-permute-start | bytes 491528 | tf_op jit(solution)/shard_map/ppermute | solution.py:18
  79.2 7.6 %collective-permute-start.34 = (bf16[1,320,128]{2,1,0:T(8,128)(2,1)S(1)}, bf16[1,320,128]{2,1,0:T(8,128)(2,1)S(1)}, u32[]{:S(2)}, u32[]{:S(2)}) collective-permute-start(bf16[1,320,128]{2,1,0:T(8,128)(2,1)S(1)} %get-tuple-element.90), channel_id=1, source_target_pairs={{0,16},{4,20},{8,24},{12,28},{16,0},{20,4},{24,8},{28,12},{1,17},{... | collective-permute-start | bytes 245768 | tf_op jit(solution)/shard_map/ppermute | solution.py:18
  85.7 6.2 %collective-permute-start.29 = (bf16[1,320,128]{2,1,0:T(8,128)(2,1)S(1)}, bf16[1,320,128]{2,1,0:T(8,128)(2,1)S(1)}, u32[]{:S(2)}, u32[]{:S(2)}) collective-permute-start(bf16[1,320,128]{2,1,0:T(8,128)(2,1)S(1)} %slice.119), channel_id=1, source_target_pairs={{0,16},{4,20},{8,24},{12,28},{16,0},{20,4},{24,8},{28,12},{1,17},{... | collective-permute-start | bytes 245768 | tf_op jit(solution)/shard_map/ppermute | solution.py:18

commit v3 on v2

--- a/solution.py
+++ b/solution.py
@@ -580,7 +580,7 @@
         [vmem] * 6,
         [quarter_t, quarter_t, pair_t, whole_t, half_t, half_t],
         [shifted_of(channels), pltpu.VMEM((group * cells, channels), BF16)],
-        [far_a],
+        [],
         flops=work * 0 // 8,
     )(hidden, *cots, bias5, near5)
     out_far = over_x(outs[2])
@@ -597,7 +597,7 @@
         [vmem] * 4,
         [whole_t, half_t, half_t, weight_t],
         [shifted_of(channels), pltpu.SemaphoreType.DMA],
-        [hidden_core],
+        [far_a, hidden_core],
         flops=work * 0 // 8,
     )(slope5, factor4, near5, weight4)
     kept4_core, across4 = over_core(kept4), over_a(sent4)
@@ -611,7 +611,7 @@
         [quarter_t, quarter_t, pair_t],
         [shifted_of(channels)],
         [kept5_core],
-        flops=work * 8 // 8,
+        flops=work * 4 // 8,
     )(slope4, near4)
     back_far = over_x(backs[2])
 

time: 92.9 us -> 90.4 us (0.973)
  waiting for transfers between devices: 20.6 us -> 17.8 us
    ppermute x35, waiting for transfers between devices: 20.6 us -> 17.8 us  [swap(): return lax.ppermute(value, axis_name, [(i, i ^ bit) for i in range(size)])]
  transfers between devices with their start and end apart: 35 -> 35, of which waited for: 12 -> 11; matrix products, arithmetic and copies ran while one was open for 8% -> 8% of each run, Pallas kernels for 35% -> 36%
where the time goes in v3:
time: 90.4 us; the launch traced here: 90.3 us
  Pallas kernels  32.9 us (36%)
  starting transfers between devices  29.2 us (32%)
  waiting for transfers between devices  17.8 us (20%)
  local copies, waits for them, and re-layouts  5.89 us (7%)
  other arithmetic  3.34 us (4%)
  between operations  1.18 us (1%)
    pallas_call x10, Pallas kernels, call(): return lambda *args: called(info, *args, *after)  32.9 us
    ppermute x35, starting transfers between devices, swap(): return lax.ppermute(value, axis_name, [(i, i ^ bit) for i in range(size)])  29.2 us
    ppermute x35, waiting for transfers between devices, swap(): return lax.ppermute(value, axis_name, [(i, i ^ bit) for i in range(size)])  17.8 us
    unnamed x10, local copies, waits for them, and re-layouts  4.69 us
  transfers between devices with their start and end apart: 35, of which 11 were waited for; matrix products, arithmetic and copies ran while one was open for 8% of the time, Pallas kernels for 36%

profile of v3, /device:TPU:0, one launch (start us, length us, event | category | flops | bytes accessed | tf_op | source)
XLA Modules:
  0.0 90.3 jit_solution(2550874920302941527)
XLA Ops:
  0.7 1.1 %copy.30 = bf16[2,6,13,13,128]{4,3,2,1,0:T(8,128)(2,1)S(1)} copy(bf16[2,6,13,13,128]{4,0,3,2,1:T(2,128)(2,1)} %param.7) | data formatting | bytes 1038336 | tf_op args[0]
  2.0 0.5 collective-permute-start
  2.5 2.6 %collective-permute-start.1 = (bf16[2,3,208,128]{3,2,1,0:T(8,128)(2,1)S(1)}, bf16[2,3,208,128]{3,2,1,0:T(8,128)(2,1)S(1)}, u32[]{:S(2)}, u32[]{:S(2)}) collective-permute-start(bf16[2,3,208,128]{3,2,1,0:T(8,128)(2,1)S(1)} %bitcast.69), channel_id=1, source_target_pairs={{0,2},{1,3},{2,0},{3,1},{4,6},{5,7},{6,4},{7,5},{8,10},{9,11},{10,... | collective-permute-start | bytes 958472 | tf_op jit(solution)/shard_map/ppermute | solution.py:18
  5.1 1.6 %collective-permute-start.3 = (bf16[2,3,208,128]{3,2,1,0:T(8,128)(2,1)S(1)}, bf16[2,3,208,128]{3,2,1,0:T(8,128)(2,1)S(1)}, u32[]{:S(2)}, u32[]{:S(2)}) collective-permute-start(bf16[2,3,208,128]{3,2,1,0:T(8,128)(2,1)S(1)} %bitcast.50), channel_id=1, source_target_pairs={{0,8},{4,12},{8,0},{12,4},{16,24},{20,28},{24,16},{28,20},{1,9},{5... | collective-permute-start | bytes 958472 | tf_op jit(solution)/shard_map/ppermute | solution.py:18
  6.7 1.1 %copy.31 = bf16[2,6,13,13,128]{4,3,2,1,0:T(8,128)(2,1)S(1)} copy(bf16[2,6,13,13,128]{4,0,3,2,1:T(2,128)(2,1)} %param.13) | data formatting | bytes 1038336 | tf_op args[6]
  8.1 0.6 collective-permute-start.5
  8.8 0.6 gather_fusion
  9.6 4.2 %conv4_part.1 = (f32[2,624,256]{2,1,0:T(8,128)S(1)}, bf16[9,256,512]{2,1,0:T(8,128)(2,1)S(1)}) custom-call(s32[5]{0:T(128)S(1)} %pad_add_fusion.info, bf16[2,3,208,128]{3,2,1,0:T(8,128)(2,1)S(1)} %bitcast.51, bf16[3,208,128]{2,1,0:T(8,128)(2,1)S(1)} %collective-permute-done.refs_1_, bf16[9,512,512]{2,1,0:T(8,128)(2,1)} %bitcast.57, ...), custom_call_target="tpu_custom_call" | custom-call | tf_op jit(solution)/shard_map/conv4_part/pallas_call | solution.py:446
  13.8 0.8 pick.1
  14.6 1.8 %collective-permute-start.11 = (bf16[2,3,208,128]{3,2,1,0:T(8,128)(2,1)S(1)}, bf16[2,3,208,128]{3,2,1,0:T(8,128)(2,1)S(1)}, u32[]{:S(2)}, u32[]{:S(2)}) collective-permute-start(bf16[2,3,208,128]{3,2,1,0:T(8,128)(2,1)S(1)} %after_part.1.refs_0_.refs_1_), channel_id=1, source_target_pairs={{0,8},{4,12},{8,0},{12,4},{16,24},{20,28},{24,16},{28,20},{1,9},{5... | collective-permute-start | bytes 958472 | tf_op jit(solution)/shard_map/ppermute | solution.py:18
  16.5 3.2 %conv4.1 = (bf16[4,3,208,128]{3,2,1,0:T(8,128)(2,1)S(1)}, f32[2,624,256]{2,1,0:T(8,128)S(1)}, bf16[9,512,512]{2,1,0:T(8,128)(2,1)S(1)}) custom-call(s32[5]{0:T(128)S(1)} %pad_add_fusion.info, f32[2,624,256]{2,1,0:T(8,128)S(1)} %get-tuple-element.37.refs_1_.refs_0_, bf16[2,3,208,128]{3,2,1,0:T(8,128)(2,1)S(1)} %after_part.1.refs_0_.refs_1_, ...), custom_call_target="tpu_custom_call" | custom-call | tf_op jit(solution)/shard_map/conv4/pallas_call | solution.py:446
  19.7 1.6 %collective-permute-start.9 = (bf16[4,3,208,128]{3,2,1,0:T(8,128)(2,1)S(1)}, bf16[4,3,208,128]{3,2,1,0:T(8,128)(2,1)S(1)}, u32[]{:S(2)}, u32[]{:S(2)}) collective-permute-start(bf16[4,3,208,128]{3,2,1,0:T(8,128)(2,1)S(1)} %get-tuple-element.39.refs_0_), channel_id=1, source_target_pairs={{0,4},{4,0},{8,12},{12,8},{16,20},{20,16},{24,28},{28,24},{1,5},{5... | collective-permute-start | bytes 1916936 | tf_op jit(solution)/shard_map/ppermute | solution.py:18
  21.3 0.6 collective-permute-start.6
  22.0 0.7 collective-permute-done.4.refs_2_
  22.9 5.6 %conv5.1 = (bf16[3,208,128]{2,1,0:T(8,128)(2,1)S(1)}, bf16[3,208,128]{2,1,0:T(8,128)(2,1)S(1)}, bf16[2,3,208,128]{3,2,1,0:T(8,128)(2,1)S(1)}, bf16[3,208,512]{2,...) custom-call(s32[5]{0:T(128)S(1)} %pad_add_fusion.info, ...), custom_call_target="tpu_custom_call" | custom-call | tf_op jit(solution)/shard_map/conv5/pallas_call | solution.py:446
  28.9 1.5 %collective-permute-start.10 = (bf16[2,3,208,128]{3,2,1,0:T(8,128)(2,1)S(1)}, bf16[2,3,208,128]{3,2,1,0:T(8,128)(2,1)S(1)}, u32[]{:S(2)}, u32[]{:S(2)}) collective-permute-start(bf16[2,3,208,128]{3,2,1,0:T(8,128)(2,1)S(1)} %get-tuple-element.45), channel_id=1, source_target_pairs={{0,2},{1,3},{2,0},{3,1},{4,6},{5,7},{6,4},{7,5},{8,10},{9,11},{10,... | collective-permute-start | bytes 958472 | tf_op jit(solution)/shard_map/ppermute | solution.py:18
  30.9 4.5 %back5.1 = (bf16[3,208,512]{2,1,0:T(8,128)(2,1)S(1)}, bf16[3,208,256]{2,1,0:T(8,128)(2,1)S(1)}, bf16[3,208,256]{2,1,0:T(8,128)(2,1)S(1)}, bf16[9,512,512]{2,1,0:T(8,128)(2,1)S(1)}) custom-call(s32[5]{0:T(128)S(1)} %pad_add_fusion.info, bf16[3,208,512]{2,1,0:T(8,128)(2,1)S(1)} %get-tuple-element.46.refs_0_, f32[2,624,256]{2,1,0:T(8,128)S(1)} %get-tuple-element.40.refs_1_, ...), custom_call_target="tpu_custom_call" | custom-call | tf_op jit(solution)/shard_map/back5/pallas_call | solution.py:446
  35.6 1.4 %collective-permute-start.17 = (bf16[3,208,256]{2,1,0:T(8,128)(2,1)S(1)}, bf16[3,208,256]{2,1,0:T(8,128)(2,1)S(1)}, u32[]{:S(2)}, u32[]{:S(2)}) collective-permute-start(bf16[3,208,256]{2,1,0:T(8,128)(2,1)S(1)} %get-tuple-element.56), channel_id=1, source_target_pairs={{0,8},{4,12},{8,0},{12,4},{16,24},{20,28},{24,16},{28,20},{1,9},{5... | collective-permute-start | bytes 958472 | tf_op jit(solution)/shard_map/ppermute | solution.py:18
  37.0 4.6 %back4.1 = (bf16[3,208,128]{2,1,0:T(8,128)(2,1)S(1)}, bf16[3,208,128]{2,1,0:T(8,128)(2,1)S(1)}, bf16[2,3,208,128]{3,2,1,0:T(8,128)(2,1)S(1)}) custom-call(s32[5]{0:T(128)S(1)} %pad_add_fusion.info, bf16[3,208,512]{2,1,0:T(8,128)(2,1)S(1)} %get-tuple-element.47.refs_0_, bf16[9,512,512]{2,1,0:T(8,128)(2,1)S(1)} %get-tuple-element.48.refs_1_, ...), custom_call_target="tpu_custom_call" | custom-call | flops 1472200704 | tf_op jit(solution)/shard_map/back4/pallas_call | solution.py:446
  41.6 0.6 collective-permute-start.18
  42.2 0.9 collective-permute-done.8.refs_0_
  43.8 1.6 %collective-permute-done.15.refs_8_.refs_3_ = bf16[3,208,128]{2,1,0:T(8,128)(2,1)S(1)} collective-permute-done((bf16[3,208,128]{2,1,0:T(8,128)(2,1)S(1)}, bf16[3,208,128]{2,1,0:T(8,128)(2,1)S(1)}, u32[]{:S(2)}, u32[]{:S(2)}) %collective-permute-start.15) | collective-permute-done | bytes 159776 | tf_op jit(solution)/shard_map/ppermute | solution.py:18
  45.5 4.3 %grad5.1 = (bf16[4,272,128]{2,1,0:T(8,128)(2,1)S(1)}, bf16[4,272,128]{2,1,0:T(8,128)(2,1)S(1)}, bf16[4,320,128]{2,1,0:T(8,128)(2,1)S(1)}, bf16[4,320,128]{2,1,0:T(8,128)(2,1)S(1)}) custom-call(s32[5]{0:T(128)S(1)} %pad_add_fusion.info, bf16[4,3,208,128]{3,2,1,0:T(8,128)(2,1)S(1)} %get-tuple-element.39.refs_0_, ...), custom_call_target="tpu_custom_call" | custom-call | tf_op jit(solution)/shard_map/grad5/pallas_call | solution.py:446
  49.8 1.5 %collective-permute-done.18.refs_2_.refs_1_ = bf16[2,3,208,128]{3,2,1,0:T(8,128)(2,1)S(1)} collective-permute-done((bf16[2,3,208,128]{3,2,1,0:T(8,128)(2,1)S(1)}, bf16[2,3,208,128]{3,2,1,0:T(8,128)(2,1)S(1)}, u32[]{:S(2)}, u32[]{:S(2)}) %collective-permute-start.18) | collective-permute-done | bytes 319520 | tf_op jit(solution)/shard_map/ppermute | solution.py:18
  51.3 0.5 collective-permute-start.30
  51.8 1.0 %collective-permute-start.20 = (bf16[4,320,128]{2,1,0:T(8,128)(2,1)S(1)}, bf16[4,320,128]{2,1,0:T(8,128)(2,1)S(1)}, u32[]{:S(2)}, u32[]{:S(2)}) collective-permute-start(bf16[4,320,128]{2,1,0:T(8,128)(2,1)S(1)} %get-tuple-element.60), channel_id=1, source_target_pairs={{0,8},{4,12},{8,0},{12,4},{16,24},{20,28},{24,16},{28,20},{1,9},{5... | collective-permute-start | bytes 983048 | tf_op jit(solution)/shard_map/ppermute | solution.py:18
  52.9 4.3 %grad4.1 = (bf16[4,272,128]{2,1,0:T(8,128)(2,1)S(1)}, bf16[4,272,128]{2,1,0:T(8,128)(2,1)S(1)}, bf16[4,320,128]{2,1,0:T(8,128)(2,1)S(1)}, bf16[4,320,128]{2,1,0:T(8,128)(2,1)S(1)}) custom-call(s32[5]{0:T(128)S(1)} %pad_add_fusion.info, bf16[2,3,208,128]{3,2,1,0:T(8,128)(2,1)S(1)} %bitcast.52, bf16[2,3,208,128]{3,2,1,0:T(8,128)(2,1)S(1)} %after_part.1.refs_0_.refs_1_, ...), custom_call_target="tpu_custom_call" | custom-call | tf_op jit(solution)/shard_map/grad4/pallas_call | solution.py:446
  57.2 1.2 %collective-permute-start.24 = (bf16[4,272,128]{2,1,0:T(8,128)(2,1)S(1)}, bf16[4,272,128]{2,1,0:T(8,128)(2,1)S(1)}, u32[]{:S(2)}, u32[]{:S(2)}) collective-permute-start(bf16[4,272,128]{2,1,0:T(8,128)(2,1)S(1)} %get-tuple-element.64), channel_id=1, source_target_pairs={{0,2},{1,3},{2,0},{3,1},{4,6},{5,7},{6,4},{7,5},{8,10},{9,11},{10,... | collective-permute-start | bytes 835592 | tf_op jit(solution)/shard_map/ppermute | solution.py:18
  58.4 2.2 %collective-permute-done.30 = bf16[4,272,128]{2,1,0:T(8,128)(2,1)S(1)} collective-permute-done((bf16[4,272,128]{2,1,0:T(8,128)(2,1)S(1)}, bf16[4,272,128]{2,1,0:T(8,128)(2,1)S(1)}, u32[]{:S(2)}, u32[]{:S(2)}) %collective-permute-start.30) | collective-permute-done | bytes 278560 | tf_op jit(solution)/shard_map/ppermute | solution.py:18
  60.7 0.7 collective-permute-start.31
  61.4 1.6 %collective-permute-start.22 = (bf16[4,320,128]{2,1,0:T(8,128)(2,1)S(1)}, bf16[4,320,128]{2,1,0:T(8,128)(2,1)S(1)}, u32[]{:S(2)}, u32[]{:S(2)}) collective-permute-start(bf16[4,320,128]{2,1,0:T(8,128)(2,1)S(1)} %get-tuple-element.62), channel_id=1, source_target_pairs={{0,4},{4,0},{8,12},{12,8},{16,20},{20,16},{24,28},{28,24},{1,5},{5... | collective-permute-start | bytes 983048 | tf_op jit(solution)/shard_map/ppermute | solution.py:18
  63.1 0.5 collective-permute-start.33
  63.6 3.2 %collective-permute-done.24 = bf16[4,272,128]{2,1,0:T(8,128)(2,1)S(1)} collective-permute-done((bf16[4,272,128]{2,1,0:T(8,128)(2,1)S(1)}, bf16[4,272,128]{2,1,0:T(8,128)(2,1)S(1)}, u32[]{:S(2)}, u32[]{:S(2)}) %collective-permute-start.24) | collective-permute-done | bytes 278560 | tf_op jit(solution)/shard_map/ppermute | solution.py:18
  67.0 2.6 %collective-permute-start.32 = (bf16[1,272,128]{2,1,0:T(8,128)(2,1)S(1)}, bf16[1,272,128]{2,1,0:T(8,128)(2,1)S(1)}, u32[]{:S(2)}, u32[]{:S(2)}) collective-permute-start(bf16[1,272,128]{2,1,0:T(8,128)(2,1)S(1)} %get-tuple-element.92), channel_id=1, source_target_pairs={{0,16},{4,20},{8,24},{12,28},{16,0},{20,4},{24,8},{28,12},{1,17},{... | collective-permute-start | bytes 208904 | tf_op jit(solution)/shard_map/ppermute | solution.py:18
  69.6 1.5 %collective-permute-start.27 = (bf16[2,272,128]{2,1,0:T(8,128)(2,1)S(1)}, bf16[2,272,128]{2,1,0:T(8,128)(2,1)S(1)}, u32[]{:S(2)}, u32[]{:S(2)}) collective-permute-start(bf16[2,272,128]{2,1,0:T(8,128)(2,1)S(1)} %slice.114), channel_id=1, source_target_pairs={{0,4},{4,0},{8,12},{12,8},{16,20},{20,16},{24,28},{28,24},{1,5},{5... | collective-permute-start | bytes 417800 | tf_op jit(solution)/shard_map/ppermute | solution.py:18
  71.3 0.6 collective-permute-start.25
  71.9 2.8 %collective-permute-done.27 = bf16[2,272,128]{2,1,0:T(8,128)(2,1)S(1)} collective-permute-done((bf16[2,272,128]{2,1,0:T(8,128)(2,1)S(1)}, bf16[2,272,128]{2,1,0:T(8,128)(2,1)S(1)}, u32[]{:S(2)}, u32[]{:S(2)}) %collective-permute-start.27) | collective-permute-done | bytes 139296 | tf_op jit(solution)/shard_map/ppermute | solution.py:18
  74.7 1.2 %collective-permute-start.28 = (bf16[1,272,128]{2,1,0:T(8,128)(2,1)S(1)}, bf16[1,272,128]{2,1,0:T(8,128)(2,1)S(1)}, u32[]{:S(2)}, u32[]{:S(2)}) collective-permute-start(bf16[1,272,128]{2,1,0:T(8,128)(2,1)S(1)} %slice.116), channel_id=1, source_target_pairs={{0,16},{4,20},{8,24},{12,28},{16,0},{20,4},{24,8},{28,12},{1,17},{... | collective-permute-start | bytes 208904 | tf_op jit(solution)/shard_map/ppermute | solution.py:18
  76.0 0.6 collective-permute-start.23
  76.6 2.4 %collective-permute-start.34 = (bf16[1,320,128]{2,1,0:T(8,128)(2,1)S(1)}, bf16[1,320,128]{2,1,0:T(8,128)(2,1)S(1)}, u32[]{:S(2)}, u32[]{:S(2)}) collective-permute-start(bf16[1,320,128]{2,1,0:T(8,128)(2,1)S(1)} %get-tuple-element.90), channel_id=1, source_target_pairs={{0,16},{4,20},{8,24},{12,28},{16,0},{20,4},{24,8},{28,12},{1,17},{... | collective-permute-start | bytes 245768 | tf_op jit(solution)/shard_map/ppermute | solution.py:18
  79.0 0.7 join_grad.1
  79.6 1.2 %copy.33 = bf16[2,6,13,13,128]{4,0,3,2,1:T(2,128)(2,1)} copy(bf16[2,6,13,13,128]{4,3,2,1,0:T(8,128)(2,1)S(1)} %bitcast.54) | data formatting | bytes 1038336
  80.9 2.1 %collective-permute-done.28 = bf16[1,272,128]{2,1,0:T(8,128)(2,1)S(1)} collective-permute-done((bf16[1,272,128]{2,1,0:T(8,128)(2,1)S(1)}, bf16[1,272,128]{2,1,0:T(8,128)(2,1)S(1)}, u32[]{:S(2)}, u32[]{:S(2)}) %collective-permute-start.28) | collective-permute-done | bytes 69664 | tf_op jit(solution)/shard_map/ppermute | solution.py:18
  84.2 0.7 convert.16
  85.0 0.7 join_out.1
  85.7 1.2 %copy.32 = bf16[2,6,13,13,128]{4,0,3,2,1:T(2,128)(2,1)} copy(bf16[2,6,13,13,128]{4,3,2,1,0:T(8,128)(2,1)S(1)} %bitcast.53) | data formatting | bytes 1038336
  86.9 2.6 %collective-permute-done.29 = bf16[1,320,128]{2,1,0:T(8,128)(2,1)S(1)} collective-permute-done((bf16[1,320,128]{2,1,0:T(8,128)(2,1)S(1)}, bf16[1,320,128]{2,1,0:T(8,128)(2,1)S(1)}, u32[]{:S(2)}, u32[]{:S(2)}) %collective-permute-start.29) | collective-permute-done | bytes 81952 | tf_op jit(solution)/shard_map/ppermute | solution.py:18
  89.5 0.7 convert.14
  (99 shorter events, 4.9 us)
Async XLA Ops:
  0.6 8.1 %copy-start = (s32[2,2]{1,0:T(2,128)S(1)}, s32[2,2]{1,0:T(2,128)}, u32[]{:S(2)}) copy-start(s32[2,2]{1,0:T(2,128)} %param.8) | copy-start | bytes 52
  2.0 7.6 %collective-permute-start = (bf16[3,208,128]{2,1,0:T(8,128)(2,1)S(1)}, bf16[3,208,128]{2,1,0:T(8,128)(2,1)S(1)}, u32[]{:S(2)}, u32[]{:S(2)}) collective-permute-start(bf16[3,208,128]{2,1,0:T(8,128)(2,1)S(1)} %constant_dynamic-slice_fusion.3), channel_id=1, source_target_pairs={{0,1},{1,0},{2,3},{3,2},{4,5},{5,4},{6,7},{7,6},{8,9},{9,8},{10,11... | collective-permute-start | bytes 479240 | tf_op jit(solution)/shard_map/ppermute | solution.py:18
  2.5 11.2 %collective-permute-start.1 = (bf16[2,3,208,128]{3,2,1,0:T(8,128)(2,1)S(1)}, bf16[2,3,208,128]{3,2,1,0:T(8,128)(2,1)S(1)}, u32[]{:S(2)}, u32[]{:S(2)}) collective-permute-start(bf16[2,3,208,128]{3,2,1,0:T(8,128)(2,1)S(1)} %bitcast.69), channel_id=1, source_target_pairs={{0,2},{1,3},{2,0},{3,1},{4,6},{5,7},{6,4},{7,5},{8,10},{9,11},{10,... | collective-permute-start | bytes 958472 | tf_op jit(solution)/shard_map/ppermute | solution.py:18
  5.1 11.3 %collective-permute-start.3 = (bf16[2,3,208,128]{3,2,1,0:T(8,128)(2,1)S(1)}, bf16[2,3,208,128]{3,2,1,0:T(8,128)(2,1)S(1)}, u32[]{:S(2)}, u32[]{:S(2)}) collective-permute-start(bf16[2,3,208,128]{3,2,1,0:T(8,128)(2,1)S(1)} %bitcast.50), channel_id=1, source_target_pairs={{0,8},{4,12},{8,0},{12,4},{16,24},{20,28},{24,16},{28,20},{1,9},{5... | collective-permute-start | bytes 958472 | tf_op jit(solution)/shard_map/ppermute | solution.py:18
  8.0 8.4 %copy-start.2 = (f32[512]{0:T(512)S(1)}, f32[512]{0:T(512)}, u32[]{:S(2)}) copy-start(f32[512]{0:T(512)} %param.10) | copy-start | bytes 6148
  8.1 13.2 %collective-permute-start.5 = (bf16[2,3,208,128]{3,2,1,0:T(8,128)(2,1)S(1)}, bf16[2,3,208,128]{3,2,1,0:T(8,128)(2,1)S(1)}, u32[]{:S(2)}, u32[]{:S(2)}) collective-permute-start(bf16[2,3,208,128]{3,2,1,0:T(8,128)(2,1)S(1)} %pad_maximum_fusion), channel_id=1, source_target_pairs={{0,2},{1,3},{2,0},{3,1},{4,6},{5,7},{6,4},{7,5},{8,10},{9,11},{10,... | collective-permute-start | bytes 958472 | tf_op jit(solution)/shard_map/ppermute | solution.py:18
  14.5 1.9 %collective-permute-start.2 = (bf16[3,208,128]{2,1,0:T(8,128)(2,1)S(1)}, bf16[3,208,128]{2,1,0:T(8,128)(2,1)S(1)}, u32[]{:S(2)}, u32[]{:S(2)}) collective-permute-start(bf16[3,208,128]{2,1,0:T(8,128)(2,1)S(1)} %pick.1), channel_id=1, source_target_pairs={{0,1},{1,0},{2,3},{3,2},{4,5},{5,4},{6,7},{7,6},{8,9},{9,8},{10,11... | collective-permute-start | bytes 479240 | tf_op jit(solution)/shard_map/ppermute | solution.py:18
  14.6 15.8 %collective-permute-start.11 = (bf16[2,3,208,128]{3,2,1,0:T(8,128)(2,1)S(1)}, bf16[2,3,208,128]{3,2,1,0:T(8,128)(2,1)S(1)}, u32[]{:S(2)}, u32[]{:S(2)}) collective-permute-start(bf16[2,3,208,128]{3,2,1,0:T(8,128)(2,1)S(1)} %after_part.1.refs_0_.refs_1_), channel_id=1, source_target_pairs={{0,8},{4,12},{8,0},{12,4},{16,24},{20,28},{24,16},{28,20},{1,9},{5... | collective-permute-start | bytes 958472 | tf_op jit(solution)/shard_map/ppermute | solution.py:18
  16.5 6.4 %copy-start.1 = (f32[512]{0:T(512)S(1)}, f32[512]{0:T(512)}, u32[]{:S(2)}) copy-start(f32[512]{0:T(512)} %param.12) | copy-start | bytes 6148
  19.7 23.4 %collective-permute-start.9 = (bf16[4,3,208,128]{3,2,1,0:T(8,128)(2,1)S(1)}, bf16[4,3,208,128]{3,2,1,0:T(8,128)(2,1)S(1)}, u32[]{:S(2)}, u32[]{:S(2)}) collective-permute-start(bf16[4,3,208,128]{3,2,1,0:T(8,128)(2,1)S(1)} %get-tuple-element.39.refs_0_), channel_id=1, source_target_pairs={{0,4},{4,0},{8,12},{12,8},{16,20},{20,16},{24,28},{28,24},{1,5},{5... | collective-permute-start | bytes 1916936 | tf_op jit(solution)/shard_map/ppermute | solution.py:18
  21.3 1.4 %collective-permute-start.4 = (bf16[3,208,128]{2,1,0:T(8,128)(2,1)S(1)}, bf16[3,208,128]{2,1,0:T(8,128)(2,1)S(1)}, u32[]{:S(2)}, u32[]{:S(2)}) collective-permute-start(bf16[3,208,128]{2,1,0:T(8,128)(2,1)S(1)} %get-tuple-element.82.refs_4_), channel_id=1, source_target_pairs={{0,1},{1,0},{2,3},{3,2},{4,5},{5,4},{6,7},{7,6},{8,9},{9,8},{10,11... | collective-permute-start | bytes 479240 | tf_op jit(solution)/shard_map/ppermute | solution.py:18
  21.3 1.6 %collective-permute-start.6 = (bf16[1,3,208,128]{3,2,1,0:T(8,128)(2,1)S(1)}, bf16[1,3,208,128]{3,2,1,0:T(8,128)(2,1)S(1)}, u32[]{:S(2)}, u32[]{:S(2)}) collective-permute-start(bf16[1,3,208,128]{3,2,1,0:T(8,128)(2,1)S(1)} %slice.110), channel_id=1, source_target_pairs={{0,1},{1,0},{2,3},{3,2},{4,5},{5,4},{6,7},{7,6},{8,9},{9,8},{10,11... | collective-permute-start | bytes 479240 | tf_op jit(solution)/shard_map/ppermute | solution.py:18
  21.9 9.0 %collective-permute-start.7 = (bf16[2,3,208,128]{3,2,1,0:T(8,128)(2,1)S(1)}, bf16[2,3,208,128]{3,2,1,0:T(8,128)(2,1)S(1)}, u32[]{:S(2)}, u32[]{:S(2)}) collective-permute-start(bf16[2,3,208,128]{3,2,1,0:T(8,128)(2,1)S(1)} %slice.86), channel_id=1, source_target_pairs={{0,1},{1,0},{2,3},{3,2},{4,5},{5,4},{6,7},{7,6},{8,9},{9,8},{10,11... | collective-permute-start | bytes 958472 | tf_op jit(solution)/shard_map/ppermute | solution.py:18
  28.5 7.1 %collective-permute-start.12 = (bf16[3,208,256]{2,1,0:T(8,128)(2,1)S(1)}, bf16[3,208,256]{2,1,0:T(8,128)(2,1)S(1)}, u32[]{:S(2)}, u32[]{:S(2)}) collective-permute-start(bf16[3,208,256]{2,1,0:T(8,128)(2,1)S(1)} %get-tuple-element.49.refs_4_), channel_id=1, source_target_pairs={{0,1},{1,0},{2,3},{3,2},{4,5},{5,4},{6,7},{7,6},{8,9},{9,8},{10,11... | collective-permute-start | bytes 958472 | tf_op jit(solution)/shard_map/ppermute | solution.py:18
  28.9 12.7 %collective-permute-start.10 = (bf16[2,3,208,128]{3,2,1,0:T(8,128)(2,1)S(1)}, bf16[2,3,208,128]{3,2,1,0:T(8,128)(2,1)S(1)}, u32[]{:S(2)}, u32[]{:S(2)}) collective-permute-start(bf16[2,3,208,128]{3,2,1,0:T(8,128)(2,1)S(1)} %get-tuple-element.45), channel_id=1, source_target_pairs={{0,2},{1,3},{2,0},{3,1},{4,6},{5,7},{6,4},{7,5},{8,10},{9,11},{10,... | collective-permute-start | bytes 958472 | tf_op jit(solution)/shard_map/ppermute | solution.py:18
  30.4 12.6 %collective-permute-start.8 = (bf16[3,208,256]{2,1,0:T(8,128)(2,1)S(1)}, bf16[3,208,256]{2,1,0:T(8,128)(2,1)S(1)}, u32[]{:S(2)}, u32[]{:S(2)}) collective-permute-start(bf16[3,208,256]{2,1,0:T(8,128)(2,1)S(1)} %get-tuple-element.44), channel_id=1, source_target_pairs={{0,4},{4,0},{8,12},{12,8},{16,20},{20,16},{24,28},{28,24},{1,5},{5... | collective-permute-start | bytes 958472 | tf_op jit(solution)/shard_map/ppermute | solution.py:18
  35.5 8.2 %collective-permute-start.16 = (bf16[3,208,256]{2,1,0:T(8,128)(2,1)S(1)}, bf16[3,208,256]{2,1,0:T(8,128)(2,1)S(1)}, u32[]{:S(2)}, u32[]{:S(2)}) collective-permute-start(bf16[3,208,256]{2,1,0:T(8,128)(2,1)S(1)} %get-tuple-element.54.refs_4_), channel_id=1, source_target_pairs={{0,1},{1,0},{2,3},{3,2},{4,5},{5,4},{6,7},{7,6},{8,9},{9,8},{10,11... | collective-permute-start | bytes 958472 | tf_op jit(solution)/shard_map/ppermute | solution.py:18
  35.6 14.2 %collective-permute-start.17 = (bf16[3,208,256]{2,1,0:T(8,128)(2,1)S(1)}, bf16[3,208,256]{2,1,0:T(8,128)(2,1)S(1)}, u32[]{:S(2)}, u32[]{:S(2)}) collective-permute-start(bf16[3,208,256]{2,1,0:T(8,128)(2,1)S(1)} %get-tuple-element.56), channel_id=1, source_target_pairs={{0,8},{4,12},{8,0},{12,4},{16,24},{20,28},{24,16},{28,20},{1,9},{5... | collective-permute-start | bytes 958472 | tf_op jit(solution)/shard_map/ppermute | solution.py:18
  41.6 9.7 %collective-permute-start.18 = (bf16[2,3,208,128]{3,2,1,0:T(8,128)(2,1)S(1)}, bf16[2,3,208,128]{3,2,1,0:T(8,128)(2,1)S(1)}, u32[]{:S(2)}, u32[]{:S(2)}) collective-permute-start(bf16[2,3,208,128]{3,2,1,0:T(8,128)(2,1)S(1)} %get-tuple-element.58), channel_id=1, source_target_pairs={{0,2},{1,3},{2,0},{3,1},{4,6},{5,7},{6,4},{7,5},{8,10},{9,11},{10,... | collective-permute-start | bytes 958472 | tf_op jit(solution)/shard_map/ppermute | solution.py:18
  43.1 2.4 %collective-permute-start.13 = (bf16[2,3,208,128]{3,2,1,0:T(8,128)(2,1)S(1)}, bf16[2,3,208,128]{3,2,1,0:T(8,128)(2,1)S(1)}, u32[]{:S(2)}, u32[]{:S(2)}) collective-permute-start(bf16[2,3,208,128]{3,2,1,0:T(8,128)(2,1)S(1)} %slice.87), channel_id=1, source_target_pairs={{0,1},{1,0},{2,3},{3,2},{4,5},{5,4},{6,7},{7,6},{8,9},{9,8},{10,11... | collective-permute-start | bytes 958472 | tf_op jit(solution)/shard_map/ppermute | solution.py:18
  43.2 2.3 %collective-permute-start.14 = (bf16[3,208,256]{2,1,0:T(8,128)(2,1)S(1)}, bf16[3,208,256]{2,1,0:T(8,128)(2,1)S(1)}, u32[]{:S(2)}, u32[]{:S(2)}) collective-permute-start(bf16[3,208,256]{2,1,0:T(8,128)(2,1)S(1)} %get-tuple-element.52.refs_6_), channel_id=1, source_target_pairs={{0,1},{1,0},{2,3},{3,2},{4,5},{5,4},{6,7},{7,6},{8,9},{9,8},{10,11... | collective-permute-start | bytes 958472 | tf_op jit(solution)/shard_map/ppermute | solution.py:18
  43.7 1.8 %collective-permute-start.15 = (bf16[3,208,128]{2,1,0:T(8,128)(2,1)S(1)}, bf16[3,208,128]{2,1,0:T(8,128)(2,1)S(1)}, u32[]{:S(2)}, u32[]{:S(2)}) collective-permute-start(bf16[3,208,128]{2,1,0:T(8,128)(2,1)S(1)} %slice_bitcast_fusion.1), channel_id=1, source_target_pairs={{0,1},{1,0},{2,3},{3,2},{4,5},{5,4},{6,7},{7,6},{8,9},{9,8},{10,11... | collective-permute-start | bytes 479240 | tf_op jit(solution)/shard_map/ppermute | solution.py:18
  51.3 1.6 %collective-permute-start.19 = (bf16[3,208,256]{2,1,0:T(8,128)(2,1)S(1)}, bf16[3,208,256]{2,1,0:T(8,128)(2,1)S(1)}, u32[]{:S(2)}, u32[]{:S(2)}) collective-permute-start(bf16[3,208,256]{2,1,0:T(8,128)(2,1)S(1)} %after_grad5.1.refs_6_), channel_id=1, source_target_pairs={{0,1},{1,0},{2,3},{3,2},{4,5},{5,4},{6,7},{7,6},{8,9},{9,8},{10,11... | collective-permute-start | bytes 958472 | tf_op jit(solution)/shard_map/ppermute | solution.py:18
  51.3 9.3 %collective-permute-start.30 = (bf16[4,272,128]{2,1,0:T(8,128)(2,1)S(1)}, bf16[4,272,128]{2,1,0:T(8,128)(2,1)S(1)}, u32[]{:S(2)}, u32[]{:S(2)}) collective-permute-start(bf16[4,272,128]{2,1,0:T(8,128)(2,1)S(1)} %get-tuple-element.67), channel_id=1, source_target_pairs={{0,2},{1,3},{2,0},{3,1},{4,6},{5,7},{6,4},{7,5},{8,10},{9,11},{10,... | collective-permute-start | bytes 835592 | tf_op jit(solution)/shard_map/ppermute | solution.py:18
  51.8 11.2 %collective-permute-start.20 = (bf16[4,320,128]{2,1,0:T(8,128)(2,1)S(1)}, bf16[4,320,128]{2,1,0:T(8,128)(2,1)S(1)}, u32[]{:S(2)}, u32[]{:S(2)}) collective-permute-start(bf16[4,320,128]{2,1,0:T(8,128)(2,1)S(1)} %get-tuple-element.60), channel_id=1, source_target_pairs={{0,8},{4,12},{8,0},{12,4},{16,24},{20,28},{24,16},{28,20},{1,9},{5... | collective-permute-start | bytes 983048 | tf_op jit(solution)/shard_map/ppermute | solution.py:18
  57.2 9.6 %collective-permute-start.24 = (bf16[4,272,128]{2,1,0:T(8,128)(2,1)S(1)}, bf16[4,272,128]{2,1,0:T(8,128)(2,1)S(1)}, u32[]{:S(2)}, u32[]{:S(2)}) collective-permute-start(bf16[4,272,128]{2,1,0:T(8,128)(2,1)S(1)} %get-tuple-element.64), channel_id=1, source_target_pairs={{0,2},{1,3},{2,0},{3,1},{4,6},{5,7},{6,4},{7,5},{8,10},{9,11},{10,... | collective-permute-start | bytes 835592 | tf_op jit(solution)/shard_map/ppermute | solution.py:18
  60.7 6.2 %collective-permute-start.31 = (bf16[2,272,128]{2,1,0:T(8,128)(2,1)S(1)}, bf16[2,272,128]{2,1,0:T(8,128)(2,1)S(1)}, u32[]{:S(2)}, u32[]{:S(2)}) collective-permute-start(bf16[2,272,128]{2,1,0:T(8,128)(2,1)S(1)} %get-tuple-element.88), channel_id=1, source_target_pairs={{0,8},{4,12},{8,0},{12,4},{16,24},{20,28},{24,16},{28,20},{1,9},{5... | collective-permute-start | bytes 417800 | tf_op jit(solution)/shard_map/ppermute | solution.py:18
  61.4 9.7 %collective-permute-start.22 = (bf16[4,320,128]{2,1,0:T(8,128)(2,1)S(1)}, bf16[4,320,128]{2,1,0:T(8,128)(2,1)S(1)}, u32[]{:S(2)}, u32[]{:S(2)}) collective-permute-start(bf16[4,320,128]{2,1,0:T(8,128)(2,1)S(1)} %get-tuple-element.62), channel_id=1, source_target_pairs={{0,4},{4,0},{8,12},{12,8},{16,20},{20,16},{24,28},{28,24},{1,5},{5... | collective-permute-start | bytes 983048 | tf_op jit(solution)/shard_map/ppermute | solution.py:18
  63.1 8.2 %collective-permute-start.33 = (bf16[2,320,128]{2,1,0:T(8,128)(2,1)S(1)}, bf16[2,320,128]{2,1,0:T(8,128)(2,1)S(1)}, u32[]{:S(2)}, u32[]{:S(2)}) collective-permute-start(bf16[2,320,128]{2,1,0:T(8,128)(2,1)S(1)} %get-tuple-element.86), channel_id=1, source_target_pairs={{0,2},{1,3},{2,0},{3,1},{4,6},{5,7},{6,4},{7,5},{8,10},{9,11},{10,... | collective-permute-start | bytes 491528 | tf_op jit(solution)/shard_map/ppermute | solution.py:18
  63.6 21.3 %collective-permute-start.21 = (bf16[3,208,128]{2,1,0:T(8,128)(2,1)S(1)}, bf16[3,208,128]{2,1,0:T(8,128)(2,1)S(1)}, u32[]{:S(2)}, u32[]{:S(2)}) collective-permute-start(bf16[3,208,128]{2,1,0:T(8,128)(2,1)S(1)} %after_step.6), channel_id=1, source_target_pairs={{0,1},{1,0},{2,3},{3,2},{4,5},{5,4},{6,7},{7,6},{8,9},{9,8},{10,11... | collective-permute-start | bytes 479240 | tf_op jit(solution)/shard_map/ppermute | solution.py:18
  67.0 16.5 %collective-permute-start.32 = (bf16[1,272,128]{2,1,0:T(8,128)(2,1)S(1)}, bf16[1,272,128]{2,1,0:T(8,128)(2,1)S(1)}, u32[]{:S(2)}, u32[]{:S(2)}) collective-permute-start(bf16[1,272,128]{2,1,0:T(8,128)(2,1)S(1)} %get-tuple-element.92), channel_id=1, source_target_pairs={{0,16},{4,20},{8,24},{12,28},{16,0},{20,4},{24,8},{28,12},{1,17},{... | collective-permute-start | bytes 208904 | tf_op jit(solution)/shard_map/ppermute | solution.py:18
  69.6 5.1 %collective-permute-start.27 = (bf16[2,272,128]{2,1,0:T(8,128)(2,1)S(1)}, bf16[2,272,128]{2,1,0:T(8,128)(2,1)S(1)}, u32[]{:S(2)}, u32[]{:S(2)}) collective-permute-start(bf16[2,272,128]{2,1,0:T(8,128)(2,1)S(1)} %slice.114), channel_id=1, source_target_pairs={{0,4},{4,0},{8,12},{12,8},{16,20},{20,16},{24,28},{28,24},{1,5},{5... | collective-permute-start | bytes 417800 | tf_op jit(solution)/shard_map/ppermute | solution.py:18
  71.1 4.9 %collective-permute-start.26 = (bf16[3,208,128]{2,1,0:T(8,128)(2,1)S(1)}, bf16[3,208,128]{2,1,0:T(8,128)(2,1)S(1)}, u32[]{:S(2)}, u32[]{:S(2)}) collective-permute-start(bf16[3,208,128]{2,1,0:T(8,128)(2,1)S(1)} %slice_bitcast_fusion), channel_id=1, source_target_pairs={{0,1},{1,0},{2,3},{3,2},{4,5},{5,4},{6,7},{7,6},{8,9},{9,8},{10,11... | collective-permute-start | bytes 479240 | tf_op jit(solution)/shard_map/ppermute | solution.py:18
  71.3 5.3 %collective-permute-start.25 = (bf16[3,208,128]{2,1,0:T(8,128)(2,1)S(1)}, bf16[3,208,128]{2,1,0:T(8,128)(2,1)S(1)}, u32[]{:S(2)}, u32[]{:S(2)}) collective-permute-start(bf16[3,208,128]{2,1,0:T(8,128)(2,1)S(1)} %get-tuple-element.65), channel_id=1, source_target_pairs={{0,1},{1,0},{2,3},{3,2},{4,5},{5,4},{6,7},{7,6},{8,9},{9,8},{10,11... | collective-permute-start | bytes 479240 | tf_op jit(solution)/shard_map/ppermute | solution.py:18
  74.7 8.2 %collective-permute-start.28 = (bf16[1,272,128]{2,1,0:T(8,128)(2,1)S(1)}, bf16[1,272,128]{2,1,0:T(8,128)(2,1)S(1)}, u32[]{:S(2)}, u32[]{:S(2)}) collective-permute-start(bf16[1,272,128]{2,1,0:T(8,128)(2,1)S(1)} %slice.116), channel_id=1, source_target_pairs={{0,16},{4,20},{8,24},{12,28},{16,0},{20,4},{24,8},{28,12},{1,17},{... | collective-permute-start | bytes 208904 | tf_op jit(solution)/shard_map/ppermute | solution.py:18
  76.0 7.5 %collective-permute-start.23 = (bf16[2,320,128]{2,1,0:T(8,128)(2,1)S(1)}, bf16[2,320,128]{2,1,0:T(8,128)(2,1)S(1)}, u32[]{:S(2)}, u32[]{:S(2)}) collective-permute-start(bf16[2,320,128]{2,1,0:T(8,128)(2,1)S(1)} %slice.112), channel_id=1, source_target_pairs={{0,2},{1,3},{2,0},{3,1},{4,6},{5,7},{6,4},{7,5},{8,10},{9,11},{10,... | collective-permute-start | bytes 491528 | tf_op jit(solution)/shard_map/ppermute | solution.py:18
  76.6 7.6 %collective-permute-start.34 = (bf16[1,320,128]{2,1,0:T(8,128)(2,1)S(1)}, bf16[1,320,128]{2,1,0:T(8,128)(2,1)S(1)}, u32[]{:S(2)}, u32[]{:S(2)}) collective-permute-start(bf16[1,320,128]{2,1,0:T(8,128)(2,1)S(1)} %get-tuple-element.90), channel_id=1, source_target_pairs={{0,16},{4,20},{8,24},{12,28},{16,0},{20,4},{24,8},{28,12},{1,17},{... | collective-permute-start | bytes 245768 | tf_op jit(solution)/shard_map/ppermute | solution.py:18
  84.1 5.4 %collective-permute-start.29 = (bf16[1,320,128]{2,1,0:T(8,128)(2,1)S(1)}, bf16[1,320,128]{2,1,0:T(8,128)(2,1)S(1)}, u32[]{:S(2)}, u32[]{:S(2)}) collective-permute-start(bf16[1,320,128]{2,1,0:T(8,128)(2,1)S(1)} %slice.119), channel_id=1, source_target_pairs={{0,16},{4,20},{8,24},{12,28},{16,0},{20,4},{24,8},{28,12},{1,17},{... | collective-permute-start | bytes 245768 | tf_op jit(solution)/shard_map/ppermute | solution.py:18

commit v4 on v3

--- a/solution.py
+++ b/solution.py
@@ -586,6 +586,7 @@
     out_far = over_x(outs[2])
     hidden_core = over_core(hidden[2:])
 
+    out1_core = over_core(outs[1])
 
     kept5_core, across5 = over_core(kept5), over_y(sent5)
 
@@ -620,9 +621,9 @@
 
     hidden_both, across5_core = over_core(hidden_y[2:]), over_core(across5)
 
-    chunks5 = (("xab", 0, 4), ("axb", 4, 5))
+    chunks5 = (("axb", 0, 5), ("xab", 5, 4))
     own, other = 0, 1
-    chunks4 = (("xyb", 0, 4), ("yxb", 4, 5))
+    chunks4 = (("yxb", 0, 5), ("xyb", 5, 4))
     blocks5 = kernel_grad(
         "grad5",
         chunks5,
@@ -630,9 +631,9 @@
         False,
         (hidden, hidden_core, hidden_y, hidden_both),
         (kept5, kept5_core, across5, across5_core),
-        [out3, kept4_core, backs[0]],
+        [out1_core, out3, kept4_core, backs[0]],
     )
-    (across4,) = held("after_grad5", [across4], [blocks5[0], back_far])
+    (across4,) = held("after_grad5", [across4], [blocks5[0]])
     across4_core = over_core(across4)
     blocks4 = kernel_grad(
         "grad4",
@@ -641,7 +642,7 @@
         True,
         (near, far, near_a, far_a),
         (kept4, kept4_core, across4, across4_core),
-        [blocks5[0]],
+        [blocks5[0], back_far],
     )
 
     kept5, moved5 = sends(blocks5, chunks5)
@@ -657,8 +658,6 @@
     b5_1 = halved(b5_0, chunks5[1], 1, [b4_0])
     a5_2 = halved(a5_1, chunks5[0], 2, [b4_1])
     b5_2 = halved(b5_1, chunks5[1], 2, [b4_1])
-    out1, = held("after_step", [outs[1]], [b5_0])
-    out1_core = over_core(out1)
 
 
     back1, back_far = held("after_step", [backs[1], back_far], [a4_0])

time: 90.4 us -> 89.7 us (level)
  waiting for transfers between devices: 17.8 us -> 13.3 us
  starting transfers between devices: 29.2 us -> 32.9 us
    ppermute x35, waiting for transfers between devices: 17.8 us -> 13.3 us  [swap(): return lax.ppermute(value, axis_name, [(i, i ^ bit) for i in range(size)])]
    ppermute x35, starting transfers between devices: 29.2 us -> 32.9 us  [swap(): return lax.ppermute(value, axis_name, [(i, i ^ bit) for i in range(size)])]
  transfers between devices with their start and end apart: 35 -> 35, of which waited for: 11 -> 9; matrix products, arithmetic and copies ran while one was open for 8% -> 7% of each run, Pallas kernels for 36% -> 37%
where the time goes in v4:
time: 89.7 us; the launch traced here: 89.5 us
  starting transfers between devices  32.9 us (37%)
  Pallas kernels  32.9 us (37%)
  waiting for transfers between devices  13.3 us (15%)
  local copies, waits for them, and re-layouts  5.89 us (7%)
  other arithmetic  3.33 us (4%)
  between operations  1.14 us (1%)
    pallas_call x10, Pallas kernels, call(): return lambda *args: called(info, *args, *after)  32.9 us
    ppermute x35, starting transfers between devices, swap(): return lax.ppermute(value, axis_name, [(i, i ^ bit) for i in range(size)])  32.9 us
    ppermute x35, waiting for transfers between devices, swap(): return lax.ppermute(value, axis_name, [(i, i ^ bit) for i in range(size)])  13.3 us
    unnamed x10, local copies, waits for them, and re-layouts  4.69 us
  transfers between devices with their start and end apart: 35, of which 9 were waited for; matrix products, arithmetic and copies ran while one was open for 7% of the time, Pallas kernels for 37%

profile of v4, /device:TPU:0, one launch (start us, length us, event | category | flops | bytes accessed | tf_op | source)
XLA Modules:
  0.0 89.5 jit_solution(7541223603976003534)
XLA Ops:
  0.7 1.1 %copy.29 = bf16[2,6,13,13,128]{4,3,2,1,0:T(8,128)(2,1)S(1)} copy(bf16[2,6,13,13,128]{4,0,3,2,1:T(2,128)(2,1)} %param.7) | data formatting | bytes 1038336 | tf_op args[0]
  2.0 0.5 collective-permute-start
  2.5 2.6 %collective-permute-start.1 = (bf16[2,3,208,128]{3,2,1,0:T(8,128)(2,1)S(1)}, bf16[2,3,208,128]{3,2,1,0:T(8,128)(2,1)S(1)}, u32[]{:S(2)}, u32[]{:S(2)}) collective-permute-start(bf16[2,3,208,128]{3,2,1,0:T(8,128)(2,1)S(1)} %bitcast.69), channel_id=1, source_target_pairs={{0,2},{1,3},{2,0},{3,1},{4,6},{5,7},{6,4},{7,5},{8,10},{9,11},{10,... | collective-permute-start | bytes 958472 | tf_op jit(solution)/shard_map/ppermute | solution.py:18
  5.1 1.6 %collective-permute-start.3 = (bf16[2,3,208,128]{3,2,1,0:T(8,128)(2,1)S(1)}, bf16[2,3,208,128]{3,2,1,0:T(8,128)(2,1)S(1)}, u32[]{:S(2)}, u32[]{:S(2)}) collective-permute-start(bf16[2,3,208,128]{3,2,1,0:T(8,128)(2,1)S(1)} %bitcast.50), channel_id=1, source_target_pairs={{0,8},{4,12},{8,0},{12,4},{16,24},{20,28},{24,16},{28,20},{1,9},{5... | collective-permute-start | bytes 958472 | tf_op jit(solution)/shard_map/ppermute | solution.py:18
  6.7 1.1 %copy.30 = bf16[2,6,13,13,128]{4,3,2,1,0:T(8,128)(2,1)S(1)} copy(bf16[2,6,13,13,128]{4,0,3,2,1:T(2,128)(2,1)} %param.13) | data formatting | bytes 1038336 | tf_op args[6]
  8.1 0.6 collective-permute-start.5
  8.8 0.6 gather_fusion
  9.6 4.2 %conv4_part.1 = (f32[2,624,256]{2,1,0:T(8,128)S(1)}, bf16[9,256,512]{2,1,0:T(8,128)(2,1)S(1)}) custom-call(s32[5]{0:T(128)S(1)} %pad_add_fusion.info, bf16[2,3,208,128]{3,2,1,0:T(8,128)(2,1)S(1)} %bitcast.51, bf16[3,208,128]{2,1,0:T(8,128)(2,1)S(1)} %collective-permute-done.refs_1_, bf16[9,512,512]{2,1,0:T(8,128)(2,1)} %bitcast.57, ...), custom_call_target="tpu_custom_call" | custom-call | tf_op jit(solution)/shard_map/conv4_part/pallas_call | solution.py:446
  13.8 0.8 pick.1
  14.6 1.8 %collective-permute-start.11 = (bf16[2,3,208,128]{3,2,1,0:T(8,128)(2,1)S(1)}, bf16[2,3,208,128]{3,2,1,0:T(8,128)(2,1)S(1)}, u32[]{:S(2)}, u32[]{:S(2)}) collective-permute-start(bf16[2,3,208,128]{3,2,1,0:T(8,128)(2,1)S(1)} %after_part.1.refs_0_.refs_1_), channel_id=1, source_target_pairs={{0,8},{4,12},{8,0},{12,4},{16,24},{20,28},{24,16},{28,20},{1,9},{5... | collective-permute-start | bytes 958472 | tf_op jit(solution)/shard_map/ppermute | solution.py:18
  16.5 3.2 %conv4.1 = (bf16[4,3,208,128]{3,2,1,0:T(8,128)(2,1)S(1)}, f32[2,624,256]{2,1,0:T(8,128)S(1)}, bf16[9,512,512]{2,1,0:T(8,128)(2,1)S(1)}) custom-call(s32[5]{0:T(128)S(1)} %pad_add_fusion.info, f32[2,624,256]{2,1,0:T(8,128)S(1)} %get-tuple-element.37.refs_1_.refs_0_, bf16[2,3,208,128]{3,2,1,0:T(8,128)(2,1)S(1)} %after_part.1.refs_0_.refs_1_, ...), custom_call_target="tpu_custom_call" | custom-call | tf_op jit(solution)/shard_map/conv4/pallas_call | solution.py:446
  19.7 1.6 %collective-permute-start.9 = (bf16[4,3,208,128]{3,2,1,0:T(8,128)(2,1)S(1)}, bf16[4,3,208,128]{3,2,1,0:T(8,128)(2,1)S(1)}, u32[]{:S(2)}, u32[]{:S(2)}) collective-permute-start(bf16[4,3,208,128]{3,2,1,0:T(8,128)(2,1)S(1)} %get-tuple-element.39.refs_0_), channel_id=1, source_target_pairs={{0,4},{4,0},{8,12},{12,8},{16,20},{20,16},{24,28},{28,24},{1,5},{5... | collective-permute-start | bytes 1916936 | tf_op jit(solution)/shard_map/ppermute | solution.py:18
  21.3 0.6 collective-permute-start.6
  22.0 0.7 collective-permute-done.4.refs_2_
  22.9 5.6 %conv5.1 = (bf16[3,208,128]{2,1,0:T(8,128)(2,1)S(1)}, bf16[3,208,128]{2,1,0:T(8,128)(2,1)S(1)}, bf16[2,3,208,128]{3,2,1,0:T(8,128)(2,1)S(1)}, bf16[3,208,512]{2,...) custom-call(s32[5]{0:T(128)S(1)} %pad_add_fusion.info, ...), custom_call_target="tpu_custom_call" | custom-call | tf_op jit(solution)/shard_map/conv5/pallas_call | solution.py:446
  28.9 1.5 %collective-permute-start.10 = (bf16[2,3,208,128]{3,2,1,0:T(8,128)(2,1)S(1)}, bf16[2,3,208,128]{3,2,1,0:T(8,128)(2,1)S(1)}, u32[]{:S(2)}, u32[]{:S(2)}) collective-permute-start(bf16[2,3,208,128]{3,2,1,0:T(8,128)(2,1)S(1)} %get-tuple-element.45), channel_id=1, source_target_pairs={{0,2},{1,3},{2,0},{3,1},{4,6},{5,7},{6,4},{7,5},{8,10},{9,11},{10,... | collective-permute-start | bytes 958472 | tf_op jit(solution)/shard_map/ppermute | solution.py:18
  30.4 0.5 collective-permute-start.8
  30.9 4.5 %back5.1 = (bf16[3,208,512]{2,1,0:T(8,128)(2,1)S(1)}, bf16[3,208,256]{2,1,0:T(8,128)(2,1)S(1)}, bf16[3,208,256]{2,1,0:T(8,128)(2,1)S(1)}, bf16[9,512,512]{2,1,0:T(8,128)(2,1)S(1)}) custom-call(s32[5]{0:T(128)S(1)} %pad_add_fusion.info, bf16[3,208,512]{2,1,0:T(8,128)(2,1)S(1)} %get-tuple-element.46.refs_0_, f32[2,624,256]{2,1,0:T(8,128)S(1)} %get-tuple-element.40.refs_1_, ...), custom_call_target="tpu_custom_call" | custom-call | tf_op jit(solution)/shard_map/back5/pallas_call | solution.py:446
  35.5 0.6 collective-permute-start.15
  36.1 4.6 %back4.1 = (bf16[3,208,128]{2,1,0:T(8,128)(2,1)S(1)}, bf16[3,208,128]{2,1,0:T(8,128)(2,1)S(1)}, bf16[2,3,208,128]{3,2,1,0:T(8,128)(2,1)S(1)}) custom-call(s32[5]{0:T(128)S(1)} %pad_add_fusion.info, bf16[3,208,512]{2,1,0:T(8,128)(2,1)S(1)} %get-tuple-element.47.refs_0_, bf16[9,512,512]{2,1,0:T(8,128)(2,1)S(1)} %get-tuple-element.48.refs_1_, ...), custom_call_target="tpu_custom_call" | custom-call | flops 1472200704 | tf_op jit(solution)/shard_map/back4/pallas_call | solution.py:446
  40.7 1.4 %collective-permute-start.16 = (bf16[3,208,256]{2,1,0:T(8,128)(2,1)S(1)}, bf16[3,208,256]{2,1,0:T(8,128)(2,1)S(1)}, u32[]{:S(2)}, u32[]{:S(2)}) collective-permute-start(bf16[3,208,256]{2,1,0:T(8,128)(2,1)S(1)} %get-tuple-element.53), channel_id=1, source_target_pairs={{0,8},{4,12},{8,0},{12,4},{16,24},{20,28},{24,16},{28,20},{1,9},{5... | collective-permute-start | bytes 958472 | tf_op jit(solution)/shard_map/ppermute | solution.py:18
  42.1 1.0 %collective-permute-done.8.refs_0_ = bf16[3,208,256]{2,1,0:T(8,128)(2,1)S(1)} collective-permute-done((bf16[3,208,256]{2,1,0:T(8,128)(2,1)S(1)}, bf16[3,208,256]{2,1,0:T(8,128)(2,1)S(1)}, u32[]{:S(2)}, u32[]{:S(2)}) %collective-permute-start.8) | collective-permute-done | bytes 319520 | tf_op jit(solution)/shard_map/ppermute | solution.py:18
  43.8 1.5 %collective-permute-start.20 = (bf16[2,3,208,128]{3,2,1,0:T(8,128)(2,1)S(1)}, bf16[2,3,208,128]{3,2,1,0:T(8,128)(2,1)S(1)}, u32[]{:S(2)}, u32[]{:S(2)}) collective-permute-start(bf16[2,3,208,128]{3,2,1,0:T(8,128)(2,1)S(1)} %get-tuple-element.57), channel_id=1, source_target_pairs={{0,2},{1,3},{2,0},{3,1},{4,6},{5,7},{6,4},{7,5},{8,10},{9,11},{10,... | collective-permute-start | bytes 958472 | tf_op jit(solution)/shard_map/ppermute | solution.py:18
  45.5 4.3 %grad5.1 = (bf16[4,336,128]{2,1,0:T(8,128)(2,1)S(1)}, bf16[4,336,128]{2,1,0:T(8,128)(2,1)S(1)}, bf16[4,256,128]{2,1,0:T(8,128)(2,1)S(1)}, bf16[4,256,128]{2,1,0:T(8,128)(2,1)S(1)}) custom-call(s32[5]{0:T(128)S(1)} %pad_add_fusion.info, bf16[4,3,208,128]{3,2,1,0:T(8,128)(2,1)S(1)} %get-tuple-element.39.refs_0_, ...), custom_call_target="tpu_custom_call" | custom-call | tf_op jit(solution)/shard_map/grad5/pallas_call | solution.py:446
  50.2 1.3 %collective-permute-start.32 = (bf16[4,256,128]{2,1,0:T(8,128)(2,1)S(1)}, bf16[4,256,128]{2,1,0:T(8,128)(2,1)S(1)}, u32[]{:S(2)}, u32[]{:S(2)}) collective-permute-start(bf16[4,256,128]{2,1,0:T(8,128)(2,1)S(1)} %get-tuple-element.67), channel_id=1, source_target_pairs={{0,2},{1,3},{2,0},{3,1},{4,6},{5,7},{6,4},{7,5},{8,10},{9,11},{10,... | collective-permute-start | bytes 786440 | tf_op jit(solution)/shard_map/ppermute | solution.py:18
  51.5 1.3 %collective-permute-start.29 = (bf16[4,336,128]{2,1,0:T(8,128)(2,1)S(1)}, bf16[4,336,128]{2,1,0:T(8,128)(2,1)S(1)}, u32[]{:S(2)}, u32[]{:S(2)}) collective-permute-start(bf16[4,336,128]{2,1,0:T(8,128)(2,1)S(1)} %get-tuple-element.65), channel_id=1, source_target_pairs={{0,8},{4,12},{8,0},{12,4},{16,24},{20,28},{24,16},{28,20},{1,9},{5... | collective-permute-start | bytes 1032200 | tf_op jit(solution)/shard_map/ppermute | solution.py:18
  52.8 1.3 %collective-permute-done.20.refs_9_.refs_1_ = bf16[2,3,208,128]{3,2,1,0:T(8,128)(2,1)S(1)} collective-permute-done((bf16[2,3,208,128]{3,2,1,0:T(8,128)(2,1)S(1)}, bf16[2,3,208,128]{3,2,1,0:T(8,128)(2,1)S(1)}, u32[]{:S(2)}, u32[]{:S(2)}) %collective-permute-start.20) | collective-permute-done | bytes 319520 | tf_op jit(solution)/shard_map/ppermute | solution.py:18
  54.1 4.3 %grad4.1 = (bf16[4,336,128]{2,1,0:T(8,128)(2,1)S(1)}, bf16[4,336,128]{2,1,0:T(8,128)(2,1)S(1)}, bf16[4,256,128]{2,1,0:T(8,128)(2,1)S(1)}, bf16[4,256,128]{2,1,0:T(8,128)(2,1)S(1)}) custom-call(s32[5]{0:T(128)S(1)} %pad_add_fusion.info, bf16[2,3,208,128]{3,2,1,0:T(8,128)(2,1)S(1)} %bitcast.52, bf16[2,3,208,128]{3,2,1,0:T(8,128)(2,1)S(1)} %after_part.1.refs_0_.refs_1_, ...), custom_call_target="tpu_custom_call" | custom-call | tf_op jit(solution)/shard_map/grad4/pallas_call | solution.py:446
  58.4 1.6 %collective-permute-start.23 = (bf16[4,336,128]{2,1,0:T(8,128)(2,1)S(1)}, bf16[4,336,128]{2,1,0:T(8,128)(2,1)S(1)}, u32[]{:S(2)}, u32[]{:S(2)}) collective-permute-start(bf16[4,336,128]{2,1,0:T(8,128)(2,1)S(1)} %get-tuple-element.62), channel_id=1, source_target_pairs={{0,4},{4,0},{8,12},{12,8},{16,20},{20,16},{24,28},{28,24},{1,5},{5... | collective-permute-start | bytes 1032200 | tf_op jit(solution)/shard_map/ppermute | solution.py:18
  60.0 1.6 %collective-permute-start.21 = (bf16[4,256,128]{2,1,0:T(8,128)(2,1)S(1)}, bf16[4,256,128]{2,1,0:T(8,128)(2,1)S(1)}, u32[]{:S(2)}, u32[]{:S(2)}) collective-permute-start(bf16[4,256,128]{2,1,0:T(8,128)(2,1)S(1)} %get-tuple-element.59), channel_id=1, source_target_pairs={{0,2},{1,3},{2,0},{3,1},{4,6},{5,7},{6,4},{7,5},{8,10},{9,11},{10,... | collective-permute-start | bytes 786440 | tf_op jit(solution)/shard_map/ppermute | solution.py:18
  61.7 1.3 %collective-permute-start.33 = (bf16[2,256,128]{2,1,0:T(8,128)(2,1)S(1)}, bf16[2,256,128]{2,1,0:T(8,128)(2,1)S(1)}, u32[]{:S(2)}, u32[]{:S(2)}) collective-permute-start(bf16[2,256,128]{2,1,0:T(8,128)(2,1)S(1)} %get-tuple-element.88), channel_id=1, source_target_pairs={{0,8},{4,12},{8,0},{12,4},{16,24},{20,28},{24,16},{28,20},{1,9},{5... | collective-permute-start | bytes 393224 | tf_op jit(solution)/shard_map/ppermute | solution.py:18
  63.6 5.4 %collective-permute-done.21 = bf16[4,256,128]{2,1,0:T(8,128)(2,1)S(1)} collective-permute-done((bf16[4,256,128]{2,1,0:T(8,128)(2,1)S(1)}, bf16[4,256,128]{2,1,0:T(8,128)(2,1)S(1)}, u32[]{:S(2)}, u32[]{:S(2)}) %collective-permute-start.21) | collective-permute-done | bytes 262176 | tf_op jit(solution)/shard_map/ppermute | solution.py:18
  69.2 0.6 collective-permute-start.22
  69.8 2.7 %collective-permute-start.34 = (bf16[1,256,128]{2,1,0:T(8,128)(2,1)S(1)}, bf16[1,256,128]{2,1,0:T(8,128)(2,1)S(1)}, u32[]{:S(2)}, u32[]{:S(2)}) collective-permute-start(bf16[1,256,128]{2,1,0:T(8,128)(2,1)S(1)} %get-tuple-element.92), channel_id=1, source_target_pairs={{0,16},{4,20},{8,24},{12,28},{16,0},{20,4},{24,8},{28,12},{1,17},{... | collective-permute-start | bytes 196616 | tf_op jit(solution)/shard_map/ppermute | solution.py:18
  72.7 1.0 %collective-permute-start.31 = (bf16[1,336,128]{2,1,0:T(8,128)(2,1)S(1)}, bf16[1,336,128]{2,1,0:T(8,128)(2,1)S(1)}, u32[]{:S(2)}, u32[]{:S(2)}) collective-permute-start(bf16[1,336,128]{2,1,0:T(8,128)(2,1)S(1)} %get-tuple-element.90), channel_id=1, source_target_pairs={{0,16},{4,20},{8,24},{12,28},{16,0},{20,4},{24,8},{28,12},{1,17},{... | collective-permute-start | bytes 258056 | tf_op jit(solution)/shard_map/ppermute | solution.py:18
  73.7 1.5 %collective-permute-start.26 = (bf16[2,336,128]{2,1,0:T(8,128)(2,1)S(1)}, bf16[2,336,128]{2,1,0:T(8,128)(2,1)S(1)}, u32[]{:S(2)}, u32[]{:S(2)}) collective-permute-start(bf16[2,336,128]{2,1,0:T(8,128)(2,1)S(1)} %slice.114), channel_id=1, source_target_pairs={{0,2},{1,3},{2,0},{3,1},{4,6},{5,7},{6,4},{7,5},{8,10},{9,11},{10,... | collective-permute-start | bytes 516104 | tf_op jit(solution)/shard_map/ppermute | solution.py:18
  75.8 0.7 join_out.1
  76.5 1.2 %copy.31 = bf16[2,6,13,13,128]{4,0,3,2,1:T(2,128)(2,1)} copy(bf16[2,6,13,13,128]{4,3,2,1,0:T(8,128)(2,1)S(1)} %bitcast.54) | data formatting | bytes 1038336
  77.7 2.0 %collective-permute-start.28 = (bf16[1,256,128]{2,1,0:T(8,128)(2,1)S(1)}, bf16[1,256,128]{2,1,0:T(8,128)(2,1)S(1)}, u32[]{:S(2)}, u32[]{:S(2)}) collective-permute-start(bf16[1,256,128]{2,1,0:T(8,128)(2,1)S(1)} %slice.119), channel_id=1, source_target_pairs={{0,16},{4,20},{8,24},{12,28},{16,0},{20,4},{24,8},{28,12},{1,17},{... | collective-permute-start | bytes 196616 | tf_op jit(solution)/shard_map/ppermute | solution.py:18
  79.8 0.7 convert.16
  80.6 0.5 fusion.1
  81.1 1.0 %collective-permute-start.27 = (bf16[1,336,128]{2,1,0:T(8,128)(2,1)S(1)}, bf16[1,336,128]{2,1,0:T(8,128)(2,1)S(1)}, u32[]{:S(2)}, u32[]{:S(2)}) collective-permute-start(bf16[1,336,128]{2,1,0:T(8,128)(2,1)S(1)} %slice.116), channel_id=1, source_target_pairs={{0,16},{4,20},{8,24},{12,28},{16,0},{20,4},{24,8},{28,12},{1,17},{... | collective-permute-start | bytes 258056 | tf_op jit(solution)/shard_map/ppermute | solution.py:18
  82.1 2.0 %collective-permute-done.28 = bf16[1,256,128]{2,1,0:T(8,128)(2,1)S(1)} collective-permute-done((bf16[1,256,128]{2,1,0:T(8,128)(2,1)S(1)}, bf16[1,256,128]{2,1,0:T(8,128)(2,1)S(1)}, u32[]{:S(2)}, u32[]{:S(2)}) %collective-permute-start.28) | collective-permute-done | bytes 65568 | tf_op jit(solution)/shard_map/ppermute | solution.py:18
  84.1 0.7 join_grad.1
  84.8 1.2 %copy.32 = bf16[2,6,13,13,128]{4,0,3,2,1:T(2,128)(2,1)} copy(bf16[2,6,13,13,128]{4,3,2,1,0:T(8,128)(2,1)S(1)} %bitcast.53) | data formatting | bytes 1038336
  86.0 2.2 %collective-permute-done.27 = bf16[1,336,128]{2,1,0:T(8,128)(2,1)S(1)} collective-permute-done((bf16[1,336,128]{2,1,0:T(8,128)(2,1)S(1)}, bf16[1,336,128]{2,1,0:T(8,128)(2,1)S(1)}, u32[]{:S(2)}, u32[]{:S(2)}) %collective-permute-start.27) | collective-permute-done | bytes 86048 | tf_op jit(solution)/shard_map/ppermute | solution.py:18
  88.2 0.5 fusion.2
  88.7 0.7 convert.14
  (98 shorter events, 4.6 us)
Async XLA Ops:
  0.6 8.1 %copy-start = (s32[2,2]{1,0:T(2,128)S(1)}, s32[2,2]{1,0:T(2,128)}, u32[]{:S(2)}) copy-start(s32[2,2]{1,0:T(2,128)} %param.8) | copy-start | bytes 52
  2.0 7.6 %collective-permute-start = (bf16[3,208,128]{2,1,0:T(8,128)(2,1)S(1)}, bf16[3,208,128]{2,1,0:T(8,128)(2,1)S(1)}, u32[]{:S(2)}, u32[]{:S(2)}) collective-permute-start(bf16[3,208,128]{2,1,0:T(8,128)(2,1)S(1)} %constant_dynamic-slice_fusion.3), channel_id=1, source_target_pairs={{0,1},{1,0},{2,3},{3,2},{4,5},{5,4},{6,7},{7,6},{8,9},{9,8},{10,11... | collective-permute-start | bytes 479240 | tf_op jit(solution)/shard_map/ppermute | solution.py:18
  2.5 11.2 %collective-permute-start.1 = (bf16[2,3,208,128]{3,2,1,0:T(8,128)(2,1)S(1)}, bf16[2,3,208,128]{3,2,1,0:T(8,128)(2,1)S(1)}, u32[]{:S(2)}, u32[]{:S(2)}) collective-permute-start(bf16[2,3,208,128]{3,2,1,0:T(8,128)(2,1)S(1)} %bitcast.69), channel_id=1, source_target_pairs={{0,2},{1,3},{2,0},{3,1},{4,6},{5,7},{6,4},{7,5},{8,10},{9,11},{10,... | collective-permute-start | bytes 958472 | tf_op jit(solution)/shard_map/ppermute | solution.py:18
  5.1 11.3 %collective-permute-start.3 = (bf16[2,3,208,128]{3,2,1,0:T(8,128)(2,1)S(1)}, bf16[2,3,208,128]{3,2,1,0:T(8,128)(2,1)S(1)}, u32[]{:S(2)}, u32[]{:S(2)}) collective-permute-start(bf16[2,3,208,128]{3,2,1,0:T(8,128)(2,1)S(1)} %bitcast.50), channel_id=1, source_target_pairs={{0,8},{4,12},{8,0},{12,4},{16,24},{20,28},{24,16},{28,20},{1,9},{5... | collective-permute-start | bytes 958472 | tf_op jit(solution)/shard_map/ppermute | solution.py:18
  8.0 8.4 %copy-start.2 = (f32[512]{0:T(512)S(1)}, f32[512]{0:T(512)}, u32[]{:S(2)}) copy-start(f32[512]{0:T(512)} %param.10) | copy-start | bytes 6148
  8.1 13.2 %collective-permute-start.5 = (bf16[2,3,208,128]{3,2,1,0:T(8,128)(2,1)S(1)}, bf16[2,3,208,128]{3,2,1,0:T(8,128)(2,1)S(1)}, u32[]{:S(2)}, u32[]{:S(2)}) collective-permute-start(bf16[2,3,208,128]{3,2,1,0:T(8,128)(2,1)S(1)} %pad_maximum_fusion), channel_id=1, source_target_pairs={{0,2},{1,3},{2,0},{3,1},{4,6},{5,7},{6,4},{7,5},{8,10},{9,11},{10,... | collective-permute-start | bytes 958472 | tf_op jit(solution)/shard_map/ppermute | solution.py:18
  14.5 1.9 %collective-permute-start.2 = (bf16[3,208,128]{2,1,0:T(8,128)(2,1)S(1)}, bf16[3,208,128]{2,1,0:T(8,128)(2,1)S(1)}, u32[]{:S(2)}, u32[]{:S(2)}) collective-permute-start(bf16[3,208,128]{2,1,0:T(8,128)(2,1)S(1)} %pick.1), channel_id=1, source_target_pairs={{0,1},{1,0},{2,3},{3,2},{4,5},{5,4},{6,7},{7,6},{8,9},{9,8},{10,11... | collective-permute-start | bytes 479240 | tf_op jit(solution)/shard_map/ppermute | solution.py:18
  14.6 15.8 %collective-permute-start.11 = (bf16[2,3,208,128]{3,2,1,0:T(8,128)(2,1)S(1)}, bf16[2,3,208,128]{3,2,1,0:T(8,128)(2,1)S(1)}, u32[]{:S(2)}, u32[]{:S(2)}) collective-permute-start(bf16[2,3,208,128]{3,2,1,0:T(8,128)(2,1)S(1)} %after_part.1.refs_0_.refs_1_), channel_id=1, source_target_pairs={{0,8},{4,12},{8,0},{12,4},{16,24},{20,28},{24,16},{28,20},{1,9},{5... | collective-permute-start | bytes 958472 | tf_op jit(solution)/shard_map/ppermute | solution.py:18
  16.5 6.4 %copy-start.1 = (f32[512]{0:T(512)S(1)}, f32[512]{0:T(512)}, u32[]{:S(2)}) copy-start(f32[512]{0:T(512)} %param.12) | copy-start | bytes 6148
  19.7 23.4 %collective-permute-start.9 = (bf16[4,3,208,128]{3,2,1,0:T(8,128)(2,1)S(1)}, bf16[4,3,208,128]{3,2,1,0:T(8,128)(2,1)S(1)}, u32[]{:S(2)}, u32[]{:S(2)}) collective-permute-start(bf16[4,3,208,128]{3,2,1,0:T(8,128)(2,1)S(1)} %get-tuple-element.39.refs_0_), channel_id=1, source_target_pairs={{0,4},{4,0},{8,12},{12,8},{16,20},{20,16},{24,28},{28,24},{1,5},{5... | collective-permute-start | bytes 1916936 | tf_op jit(solution)/shard_map/ppermute | solution.py:18
  21.3 1.4 %collective-permute-start.4 = (bf16[3,208,128]{2,1,0:T(8,128)(2,1)S(1)}, bf16[3,208,128]{2,1,0:T(8,128)(2,1)S(1)}, u32[]{:S(2)}, u32[]{:S(2)}) collective-permute-start(bf16[3,208,128]{2,1,0:T(8,128)(2,1)S(1)} %get-tuple-element.82.refs_4_), channel_id=1, source_target_pairs={{0,1},{1,0},{2,3},{3,2},{4,5},{5,4},{6,7},{7,6},{8,9},{9,8},{10,11... | collective-permute-start | bytes 479240 | tf_op jit(solution)/shard_map/ppermute | solution.py:18
  21.3 1.6 %collective-permute-start.6 = (bf16[1,3,208,128]{3,2,1,0:T(8,128)(2,1)S(1)}, bf16[1,3,208,128]{3,2,1,0:T(8,128)(2,1)S(1)}, u32[]{:S(2)}, u32[]{:S(2)}) collective-permute-start(bf16[1,3,208,128]{3,2,1,0:T(8,128)(2,1)S(1)} %slice.110), channel_id=1, source_target_pairs={{0,1},{1,0},{2,3},{3,2},{4,5},{5,4},{6,7},{7,6},{8,9},{9,8},{10,11... | collective-permute-start | bytes 479240 | tf_op jit(solution)/shard_map/ppermute | solution.py:18
  21.9 9.0 %collective-permute-start.12 = (bf16[2,3,208,128]{3,2,1,0:T(8,128)(2,1)S(1)}, bf16[2,3,208,128]{3,2,1,0:T(8,128)(2,1)S(1)}, u32[]{:S(2)}, u32[]{:S(2)}) collective-permute-start(bf16[2,3,208,128]{3,2,1,0:T(8,128)(2,1)S(1)} %slice.86), channel_id=1, source_target_pairs={{0,1},{1,0},{2,3},{3,2},{4,5},{5,4},{6,7},{7,6},{8,9},{9,8},{10,11... | collective-permute-start | bytes 958472 | tf_op jit(solution)/shard_map/ppermute | solution.py:18
  28.5 7.0 %collective-permute-start.13 = (bf16[3,208,256]{2,1,0:T(8,128)(2,1)S(1)}, bf16[3,208,256]{2,1,0:T(8,128)(2,1)S(1)}, u32[]{:S(2)}, u32[]{:S(2)}) collective-permute-start(bf16[3,208,256]{2,1,0:T(8,128)(2,1)S(1)} %get-tuple-element.49.refs_4_), channel_id=1, source_target_pairs={{0,1},{1,0},{2,3},{3,2},{4,5},{5,4},{6,7},{7,6},{8,9},{9,8},{10,11... | collective-permute-start | bytes 958472 | tf_op jit(solution)/shard_map/ppermute | solution.py:18
  28.9 11.7 %collective-permute-start.10 = (bf16[2,3,208,128]{3,2,1,0:T(8,128)(2,1)S(1)}, bf16[2,3,208,128]{3,2,1,0:T(8,128)(2,1)S(1)}, u32[]{:S(2)}, u32[]{:S(2)}) collective-permute-start(bf16[2,3,208,128]{3,2,1,0:T(8,128)(2,1)S(1)} %get-tuple-element.45), channel_id=1, source_target_pairs={{0,2},{1,3},{2,0},{3,1},{4,6},{5,7},{6,4},{7,5},{8,10},{9,11},{10,... | collective-permute-start | bytes 958472 | tf_op jit(solution)/shard_map/ppermute | solution.py:18
  30.4 12.6 %collective-permute-start.8 = (bf16[3,208,256]{2,1,0:T(8,128)(2,1)S(1)}, bf16[3,208,256]{2,1,0:T(8,128)(2,1)S(1)}, u32[]{:S(2)}, u32[]{:S(2)}) collective-permute-start(bf16[3,208,256]{2,1,0:T(8,128)(2,1)S(1)} %get-tuple-element.44), channel_id=1, source_target_pairs={{0,4},{4,0},{8,12},{12,8},{16,20},{20,16},{24,28},{28,24},{1,5},{5... | collective-permute-start | bytes 958472 | tf_op jit(solution)/shard_map/ppermute | solution.py:18
  30.9 12.7 %collective-permute-start.7 = (bf16[3,208,128]{2,1,0:T(8,128)(2,1)S(1)}, bf16[3,208,128]{2,1,0:T(8,128)(2,1)S(1)}, u32[]{:S(2)}, u32[]{:S(2)}) collective-permute-start(bf16[3,208,128]{2,1,0:T(8,128)(2,1)S(1)} %get-tuple-element.43), channel_id=1, source_target_pairs={{0,1},{1,0},{2,3},{3,2},{4,5},{5,4},{6,7},{7,6},{8,9},{9,8},{10,11... | collective-permute-start | bytes 479240 | tf_op jit(solution)/shard_map/ppermute | solution.py:18
  35.5 8.3 %collective-permute-start.15 = (bf16[3,208,256]{2,1,0:T(8,128)(2,1)S(1)}, bf16[3,208,256]{2,1,0:T(8,128)(2,1)S(1)}, u32[]{:S(2)}, u32[]{:S(2)}) collective-permute-start(bf16[3,208,256]{2,1,0:T(8,128)(2,1)S(1)} %get-tuple-element.52.refs_4_), channel_id=1, source_target_pairs={{0,1},{1,0},{2,3},{3,2},{4,5},{5,4},{6,7},{7,6},{8,9},{9,8},{10,11... | collective-permute-start | bytes 958472 | tf_op jit(solution)/shard_map/ppermute | solution.py:18
  40.7 9.5 %collective-permute-start.16 = (bf16[3,208,256]{2,1,0:T(8,128)(2,1)S(1)}, bf16[3,208,256]{2,1,0:T(8,128)(2,1)S(1)}, u32[]{:S(2)}, u32[]{:S(2)}) collective-permute-start(bf16[3,208,256]{2,1,0:T(8,128)(2,1)S(1)} %get-tuple-element.53), channel_id=1, source_target_pairs={{0,8},{4,12},{8,0},{12,4},{16,24},{20,28},{24,16},{28,20},{1,9},{5... | collective-permute-start | bytes 958472 | tf_op jit(solution)/shard_map/ppermute | solution.py:18
  43.1 2.4 %collective-permute-start.17 = (bf16[2,3,208,128]{3,2,1,0:T(8,128)(2,1)S(1)}, bf16[2,3,208,128]{3,2,1,0:T(8,128)(2,1)S(1)}, u32[]{:S(2)}, u32[]{:S(2)}) collective-permute-start(bf16[2,3,208,128]{3,2,1,0:T(8,128)(2,1)S(1)} %slice.88), channel_id=1, source_target_pairs={{0,1},{1,0},{2,3},{3,2},{4,5},{5,4},{6,7},{7,6},{8,9},{9,8},{10,11... | collective-permute-start | bytes 958472 | tf_op jit(solution)/shard_map/ppermute | solution.py:18
  43.2 2.3 %collective-permute-start.18 = (bf16[3,208,256]{2,1,0:T(8,128)(2,1)S(1)}, bf16[3,208,256]{2,1,0:T(8,128)(2,1)S(1)}, u32[]{:S(2)}, u32[]{:S(2)}) collective-permute-start(bf16[3,208,256]{2,1,0:T(8,128)(2,1)S(1)} %get-tuple-element.55.refs_6_), channel_id=1, source_target_pairs={{0,1},{1,0},{2,3},{3,2},{4,5},{5,4},{6,7},{7,6},{8,9},{9,8},{10,11... | collective-permute-start | bytes 958472 | tf_op jit(solution)/shard_map/ppermute | solution.py:18
  43.7 1.8 %collective-permute-start.14 = (bf16[3,208,128]{2,1,0:T(8,128)(2,1)S(1)}, bf16[3,208,128]{2,1,0:T(8,128)(2,1)S(1)}, u32[]{:S(2)}, u32[]{:S(2)}) collective-permute-start(bf16[3,208,128]{2,1,0:T(8,128)(2,1)S(1)} %slice_bitcast_fusion.1), channel_id=1, source_target_pairs={{0,1},{1,0},{2,3},{3,2},{4,5},{5,4},{6,7},{7,6},{8,9},{9,8},{10,11... | collective-permute-start | bytes 479240 | tf_op jit(solution)/shard_map/ppermute | solution.py:18
  43.8 10.2 %collective-permute-start.20 = (bf16[2,3,208,128]{3,2,1,0:T(8,128)(2,1)S(1)}, bf16[2,3,208,128]{3,2,1,0:T(8,128)(2,1)S(1)}, u32[]{:S(2)}, u32[]{:S(2)}) collective-permute-start(bf16[2,3,208,128]{3,2,1,0:T(8,128)(2,1)S(1)} %get-tuple-element.57), channel_id=1, source_target_pairs={{0,2},{1,3},{2,0},{3,1},{4,6},{5,7},{6,4},{7,5},{8,10},{9,11},{10,... | collective-permute-start | bytes 958472 | tf_op jit(solution)/shard_map/ppermute | solution.py:18
  50.2 3.9 %collective-permute-start.19 = (bf16[3,208,256]{2,1,0:T(8,128)(2,1)S(1)}, bf16[3,208,256]{2,1,0:T(8,128)(2,1)S(1)}, u32[]{:S(2)}, u32[]{:S(2)}) collective-permute-start(bf16[3,208,256]{2,1,0:T(8,128)(2,1)S(1)} %after_grad5.1.refs_6_), channel_id=1, source_target_pairs={{0,1},{1,0},{2,3},{3,2},{4,5},{5,4},{6,7},{7,6},{8,9},{9,8},{10,11... | collective-permute-start | bytes 958472 | tf_op jit(solution)/shard_map/ppermute | solution.py:18
  50.2 11.4 %collective-permute-start.32 = (bf16[4,256,128]{2,1,0:T(8,128)(2,1)S(1)}, bf16[4,256,128]{2,1,0:T(8,128)(2,1)S(1)}, u32[]{:S(2)}, u32[]{:S(2)}) collective-permute-start(bf16[4,256,128]{2,1,0:T(8,128)(2,1)S(1)} %get-tuple-element.67), channel_id=1, source_target_pairs={{0,2},{1,3},{2,0},{3,1},{4,6},{5,7},{6,4},{7,5},{8,10},{9,11},{10,... | collective-permute-start | bytes 786440 | tf_op jit(solution)/shard_map/ppermute | solution.py:18
  51.5 11.5 %collective-permute-start.29 = (bf16[4,336,128]{2,1,0:T(8,128)(2,1)S(1)}, bf16[4,336,128]{2,1,0:T(8,128)(2,1)S(1)}, u32[]{:S(2)}, u32[]{:S(2)}) collective-permute-start(bf16[4,336,128]{2,1,0:T(8,128)(2,1)S(1)} %get-tuple-element.65), channel_id=1, source_target_pairs={{0,8},{4,12},{8,0},{12,4},{16,24},{20,28},{24,16},{28,20},{1,9},{5... | collective-permute-start | bytes 1032200 | tf_op jit(solution)/shard_map/ppermute | solution.py:18
  58.4 14.1 %collective-permute-start.23 = (bf16[4,336,128]{2,1,0:T(8,128)(2,1)S(1)}, bf16[4,336,128]{2,1,0:T(8,128)(2,1)S(1)}, u32[]{:S(2)}, u32[]{:S(2)}) collective-permute-start(bf16[4,336,128]{2,1,0:T(8,128)(2,1)S(1)} %get-tuple-element.62), channel_id=1, source_target_pairs={{0,4},{4,0},{8,12},{12,8},{16,20},{20,16},{24,28},{28,24},{1,5},{5... | collective-permute-start | bytes 1032200 | tf_op jit(solution)/shard_map/ppermute | solution.py:18
  60.0 9.1 %collective-permute-start.21 = (bf16[4,256,128]{2,1,0:T(8,128)(2,1)S(1)}, bf16[4,256,128]{2,1,0:T(8,128)(2,1)S(1)}, u32[]{:S(2)}, u32[]{:S(2)}) collective-permute-start(bf16[4,256,128]{2,1,0:T(8,128)(2,1)S(1)} %get-tuple-element.59), channel_id=1, source_target_pairs={{0,2},{1,3},{2,0},{3,1},{4,6},{5,7},{6,4},{7,5},{8,10},{9,11},{10,... | collective-permute-start | bytes 786440 | tf_op jit(solution)/shard_map/ppermute | solution.py:18
  61.7 8.0 %collective-permute-start.33 = (bf16[2,256,128]{2,1,0:T(8,128)(2,1)S(1)}, bf16[2,256,128]{2,1,0:T(8,128)(2,1)S(1)}, u32[]{:S(2)}, u32[]{:S(2)}) collective-permute-start(bf16[2,256,128]{2,1,0:T(8,128)(2,1)S(1)} %get-tuple-element.88), channel_id=1, source_target_pairs={{0,8},{4,12},{8,0},{12,4},{16,24},{20,28},{24,16},{28,20},{1,9},{5... | collective-permute-start | bytes 393224 | tf_op jit(solution)/shard_map/ppermute | solution.py:18
  63.2 9.4 %collective-permute-start.30 = (bf16[2,336,128]{2,1,0:T(8,128)(2,1)S(1)}, bf16[2,336,128]{2,1,0:T(8,128)(2,1)S(1)}, u32[]{:S(2)}, u32[]{:S(2)}) collective-permute-start(bf16[2,336,128]{2,1,0:T(8,128)(2,1)S(1)} %get-tuple-element.86), channel_id=1, source_target_pairs={{0,2},{1,3},{2,0},{3,1},{4,6},{5,7},{6,4},{7,5},{8,10},{9,11},{10,... | collective-permute-start | bytes 516104 | tf_op jit(solution)/shard_map/ppermute | solution.py:18
  69.2 6.1 %collective-permute-start.22 = (bf16[2,256,128]{2,1,0:T(8,128)(2,1)S(1)}, bf16[2,256,128]{2,1,0:T(8,128)(2,1)S(1)}, u32[]{:S(2)}, u32[]{:S(2)}) collective-permute-start(bf16[2,256,128]{2,1,0:T(8,128)(2,1)S(1)} %slice.112), channel_id=1, source_target_pairs={{0,4},{4,0},{8,12},{12,8},{16,20},{20,16},{24,28},{28,24},{1,5},{5... | collective-permute-start | bytes 393224 | tf_op jit(solution)/shard_map/ppermute | solution.py:18
  69.8 7.9 %collective-permute-start.34 = (bf16[1,256,128]{2,1,0:T(8,128)(2,1)S(1)}, bf16[1,256,128]{2,1,0:T(8,128)(2,1)S(1)}, u32[]{:S(2)}, u32[]{:S(2)}) collective-permute-start(bf16[1,256,128]{2,1,0:T(8,128)(2,1)S(1)} %get-tuple-element.92), channel_id=1, source_target_pairs={{0,16},{4,20},{8,24},{12,28},{16,0},{20,4},{24,8},{28,12},{1,17},{... | collective-permute-start | bytes 196616 | tf_op jit(solution)/shard_map/ppermute | solution.py:18
  72.7 7.1 %collective-permute-start.31 = (bf16[1,336,128]{2,1,0:T(8,128)(2,1)S(1)}, bf16[1,336,128]{2,1,0:T(8,128)(2,1)S(1)}, u32[]{:S(2)}, u32[]{:S(2)}) collective-permute-start(bf16[1,336,128]{2,1,0:T(8,128)(2,1)S(1)} %get-tuple-element.90), channel_id=1, source_target_pairs={{0,16},{4,20},{8,24},{12,28},{16,0},{20,4},{24,8},{28,12},{1,17},{... | collective-permute-start | bytes 258056 | tf_op jit(solution)/shard_map/ppermute | solution.py:18
  73.7 7.4 %collective-permute-start.26 = (bf16[2,336,128]{2,1,0:T(8,128)(2,1)S(1)}, bf16[2,336,128]{2,1,0:T(8,128)(2,1)S(1)}, u32[]{:S(2)}, u32[]{:S(2)}) collective-permute-start(bf16[2,336,128]{2,1,0:T(8,128)(2,1)S(1)} %slice.114), channel_id=1, source_target_pairs={{0,2},{1,3},{2,0},{3,1},{4,6},{5,7},{6,4},{7,5},{8,10},{9,11},{10,... | collective-permute-start | bytes 516104 | tf_op jit(solution)/shard_map/ppermute | solution.py:18
  75.2 8.9 %collective-permute-start.25 = (bf16[3,208,128]{2,1,0:T(8,128)(2,1)S(1)}, bf16[3,208,128]{2,1,0:T(8,128)(2,1)S(1)}, u32[]{:S(2)}, u32[]{:S(2)}) collective-permute-start(bf16[3,208,128]{2,1,0:T(8,128)(2,1)S(1)} %slice_bitcast_fusion), channel_id=1, source_target_pairs={{0,1},{1,0},{2,3},{3,2},{4,5},{5,4},{6,7},{7,6},{8,9},{9,8},{10,11... | collective-permute-start | bytes 479240 | tf_op jit(solution)/shard_map/ppermute | solution.py:18
  75.3 8.9 %collective-permute-start.24 = (bf16[3,208,128]{2,1,0:T(8,128)(2,1)S(1)}, bf16[3,208,128]{2,1,0:T(8,128)(2,1)S(1)}, u32[]{:S(2)}, u32[]{:S(2)}) collective-permute-start(bf16[3,208,128]{2,1,0:T(8,128)(2,1)S(1)} %get-tuple-element.63), channel_id=1, source_target_pairs={{0,1},{1,0},{2,3},{3,2},{4,5},{5,4},{6,7},{7,6},{8,9},{9,8},{10,11... | collective-permute-start | bytes 479240 | tf_op jit(solution)/shard_map/ppermute | solution.py:18
  77.7 6.4 %collective-permute-start.28 = (bf16[1,256,128]{2,1,0:T(8,128)(2,1)S(1)}, bf16[1,256,128]{2,1,0:T(8,128)(2,1)S(1)}, u32[]{:S(2)}, u32[]{:S(2)}) collective-permute-start(bf16[1,256,128]{2,1,0:T(8,128)(2,1)S(1)} %slice.119), channel_id=1, source_target_pairs={{0,16},{4,20},{8,24},{12,28},{16,0},{20,4},{24,8},{28,12},{1,17},{... | collective-permute-start | bytes 196616 | tf_op jit(solution)/shard_map/ppermute | solution.py:18
  81.1 7.0 %collective-permute-start.27 = (bf16[1,336,128]{2,1,0:T(8,128)(2,1)S(1)}, bf16[1,336,128]{2,1,0:T(8,128)(2,1)S(1)}, u32[]{:S(2)}, u32[]{:S(2)}) collective-permute-start(bf16[1,336,128]{2,1,0:T(8,128)(2,1)S(1)} %slice.116), channel_id=1, source_target_pairs={{0,16},{4,20},{8,24},{12,28},{16,0},{20,4},{24,8},{28,12},{1,17},{... | collective-permute-start | bytes 258056 | tf_op jit(solution)/shard_map/ppermute | solution.py:18

commit v5 on v4

--- a/solution.py
+++ b/solution.py
@@ -520,7 +520,9 @@
                 parts[n] = kept + swap(sent, "dp", n_dp, bit)
             bit //= 2
         per_dp = channels // n_dp
-        own = lax.dynamic_slice_in_dim(bias[0], (row % fine) * per_dp, per_dp, 0)
+        own = bias[0, :per_dp]
+        if fine > 1:
+            own = lax.dynamic_slice_in_dim(bias[0], (row % fine) * per_dp, per_dp, 0)
         grads = jnp.concatenate([part.transpose(0, 2, 1).astype(F32) for part in parts])
         return grads.reshape(3, 3, share, per_dp), own.astype(F32)
 

time: 89.7 us -> 89.7 us (level)
  no operation moved by 1% of the time
where the time goes in v5:
time: 89.7 us; the launch traced here: 89.5 us
  starting transfers between devices  32.9 us (37%)
  Pallas kernels  32.9 us (37%)
  waiting for transfers between devices  13.3 us (15%)
  local copies, waits for them, and re-layouts  5.9 us (7%)
  other arithmetic  3.33 us (4%)
  between operations  1.16 us (1%)
    pallas_call x10, Pallas kernels, call(): return lambda *args: called(info, *args, *after)  32.9 us
    ppermute x35, starting transfers between devices, swap(): return lax.ppermute(value, axis_name, [(i, i ^ bit) for i in range(size)])  32.9 us
    ppermute x35, waiting for transfers between devices, swap(): return lax.ppermute(value, axis_name, [(i, i ^ bit) for i in range(size)])  13.3 us
    unnamed x10, local copies, waits for them, and re-layouts  4.69 us
  transfers between devices with their start and end apart: 35, of which 9 were waited for; matrix products, arithmetic and copies ran while one was open for 7% of the time, Pallas kernels for 37%

profile of v5, /device:TPU:0, one launch (start us, length us, event | category | flops | bytes accessed | tf_op | source)
XLA Modules:
  0.0 89.5 jit_solution(6512707815814508456)
XLA Ops:
  0.7 1.1 %copy.29 = bf16[2,6,13,13,128]{4,3,2,1,0:T(8,128)(2,1)S(1)} copy(bf16[2,6,13,13,128]{4,0,3,2,1:T(2,128)(2,1)} %param.7) | data formatting | bytes 1038336 | tf_op args[0]
  2.0 0.5 collective-permute-start
  2.5 2.6 %collective-permute-start.1 = (bf16[2,3,208,128]{3,2,1,0:T(8,128)(2,1)S(1)}, bf16[2,3,208,128]{3,2,1,0:T(8,128)(2,1)S(1)}, u32[]{:S(2)}, u32[]{:S(2)}) collective-permute-start(bf16[2,3,208,128]{3,2,1,0:T(8,128)(2,1)S(1)} %bitcast.73), channel_id=1, source_target_pairs={{0,2},{1,3},{2,0},{3,1},{4,6},{5,7},{6,4},{7,5},{8,10},{9,11},{10,... | collective-permute-start | bytes 958472 | tf_op jit(solution)/shard_map/ppermute | solution.py:18
  5.1 1.6 %collective-permute-start.3 = (bf16[2,3,208,128]{3,2,1,0:T(8,128)(2,1)S(1)}, bf16[2,3,208,128]{3,2,1,0:T(8,128)(2,1)S(1)}, u32[]{:S(2)}, u32[]{:S(2)}) collective-permute-start(bf16[2,3,208,128]{3,2,1,0:T(8,128)(2,1)S(1)} %bitcast.54), channel_id=1, source_target_pairs={{0,8},{4,12},{8,0},{12,4},{16,24},{20,28},{24,16},{28,20},{1,9},{5... | collective-permute-start | bytes 958472 | tf_op jit(solution)/shard_map/ppermute | solution.py:18
  6.7 1.1 %copy.30 = bf16[2,6,13,13,128]{4,3,2,1,0:T(8,128)(2,1)S(1)} copy(bf16[2,6,13,13,128]{4,0,3,2,1:T(2,128)(2,1)} %param.13) | data formatting | bytes 1038336 | tf_op args[6]
  8.1 0.6 collective-permute-start.5
  8.8 0.6 gather_fusion
  9.6 4.2 %conv4_part.1 = (f32[2,624,256]{2,1,0:T(8,128)S(1)}, bf16[9,256,512]{2,1,0:T(8,128)(2,1)S(1)}) custom-call(s32[5]{0:T(128)S(1)} %pad_add_fusion.info, bf16[2,3,208,128]{3,2,1,0:T(8,128)(2,1)S(1)} %bitcast.55, bf16[3,208,128]{2,1,0:T(8,128)(2,1)S(1)} %collective-permute-done.refs_1_, bf16[9,512,512]{2,1,0:T(8,128)(2,1)} %bitcast.61, ...), custom_call_target="tpu_custom_call" | custom-call | tf_op jit(solution)/shard_map/conv4_part/pallas_call | solution.py:446
  13.8 0.8 pick.1
  14.6 1.8 %collective-permute-start.11 = (bf16[2,3,208,128]{3,2,1,0:T(8,128)(2,1)S(1)}, bf16[2,3,208,128]{3,2,1,0:T(8,128)(2,1)S(1)}, u32[]{:S(2)}, u32[]{:S(2)}) collective-permute-start(bf16[2,3,208,128]{3,2,1,0:T(8,128)(2,1)S(1)} %after_part.1.refs_0_.refs_1_), channel_id=1, source_target_pairs={{0,8},{4,12},{8,0},{12,4},{16,24},{20,28},{24,16},{28,20},{1,9},{5... | collective-permute-start | bytes 958472 | tf_op jit(solution)/shard_map/ppermute | solution.py:18
  16.5 3.2 %conv4.1 = (bf16[4,3,208,128]{3,2,1,0:T(8,128)(2,1)S(1)}, f32[2,624,256]{2,1,0:T(8,128)S(1)}, bf16[9,512,512]{2,1,0:T(8,128)(2,1)S(1)}) custom-call(s32[5]{0:T(128)S(1)} %pad_add_fusion.info, f32[2,624,256]{2,1,0:T(8,128)S(1)} %get-tuple-element.37.refs_1_.refs_0_, bf16[2,3,208,128]{3,2,1,0:T(8,128)(2,1)S(1)} %after_part.1.refs_0_.refs_1_, ...), custom_call_target="tpu_custom_call" | custom-call | tf_op jit(solution)/shard_map/conv4/pallas_call | solution.py:446
  19.7 1.6 %collective-permute-start.9 = (bf16[4,3,208,128]{3,2,1,0:T(8,128)(2,1)S(1)}, bf16[4,3,208,128]{3,2,1,0:T(8,128)(2,1)S(1)}, u32[]{:S(2)}, u32[]{:S(2)}) collective-permute-start(bf16[4,3,208,128]{3,2,1,0:T(8,128)(2,1)S(1)} %get-tuple-element.39.refs_0_), channel_id=1, source_target_pairs={{0,4},{4,0},{8,12},{12,8},{16,20},{20,16},{24,28},{28,24},{1,5},{5... | collective-permute-start | bytes 1916936 | tf_op jit(solution)/shard_map/ppermute | solution.py:18
  21.3 0.6 collective-permute-start.6
  22.0 0.7 collective-permute-done.4.refs_2_
  22.9 5.6 %conv5.1 = (bf16[3,208,128]{2,1,0:T(8,128)(2,1)S(1)}, bf16[3,208,128]{2,1,0:T(8,128)(2,1)S(1)}, bf16[2,3,208,128]{3,2,1,0:T(8,128)(2,1)S(1)}, bf16[3,208,512]{2,...) custom-call(s32[5]{0:T(128)S(1)} %pad_add_fusion.info, ...), custom_call_target="tpu_custom_call" | custom-call | tf_op jit(solution)/shard_map/conv5/pallas_call | solution.py:446
  28.9 1.5 %collective-permute-start.10 = (bf16[2,3,208,128]{3,2,1,0:T(8,128)(2,1)S(1)}, bf16[2,3,208,128]{3,2,1,0:T(8,128)(2,1)S(1)}, u32[]{:S(2)}, u32[]{:S(2)}) collective-permute-start(bf16[2,3,208,128]{3,2,1,0:T(8,128)(2,1)S(1)} %get-tuple-element.45), channel_id=1, source_target_pairs={{0,2},{1,3},{2,0},{3,1},{4,6},{5,7},{6,4},{7,5},{8,10},{9,11},{10,... | collective-permute-start | bytes 958472 | tf_op jit(solution)/shard_map/ppermute | solution.py:18
  30.4 0.5 collective-permute-start.8
  30.9 4.5 %back5.1 = (bf16[3,208,512]{2,1,0:T(8,128)(2,1)S(1)}, bf16[3,208,256]{2,1,0:T(8,128)(2,1)S(1)}, bf16[3,208,256]{2,1,0:T(8,128)(2,1)S(1)}, bf16[9,512,512]{2,1,0:T(8,128)(2,1)S(1)}) custom-call(s32[5]{0:T(128)S(1)} %pad_add_fusion.info, bf16[3,208,512]{2,1,0:T(8,128)(2,1)S(1)} %get-tuple-element.46.refs_0_, f32[2,624,256]{2,1,0:T(8,128)S(1)} %get-tuple-element.40.refs_1_, ...), custom_call_target="tpu_custom_call" | custom-call | tf_op jit(solution)/shard_map/back5/pallas_call | solution.py:446
  35.5 0.6 collective-permute-start.15
  36.1 4.6 %back4.1 = (bf16[3,208,128]{2,1,0:T(8,128)(2,1)S(1)}, bf16[3,208,128]{2,1,0:T(8,128)(2,1)S(1)}, bf16[2,3,208,128]{3,2,1,0:T(8,128)(2,1)S(1)}) custom-call(s32[5]{0:T(128)S(1)} %pad_add_fusion.info, bf16[3,208,512]{2,1,0:T(8,128)(2,1)S(1)} %get-tuple-element.47.refs_0_, bf16[9,512,512]{2,1,0:T(8,128)(2,1)S(1)} %get-tuple-element.48.refs_1_, ...), custom_call_target="tpu_custom_call" | custom-call | flops 1472200704 | tf_op jit(solution)/shard_map/back4/pallas_call | solution.py:446
  40.7 1.4 %collective-permute-start.16 = (bf16[3,208,256]{2,1,0:T(8,128)(2,1)S(1)}, bf16[3,208,256]{2,1,0:T(8,128)(2,1)S(1)}, u32[]{:S(2)}, u32[]{:S(2)}) collective-permute-start(bf16[3,208,256]{2,1,0:T(8,128)(2,1)S(1)} %get-tuple-element.53), channel_id=1, source_target_pairs={{0,8},{4,12},{8,0},{12,4},{16,24},{20,28},{24,16},{28,20},{1,9},{5... | collective-permute-start | bytes 958472 | tf_op jit(solution)/shard_map/ppermute | solution.py:18
  42.1 1.0 %collective-permute-done.8.refs_0_ = bf16[3,208,256]{2,1,0:T(8,128)(2,1)S(1)} collective-permute-done((bf16[3,208,256]{2,1,0:T(8,128)(2,1)S(1)}, bf16[3,208,256]{2,1,0:T(8,128)(2,1)S(1)}, u32[]{:S(2)}, u32[]{:S(2)}) %collective-permute-start.8) | collective-permute-done | bytes 319520 | tf_op jit(solution)/shard_map/ppermute | solution.py:18
  43.8 1.5 %collective-permute-start.20 = (bf16[2,3,208,128]{3,2,1,0:T(8,128)(2,1)S(1)}, bf16[2,3,208,128]{3,2,1,0:T(8,128)(2,1)S(1)}, u32[]{:S(2)}, u32[]{:S(2)}) collective-permute-start(bf16[2,3,208,128]{3,2,1,0:T(8,128)(2,1)S(1)} %get-tuple-element.57), channel_id=1, source_target_pairs={{0,2},{1,3},{2,0},{3,1},{4,6},{5,7},{6,4},{7,5},{8,10},{9,11},{10,... | collective-permute-start | bytes 958472 | tf_op jit(solution)/shard_map/ppermute | solution.py:18
  45.5 4.3 %grad5.1 = (bf16[4,336,128]{2,1,0:T(8,128)(2,1)S(1)}, bf16[4,336,128]{2,1,0:T(8,128)(2,1)S(1)}, bf16[4,256,128]{2,1,0:T(8,128)(2,1)S(1)}, bf16[4,256,128]{2,1,0:T(8,128)(2,1)S(1)}) custom-call(s32[5]{0:T(128)S(1)} %pad_add_fusion.info, bf16[4,3,208,128]{3,2,1,0:T(8,128)(2,1)S(1)} %get-tuple-element.39.refs_0_, ...), custom_call_target="tpu_custom_call" | custom-call | tf_op jit(solution)/shard_map/grad5/pallas_call | solution.py:446
  50.2 1.3 %collective-permute-start.32 = (bf16[4,256,128]{2,1,0:T(8,128)(2,1)S(1)}, bf16[4,256,128]{2,1,0:T(8,128)(2,1)S(1)}, u32[]{:S(2)}, u32[]{:S(2)}) collective-permute-start(bf16[4,256,128]{2,1,0:T(8,128)(2,1)S(1)} %get-tuple-element.67), channel_id=1, source_target_pairs={{0,2},{1,3},{2,0},{3,1},{4,6},{5,7},{6,4},{7,5},{8,10},{9,11},{10,... | collective-permute-start | bytes 786440 | tf_op jit(solution)/shard_map/ppermute | solution.py:18
  51.5 1.3 %collective-permute-start.29 = (bf16[4,336,128]{2,1,0:T(8,128)(2,1)S(1)}, bf16[4,336,128]{2,1,0:T(8,128)(2,1)S(1)}, u32[]{:S(2)}, u32[]{:S(2)}) collective-permute-start(bf16[4,336,128]{2,1,0:T(8,128)(2,1)S(1)} %get-tuple-element.65), channel_id=1, source_target_pairs={{0,8},{4,12},{8,0},{12,4},{16,24},{20,28},{24,16},{28,20},{1,9},{5... | collective-permute-start | bytes 1032200 | tf_op jit(solution)/shard_map/ppermute | solution.py:18
  52.8 1.3 %collective-permute-done.20.refs_9_.refs_1_ = bf16[2,3,208,128]{3,2,1,0:T(8,128)(2,1)S(1)} collective-permute-done((bf16[2,3,208,128]{3,2,1,0:T(8,128)(2,1)S(1)}, bf16[2,3,208,128]{3,2,1,0:T(8,128)(2,1)S(1)}, u32[]{:S(2)}, u32[]{:S(2)}) %collective-permute-start.20) | collective-permute-done | bytes 319520 | tf_op jit(solution)/shard_map/ppermute | solution.py:18
  54.1 4.3 %grad4.1 = (bf16[4,336,128]{2,1,0:T(8,128)(2,1)S(1)}, bf16[4,336,128]{2,1,0:T(8,128)(2,1)S(1)}, bf16[4,256,128]{2,1,0:T(8,128)(2,1)S(1)}, bf16[4,256,128]{2,1,0:T(8,128)(2,1)S(1)}) custom-call(s32[5]{0:T(128)S(1)} %pad_add_fusion.info, bf16[2,3,208,128]{3,2,1,0:T(8,128)(2,1)S(1)} %bitcast.56, bf16[2,3,208,128]{3,2,1,0:T(8,128)(2,1)S(1)} %after_part.1.refs_0_.refs_1_, ...), custom_call_target="tpu_custom_call" | custom-call | tf_op jit(solution)/shard_map/grad4/pallas_call | solution.py:446
  58.4 1.6 %collective-permute-start.23 = (bf16[4,336,128]{2,1,0:T(8,128)(2,1)S(1)}, bf16[4,336,128]{2,1,0:T(8,128)(2,1)S(1)}, u32[]{:S(2)}, u32[]{:S(2)}) collective-permute-start(bf16[4,336,128]{2,1,0:T(8,128)(2,1)S(1)} %get-tuple-element.62), channel_id=1, source_target_pairs={{0,4},{4,0},{8,12},{12,8},{16,20},{20,16},{24,28},{28,24},{1,5},{5... | collective-permute-start | bytes 1032200 | tf_op jit(solution)/shard_map/ppermute | solution.py:18
  60.0 1.6 %collective-permute-start.21 = (bf16[4,256,128]{2,1,0:T(8,128)(2,1)S(1)}, bf16[4,256,128]{2,1,0:T(8,128)(2,1)S(1)}, u32[]{:S(2)}, u32[]{:S(2)}) collective-permute-start(bf16[4,256,128]{2,1,0:T(8,128)(2,1)S(1)} %get-tuple-element.59), channel_id=1, source_target_pairs={{0,2},{1,3},{2,0},{3,1},{4,6},{5,7},{6,4},{7,5},{8,10},{9,11},{10,... | collective-permute-start | bytes 786440 | tf_op jit(solution)/shard_map/ppermute | solution.py:18
  61.7 1.3 %collective-permute-start.33 = (bf16[2,256,128]{2,1,0:T(8,128)(2,1)S(1)}, bf16[2,256,128]{2,1,0:T(8,128)(2,1)S(1)}, u32[]{:S(2)}, u32[]{:S(2)}) collective-permute-start(bf16[2,256,128]{2,1,0:T(8,128)(2,1)S(1)} %get-tuple-element.88), channel_id=1, source_target_pairs={{0,8},{4,12},{8,0},{12,4},{16,24},{20,28},{24,16},{28,20},{1,9},{5... | collective-permute-start | bytes 393224 | tf_op jit(solution)/shard_map/ppermute | solution.py:18
  63.6 5.4 %collective-permute-done.21 = bf16[4,256,128]{2,1,0:T(8,128)(2,1)S(1)} collective-permute-done((bf16[4,256,128]{2,1,0:T(8,128)(2,1)S(1)}, bf16[4,256,128]{2,1,0:T(8,128)(2,1)S(1)}, u32[]{:S(2)}, u32[]{:S(2)}) %collective-permute-start.21) | collective-permute-done | bytes 262176 | tf_op jit(solution)/shard_map/ppermute | solution.py:18
  69.2 0.6 collective-permute-start.22
  69.8 2.7 %collective-permute-start.34 = (bf16[1,256,128]{2,1,0:T(8,128)(2,1)S(1)}, bf16[1,256,128]{2,1,0:T(8,128)(2,1)S(1)}, u32[]{:S(2)}, u32[]{:S(2)}) collective-permute-start(bf16[1,256,128]{2,1,0:T(8,128)(2,1)S(1)} %get-tuple-element.92), channel_id=1, source_target_pairs={{0,16},{4,20},{8,24},{12,28},{16,0},{20,4},{24,8},{28,12},{1,17},{... | collective-permute-start | bytes 196616 | tf_op jit(solution)/shard_map/ppermute | solution.py:18
  72.7 1.0 %collective-permute-start.31 = (bf16[1,336,128]{2,1,0:T(8,128)(2,1)S(1)}, bf16[1,336,128]{2,1,0:T(8,128)(2,1)S(1)}, u32[]{:S(2)}, u32[]{:S(2)}) collective-permute-start(bf16[1,336,128]{2,1,0:T(8,128)(2,1)S(1)} %get-tuple-element.90), channel_id=1, source_target_pairs={{0,16},{4,20},{8,24},{12,28},{16,0},{20,4},{24,8},{28,12},{1,17},{... | collective-permute-start | bytes 258056 | tf_op jit(solution)/shard_map/ppermute | solution.py:18
  73.7 1.5 %collective-permute-start.26 = (bf16[2,336,128]{2,1,0:T(8,128)(2,1)S(1)}, bf16[2,336,128]{2,1,0:T(8,128)(2,1)S(1)}, u32[]{:S(2)}, u32[]{:S(2)}) collective-permute-start(bf16[2,336,128]{2,1,0:T(8,128)(2,1)S(1)} %slice.124), channel_id=1, source_target_pairs={{0,2},{1,3},{2,0},{3,1},{4,6},{5,7},{6,4},{7,5},{8,10},{9,11},{10,... | collective-permute-start | bytes 516104 | tf_op jit(solution)/shard_map/ppermute | solution.py:18
  75.8 0.7 join_out.1
  76.5 1.2 %copy.31 = bf16[2,6,13,13,128]{4,0,3,2,1:T(2,128)(2,1)} copy(bf16[2,6,13,13,128]{4,3,2,1,0:T(8,128)(2,1)S(1)} %bitcast.58) | data formatting | bytes 1038336
  77.7 2.0 %collective-permute-start.28 = (bf16[1,256,128]{2,1,0:T(8,128)(2,1)S(1)}, bf16[1,256,128]{2,1,0:T(8,128)(2,1)S(1)}, u32[]{:S(2)}, u32[]{:S(2)}) collective-permute-start(bf16[1,256,128]{2,1,0:T(8,128)(2,1)S(1)} %slice.129), channel_id=1, source_target_pairs={{0,16},{4,20},{8,24},{12,28},{16,0},{20,4},{24,8},{28,12},{1,17},{... | collective-permute-start | bytes 196616 | tf_op jit(solution)/shard_map/ppermute | solution.py:18
  79.8 0.7 convert.16
  80.6 0.5 fusion.1
  81.1 1.0 %collective-permute-start.27 = (bf16[1,336,128]{2,1,0:T(8,128)(2,1)S(1)}, bf16[1,336,128]{2,1,0:T(8,128)(2,1)S(1)}, u32[]{:S(2)}, u32[]{:S(2)}) collective-permute-start(bf16[1,336,128]{2,1,0:T(8,128)(2,1)S(1)} %slice.126), channel_id=1, source_target_pairs={{0,16},{4,20},{8,24},{12,28},{16,0},{20,4},{24,8},{28,12},{1,17},{... | collective-permute-start | bytes 258056 | tf_op jit(solution)/shard_map/ppermute | solution.py:18
  82.1 2.0 %collective-permute-done.28 = bf16[1,256,128]{2,1,0:T(8,128)(2,1)S(1)} collective-permute-done((bf16[1,256,128]{2,1,0:T(8,128)(2,1)S(1)}, bf16[1,256,128]{2,1,0:T(8,128)(2,1)S(1)}, u32[]{:S(2)}, u32[]{:S(2)}) %collective-permute-start.28) | collective-permute-done | bytes 65568 | tf_op jit(solution)/shard_map/ppermute | solution.py:18
  84.1 0.7 join_grad.1
  84.8 1.2 %copy.32 = bf16[2,6,13,13,128]{4,0,3,2,1:T(2,128)(2,1)} copy(bf16[2,6,13,13,128]{4,3,2,1,0:T(8,128)(2,1)S(1)} %bitcast.57) | data formatting | bytes 1038336
  86.0 2.2 %collective-permute-done.27 = bf16[1,336,128]{2,1,0:T(8,128)(2,1)S(1)} collective-permute-done((bf16[1,336,128]{2,1,0:T(8,128)(2,1)S(1)}, bf16[1,336,128]{2,1,0:T(8,128)(2,1)S(1)}, u32[]{:S(2)}, u32[]{:S(2)}) %collective-permute-start.27) | collective-permute-done | bytes 86048 | tf_op jit(solution)/shard_map/ppermute | solution.py:18
  88.3 0.7 convert.14
  89.0 0.5 fusion.2
  (100 shorter events, 4.6 us)
Async XLA Ops:
  0.6 8.1 %copy-start = (s32[2,2]{1,0:T(2,128)S(1)}, s32[2,2]{1,0:T(2,128)}, u32[]{:S(2)}) copy-start(s32[2,2]{1,0:T(2,128)} %param.8) | copy-start | bytes 52
  2.0 7.6 %collective-permute-start = (bf16[3,208,128]{2,1,0:T(8,128)(2,1)S(1)}, bf16[3,208,128]{2,1,0:T(8,128)(2,1)S(1)}, u32[]{:S(2)}, u32[]{:S(2)}) collective-permute-start(bf16[3,208,128]{2,1,0:T(8,128)(2,1)S(1)} %constant_dynamic-slice_fusion.3), channel_id=1, source_target_pairs={{0,1},{1,0},{2,3},{3,2},{4,5},{5,4},{6,7},{7,6},{8,9},{9,8},{10,11... | collective-permute-start | bytes 479240 | tf_op jit(solution)/shard_map/ppermute | solution.py:18
  2.5 11.2 %collective-permute-start.1 = (bf16[2,3,208,128]{3,2,1,0:T(8,128)(2,1)S(1)}, bf16[2,3,208,128]{3,2,1,0:T(8,128)(2,1)S(1)}, u32[]{:S(2)}, u32[]{:S(2)}) collective-permute-start(bf16[2,3,208,128]{3,2,1,0:T(8,128)(2,1)S(1)} %bitcast.73), channel_id=1, source_target_pairs={{0,2},{1,3},{2,0},{3,1},{4,6},{5,7},{6,4},{7,5},{8,10},{9,11},{10,... | collective-permute-start | bytes 958472 | tf_op jit(solution)/shard_map/ppermute | solution.py:18
  5.1 11.3 %collective-permute-start.3 = (bf16[2,3,208,128]{3,2,1,0:T(8,128)(2,1)S(1)}, bf16[2,3,208,128]{3,2,1,0:T(8,128)(2,1)S(1)}, u32[]{:S(2)}, u32[]{:S(2)}) collective-permute-start(bf16[2,3,208,128]{3,2,1,0:T(8,128)(2,1)S(1)} %bitcast.54), channel_id=1, source_target_pairs={{0,8},{4,12},{8,0},{12,4},{16,24},{20,28},{24,16},{28,20},{1,9},{5... | collective-permute-start | bytes 958472 | tf_op jit(solution)/shard_map/ppermute | solution.py:18
  8.0 8.4 %copy-start.2 = (f32[512]{0:T(512)S(1)}, f32[512]{0:T(512)}, u32[]{:S(2)}) copy-start(f32[512]{0:T(512)} %param.10) | copy-start | bytes 6148
  8.1 13.2 %collective-permute-start.5 = (bf16[2,3,208,128]{3,2,1,0:T(8,128)(2,1)S(1)}, bf16[2,3,208,128]{3,2,1,0:T(8,128)(2,1)S(1)}, u32[]{:S(2)}, u32[]{:S(2)}) collective-permute-start(bf16[2,3,208,128]{3,2,1,0:T(8,128)(2,1)S(1)} %pad_maximum_fusion), channel_id=1, source_target_pairs={{0,2},{1,3},{2,0},{3,1},{4,6},{5,7},{6,4},{7,5},{8,10},{9,11},{10,... | collective-permute-start | bytes 958472 | tf_op jit(solution)/shard_map/ppermute | solution.py:18
  14.5 1.9 %collective-permute-start.2 = (bf16[3,208,128]{2,1,0:T(8,128)(2,1)S(1)}, bf16[3,208,128]{2,1,0:T(8,128)(2,1)S(1)}, u32[]{:S(2)}, u32[]{:S(2)}) collective-permute-start(bf16[3,208,128]{2,1,0:T(8,128)(2,1)S(1)} %pick.1), channel_id=1, source_target_pairs={{0,1},{1,0},{2,3},{3,2},{4,5},{5,4},{6,7},{7,6},{8,9},{9,8},{10,11... | collective-permute-start | bytes 479240 | tf_op jit(solution)/shard_map/ppermute | solution.py:18
  14.6 15.8 %collective-permute-start.11 = (bf16[2,3,208,128]{3,2,1,0:T(8,128)(2,1)S(1)}, bf16[2,3,208,128]{3,2,1,0:T(8,128)(2,1)S(1)}, u32[]{:S(2)}, u32[]{:S(2)}) collective-permute-start(bf16[2,3,208,128]{3,2,1,0:T(8,128)(2,1)S(1)} %after_part.1.refs_0_.refs_1_), channel_id=1, source_target_pairs={{0,8},{4,12},{8,0},{12,4},{16,24},{20,28},{24,16},{28,20},{1,9},{5... | collective-permute-start | bytes 958472 | tf_op jit(solution)/shard_map/ppermute | solution.py:18
  16.5 6.4 %copy-start.1 = (f32[512]{0:T(512)S(1)}, f32[512]{0:T(512)}, u32[]{:S(2)}) copy-start(f32[512]{0:T(512)} %param.12) | copy-start | bytes 6148
  19.7 23.4 %collective-permute-start.9 = (bf16[4,3,208,128]{3,2,1,0:T(8,128)(2,1)S(1)}, bf16[4,3,208,128]{3,2,1,0:T(8,128)(2,1)S(1)}, u32[]{:S(2)}, u32[]{:S(2)}) collective-permute-start(bf16[4,3,208,128]{3,2,1,0:T(8,128)(2,1)S(1)} %get-tuple-element.39.refs_0_), channel_id=1, source_target_pairs={{0,4},{4,0},{8,12},{12,8},{16,20},{20,16},{24,28},{28,24},{1,5},{5... | collective-permute-start | bytes 1916936 | tf_op jit(solution)/shard_map/ppermute | solution.py:18
  21.3 1.4 %collective-permute-start.4 = (bf16[3,208,128]{2,1,0:T(8,128)(2,1)S(1)}, bf16[3,208,128]{2,1,0:T(8,128)(2,1)S(1)}, u32[]{:S(2)}, u32[]{:S(2)}) collective-permute-start(bf16[3,208,128]{2,1,0:T(8,128)(2,1)S(1)} %get-tuple-element.82.refs_4_), channel_id=1, source_target_pairs={{0,1},{1,0},{2,3},{3,2},{4,5},{5,4},{6,7},{7,6},{8,9},{9,8},{10,11... | collective-permute-start | bytes 479240 | tf_op jit(solution)/shard_map/ppermute | solution.py:18
  21.3 1.6 %collective-permute-start.6 = (bf16[1,3,208,128]{3,2,1,0:T(8,128)(2,1)S(1)}, bf16[1,3,208,128]{3,2,1,0:T(8,128)(2,1)S(1)}, u32[]{:S(2)}, u32[]{:S(2)}) collective-permute-start(bf16[1,3,208,128]{3,2,1,0:T(8,128)(2,1)S(1)} %slice.120), channel_id=1, source_target_pairs={{0,1},{1,0},{2,3},{3,2},{4,5},{5,4},{6,7},{7,6},{8,9},{9,8},{10,11... | collective-permute-start | bytes 479240 | tf_op jit(solution)/shard_map/ppermute | solution.py:18
  21.9 9.0 %collective-permute-start.12 = (bf16[2,3,208,128]{3,2,1,0:T(8,128)(2,1)S(1)}, bf16[2,3,208,128]{3,2,1,0:T(8,128)(2,1)S(1)}, u32[]{:S(2)}, u32[]{:S(2)}) collective-permute-start(bf16[2,3,208,128]{3,2,1,0:T(8,128)(2,1)S(1)} %slice.90), channel_id=1, source_target_pairs={{0,1},{1,0},{2,3},{3,2},{4,5},{5,4},{6,7},{7,6},{8,9},{9,8},{10,11... | collective-permute-start | bytes 958472 | tf_op jit(solution)/shard_map/ppermute | solution.py:18
  28.5 7.0 %collective-permute-start.13 = (bf16[3,208,256]{2,1,0:T(8,128)(2,1)S(1)}, bf16[3,208,256]{2,1,0:T(8,128)(2,1)S(1)}, u32[]{:S(2)}, u32[]{:S(2)}) collective-permute-start(bf16[3,208,256]{2,1,0:T(8,128)(2,1)S(1)} %get-tuple-element.49.refs_4_), channel_id=1, source_target_pairs={{0,1},{1,0},{2,3},{3,2},{4,5},{5,4},{6,7},{7,6},{8,9},{9,8},{10,11... | collective-permute-start | bytes 958472 | tf_op jit(solution)/shard_map/ppermute | solution.py:18
  28.9 11.7 %collective-permute-start.10 = (bf16[2,3,208,128]{3,2,1,0:T(8,128)(2,1)S(1)}, bf16[2,3,208,128]{3,2,1,0:T(8,128)(2,1)S(1)}, u32[]{:S(2)}, u32[]{:S(2)}) collective-permute-start(bf16[2,3,208,128]{3,2,1,0:T(8,128)(2,1)S(1)} %get-tuple-element.45), channel_id=1, source_target_pairs={{0,2},{1,3},{2,0},{3,1},{4,6},{5,7},{6,4},{7,5},{8,10},{9,11},{10,... | collective-permute-start | bytes 958472 | tf_op jit(solution)/shard_map/ppermute | solution.py:18
  30.4 12.6 %collective-permute-start.8 = (bf16[3,208,256]{2,1,0:T(8,128)(2,1)S(1)}, bf16[3,208,256]{2,1,0:T(8,128)(2,1)S(1)}, u32[]{:S(2)}, u32[]{:S(2)}) collective-permute-start(bf16[3,208,256]{2,1,0:T(8,128)(2,1)S(1)} %get-tuple-element.44), channel_id=1, source_target_pairs={{0,4},{4,0},{8,12},{12,8},{16,20},{20,16},{24,28},{28,24},{1,5},{5... | collective-permute-start | bytes 958472 | tf_op jit(solution)/shard_map/ppermute | solution.py:18
  30.9 12.7 %collective-permute-start.7 = (bf16[3,208,128]{2,1,0:T(8,128)(2,1)S(1)}, bf16[3,208,128]{2,1,0:T(8,128)(2,1)S(1)}, u32[]{:S(2)}, u32[]{:S(2)}) collective-permute-start(bf16[3,208,128]{2,1,0:T(8,128)(2,1)S(1)} %get-tuple-element.43), channel_id=1, source_target_pairs={{0,1},{1,0},{2,3},{3,2},{4,5},{5,4},{6,7},{7,6},{8,9},{9,8},{10,11... | collective-permute-start | bytes 479240 | tf_op jit(solution)/shard_map/ppermute | solution.py:18
  35.5 8.3 %collective-permute-start.15 = (bf16[3,208,256]{2,1,0:T(8,128)(2,1)S(1)}, bf16[3,208,256]{2,1,0:T(8,128)(2,1)S(1)}, u32[]{:S(2)}, u32[]{:S(2)}) collective-permute-start(bf16[3,208,256]{2,1,0:T(8,128)(2,1)S(1)} %get-tuple-element.52.refs_4_), channel_id=1, source_target_pairs={{0,1},{1,0},{2,3},{3,2},{4,5},{5,4},{6,7},{7,6},{8,9},{9,8},{10,11... | collective-permute-start | bytes 958472 | tf_op jit(solution)/shard_map/ppermute | solution.py:18
  40.7 9.5 %collective-permute-start.16 = (bf16[3,208,256]{2,1,0:T(8,128)(2,1)S(1)}, bf16[3,208,256]{2,1,0:T(8,128)(2,1)S(1)}, u32[]{:S(2)}, u32[]{:S(2)}) collective-permute-start(bf16[3,208,256]{2,1,0:T(8,128)(2,1)S(1)} %get-tuple-element.53), channel_id=1, source_target_pairs={{0,8},{4,12},{8,0},{12,4},{16,24},{20,28},{24,16},{28,20},{1,9},{5... | collective-permute-start | bytes 958472 | tf_op jit(solution)/shard_map/ppermute | solution.py:18
  43.1 2.4 %collective-permute-start.17 = (bf16[2,3,208,128]{3,2,1,0:T(8,128)(2,1)S(1)}, bf16[2,3,208,128]{3,2,1,0:T(8,128)(2,1)S(1)}, u32[]{:S(2)}, u32[]{:S(2)}) collective-permute-start(bf16[2,3,208,128]{3,2,1,0:T(8,128)(2,1)S(1)} %slice.92), channel_id=1, source_target_pairs={{0,1},{1,0},{2,3},{3,2},{4,5},{5,4},{6,7},{7,6},{8,9},{9,8},{10,11... | collective-permute-start | bytes 958472 | tf_op jit(solution)/shard_map/ppermute | solution.py:18
  43.2 2.3 %collective-permute-start.18 = (bf16[3,208,256]{2,1,0:T(8,128)(2,1)S(1)}, bf16[3,208,256]{2,1,0:T(8,128)(2,1)S(1)}, u32[]{:S(2)}, u32[]{:S(2)}) collective-permute-start(bf16[3,208,256]{2,1,0:T(8,128)(2,1)S(1)} %get-tuple-element.55.refs_6_), channel_id=1, source_target_pairs={{0,1},{1,0},{2,3},{3,2},{4,5},{5,4},{6,7},{7,6},{8,9},{9,8},{10,11... | collective-permute-start | bytes 958472 | tf_op jit(solution)/shard_map/ppermute | solution.py:18
  43.7 1.8 %collective-permute-start.14 = (bf16[3,208,128]{2,1,0:T(8,128)(2,1)S(1)}, bf16[3,208,128]{2,1,0:T(8,128)(2,1)S(1)}, u32[]{:S(2)}, u32[]{:S(2)}) collective-permute-start(bf16[3,208,128]{2,1,0:T(8,128)(2,1)S(1)} %slice_bitcast_fusion.1), channel_id=1, source_target_pairs={{0,1},{1,0},{2,3},{3,2},{4,5},{5,4},{6,7},{7,6},{8,9},{9,8},{10,11... | collective-permute-start | bytes 479240 | tf_op jit(solution)/shard_map/ppermute | solution.py:18
  43.8 10.2 %collective-permute-start.20 = (bf16[2,3,208,128]{3,2,1,0:T(8,128)(2,1)S(1)}, bf16[2,3,208,128]{3,2,1,0:T(8,128)(2,1)S(1)}, u32[]{:S(2)}, u32[]{:S(2)}) collective-permute-start(bf16[2,3,208,128]{3,2,1,0:T(8,128)(2,1)S(1)} %get-tuple-element.57), channel_id=1, source_target_pairs={{0,2},{1,3},{2,0},{3,1},{4,6},{5,7},{6,4},{7,5},{8,10},{9,11},{10,... | collective-permute-start | bytes 958472 | tf_op jit(solution)/shard_map/ppermute | solution.py:18
  50.2 3.9 %collective-permute-start.19 = (bf16[3,208,256]{2,1,0:T(8,128)(2,1)S(1)}, bf16[3,208,256]{2,1,0:T(8,128)(2,1)S(1)}, u32[]{:S(2)}, u32[]{:S(2)}) collective-permute-start(bf16[3,208,256]{2,1,0:T(8,128)(2,1)S(1)} %after_grad5.1.refs_6_), channel_id=1, source_target_pairs={{0,1},{1,0},{2,3},{3,2},{4,5},{5,4},{6,7},{7,6},{8,9},{9,8},{10,11... | collective-permute-start | bytes 958472 | tf_op jit(solution)/shard_map/ppermute | solution.py:18
  50.2 11.4 %collective-permute-start.32 = (bf16[4,256,128]{2,1,0:T(8,128)(2,1)S(1)}, bf16[4,256,128]{2,1,0:T(8,128)(2,1)S(1)}, u32[]{:S(2)}, u32[]{:S(2)}) collective-permute-start(bf16[4,256,128]{2,1,0:T(8,128)(2,1)S(1)} %get-tuple-element.67), channel_id=1, source_target_pairs={{0,2},{1,3},{2,0},{3,1},{4,6},{5,7},{6,4},{7,5},{8,10},{9,11},{10,... | collective-permute-start | bytes 786440 | tf_op jit(solution)/shard_map/ppermute | solution.py:18
  51.5 11.5 %collective-permute-start.29 = (bf16[4,336,128]{2,1,0:T(8,128)(2,1)S(1)}, bf16[4,336,128]{2,1,0:T(8,128)(2,1)S(1)}, u32[]{:S(2)}, u32[]{:S(2)}) collective-permute-start(bf16[4,336,128]{2,1,0:T(8,128)(2,1)S(1)} %get-tuple-element.65), channel_id=1, source_target_pairs={{0,8},{4,12},{8,0},{12,4},{16,24},{20,28},{24,16},{28,20},{1,9},{5... | collective-permute-start | bytes 1032200 | tf_op jit(solution)/shard_map/ppermute | solution.py:18
  58.4 14.1 %collective-permute-start.23 = (bf16[4,336,128]{2,1,0:T(8,128)(2,1)S(1)}, bf16[4,336,128]{2,1,0:T(8,128)(2,1)S(1)}, u32[]{:S(2)}, u32[]{:S(2)}) collective-permute-start(bf16[4,336,128]{2,1,0:T(8,128)(2,1)S(1)} %get-tuple-element.62), channel_id=1, source_target_pairs={{0,4},{4,0},{8,12},{12,8},{16,20},{20,16},{24,28},{28,24},{1,5},{5... | collective-permute-start | bytes 1032200 | tf_op jit(solution)/shard_map/ppermute | solution.py:18
  60.0 9.1 %collective-permute-start.21 = (bf16[4,256,128]{2,1,0:T(8,128)(2,1)S(1)}, bf16[4,256,128]{2,1,0:T(8,128)(2,1)S(1)}, u32[]{:S(2)}, u32[]{:S(2)}) collective-permute-start(bf16[4,256,128]{2,1,0:T(8,128)(2,1)S(1)} %get-tuple-element.59), channel_id=1, source_target_pairs={{0,2},{1,3},{2,0},{3,1},{4,6},{5,7},{6,4},{7,5},{8,10},{9,11},{10,... | collective-permute-start | bytes 786440 | tf_op jit(solution)/shard_map/ppermute | solution.py:18
  61.7 8.0 %collective-permute-start.33 = (bf16[2,256,128]{2,1,0:T(8,128)(2,1)S(1)}, bf16[2,256,128]{2,1,0:T(8,128)(2,1)S(1)}, u32[]{:S(2)}, u32[]{:S(2)}) collective-permute-start(bf16[2,256,128]{2,1,0:T(8,128)(2,1)S(1)} %get-tuple-element.88), channel_id=1, source_target_pairs={{0,8},{4,12},{8,0},{12,4},{16,24},{20,28},{24,16},{28,20},{1,9},{5... | collective-permute-start | bytes 393224 | tf_op jit(solution)/shard_map/ppermute | solution.py:18
  63.2 9.4 %collective-permute-start.30 = (bf16[2,336,128]{2,1,0:T(8,128)(2,1)S(1)}, bf16[2,336,128]{2,1,0:T(8,128)(2,1)S(1)}, u32[]{:S(2)}, u32[]{:S(2)}) collective-permute-start(bf16[2,336,128]{2,1,0:T(8,128)(2,1)S(1)} %get-tuple-element.86), channel_id=1, source_target_pairs={{0,2},{1,3},{2,0},{3,1},{4,6},{5,7},{6,4},{7,5},{8,10},{9,11},{10,... | collective-permute-start | bytes 516104 | tf_op jit(solution)/shard_map/ppermute | solution.py:18
  69.2 6.1 %collective-permute-start.22 = (bf16[2,256,128]{2,1,0:T(8,128)(2,1)S(1)}, bf16[2,256,128]{2,1,0:T(8,128)(2,1)S(1)}, u32[]{:S(2)}, u32[]{:S(2)}) collective-permute-start(bf16[2,256,128]{2,1,0:T(8,128)(2,1)S(1)} %slice.122), channel_id=1, source_target_pairs={{0,4},{4,0},{8,12},{12,8},{16,20},{20,16},{24,28},{28,24},{1,5},{5... | collective-permute-start | bytes 393224 | tf_op jit(solution)/shard_map/ppermute | solution.py:18
  69.8 7.9 %collective-permute-start.34 = (bf16[1,256,128]{2,1,0:T(8,128)(2,1)S(1)}, bf16[1,256,128]{2,1,0:T(8,128)(2,1)S(1)}, u32[]{:S(2)}, u32[]{:S(2)}) collective-permute-start(bf16[1,256,128]{2,1,0:T(8,128)(2,1)S(1)} %get-tuple-element.92), channel_id=1, source_target_pairs={{0,16},{4,20},{8,24},{12,28},{16,0},{20,4},{24,8},{28,12},{1,17},{... | collective-permute-start | bytes 196616 | tf_op jit(solution)/shard_map/ppermute | solution.py:18
  72.7 7.1 %collective-permute-start.31 = (bf16[1,336,128]{2,1,0:T(8,128)(2,1)S(1)}, bf16[1,336,128]{2,1,0:T(8,128)(2,1)S(1)}, u32[]{:S(2)}, u32[]{:S(2)}) collective-permute-start(bf16[1,336,128]{2,1,0:T(8,128)(2,1)S(1)} %get-tuple-element.90), channel_id=1, source_target_pairs={{0,16},{4,20},{8,24},{12,28},{16,0},{20,4},{24,8},{28,12},{1,17},{... | collective-permute-start | bytes 258056 | tf_op jit(solution)/shard_map/ppermute | solution.py:18
  73.7 7.4 %collective-permute-start.26 = (bf16[2,336,128]{2,1,0:T(8,128)(2,1)S(1)}, bf16[2,336,128]{2,1,0:T(8,128)(2,1)S(1)}, u32[]{:S(2)}, u32[]{:S(2)}) collective-permute-start(bf16[2,336,128]{2,1,0:T(8,128)(2,1)S(1)} %slice.124), channel_id=1, source_target_pairs={{0,2},{1,3},{2,0},{3,1},{4,6},{5,7},{6,4},{7,5},{8,10},{9,11},{10,... | collective-permute-start | bytes 516104 | tf_op jit(solution)/shard_map/ppermute | solution.py:18
  75.2 8.9 %collective-permute-start.25 = (bf16[3,208,128]{2,1,0:T(8,128)(2,1)S(1)}, bf16[3,208,128]{2,1,0:T(8,128)(2,1)S(1)}, u32[]{:S(2)}, u32[]{:S(2)}) collective-permute-start(bf16[3,208,128]{2,1,0:T(8,128)(2,1)S(1)} %slice_bitcast_fusion), channel_id=1, source_target_pairs={{0,1},{1,0},{2,3},{3,2},{4,5},{5,4},{6,7},{7,6},{8,9},{9,8},{10,11... | collective-permute-start | bytes 479240 | tf_op jit(solution)/shard_map/ppermute | solution.py:18
  75.3 8.9 %collective-permute-start.24 = (bf16[3,208,128]{2,1,0:T(8,128)(2,1)S(1)}, bf16[3,208,128]{2,1,0:T(8,128)(2,1)S(1)}, u32[]{:S(2)}, u32[]{:S(2)}) collective-permute-start(bf16[3,208,128]{2,1,0:T(8,128)(2,1)S(1)} %get-tuple-element.63), channel_id=1, source_target_pairs={{0,1},{1,0},{2,3},{3,2},{4,5},{5,4},{6,7},{7,6},{8,9},{9,8},{10,11... | collective-permute-start | bytes 479240 | tf_op jit(solution)/shard_map/ppermute | solution.py:18
  77.7 6.4 %collective-permute-start.28 = (bf16[1,256,128]{2,1,0:T(8,128)(2,1)S(1)}, bf16[1,256,128]{2,1,0:T(8,128)(2,1)S(1)}, u32[]{:S(2)}, u32[]{:S(2)}) collective-permute-start(bf16[1,256,128]{2,1,0:T(8,128)(2,1)S(1)} %slice.129), channel_id=1, source_target_pairs={{0,16},{4,20},{8,24},{12,28},{16,0},{20,4},{24,8},{28,12},{1,17},{... | collective-permute-start | bytes 196616 | tf_op jit(solution)/shard_map/ppermute | solution.py:18
  81.1 7.0 %collective-permute-start.27 = (bf16[1,336,128]{2,1,0:T(8,128)(2,1)S(1)}, bf16[1,336,128]{2,1,0:T(8,128)(2,1)S(1)}, u32[]{:S(2)}, u32[]{:S(2)}) collective-permute-start(bf16[1,336,128]{2,1,0:T(8,128)(2,1)S(1)} %slice.126), channel_id=1, source_target_pairs={{0,16},{4,20},{8,24},{12,28},{16,0},{20,4},{24,8},{28,12},{1,17},{... | collective-permute-start | bytes 258056 | tf_op jit(solution)/shard_map/ppermute | solution.py:18
